TPU v7x, 512 devices: a whole 4x8x8 slice. The times are simulated.
512 devices in a mesh: gx: 64 (over z_lo, x, y), gy: 8 (over z_hi, core).
Axes of the slice: x: 4, y: 8, z: 8 (z_hi: 4, z_lo: 2; z = z_hi * 2 + z_lo), core: 2. Of those that a mesh axis runs over, the one named last changes fastest.
Arguments:
- position: float32 [3, 2097152], P(None, ('gx', 'gy')), may hold values from 0.05 to 0.95, as said below
- momentum: float32 [3, 2097152], P(None, ('gx', 'gy')), may hold values from -1.6 to 1.6, as said below
- cell_first: int32 [3, 2097152], P(None, ('gx', 'gy')), may hold values from 0 to 255, as said below
- cell_second: int32 [3, 2097152], P(None, ('gx', 'gy')), may hold values from 0 to 255, as said below
- destination: int32 [2097152], P(('gx', 'gy')), may hold values from 0 to 4, as said below
- slot_index: int32 [2097152], P(('gx', 'gy')), may hold values from 0 to 4095, as said below
- pull_position: float32 [3, 2097152], P(None, ('gx', 'gy')), may hold values from -6 to 6
- pull_momentum: float32 [3, 2097152], P(None, ('gx', 'gy')), may hold values from -6 to 6
Outputs:
- grad_position: float32 [3, 2097152], P(None, ('gx', 'gy'))
- grad_momentum: float32 [3, 2097152], P(None, ('gx', 'gy'))
Inputs may be any that keep to these rules, and one draw needn't show every extreme that they name: `destination`: 0: the particle stays on its device; 1 and 2: it moves to the next and to the previous device along gx; 3 and 4: to the next and to the previous device along gy (both axes wrap). From the particles of one device at most 256 go to each of its four neighbours, and in every draw some device sends exactly 256 to one neighbour. Between two neighbouring devices as many particles move one way as the other. A particle that moves to the next (previous) device along an axis lies in the last (first) cell layer of its device along that axis in cell_first. Over all particles the destination device and slot_index fill every index of every device exactly once. `cell_first`: the first component is below 2, the second below 8, the third below 256. `cell_second`: the cell_first of the particle that lands at this index, moved with it: a particle moving along gx goes from the last layer to the first or from the first to the last, likewise along gy; other components stay. The first component is below 2, the second below 8, the third below 256. `position`: A particle's drift_one leaves its cell along an axis exactly where destination sends it across that axis, in that direction. `momentum`: momenta of particles that move carry them across the cell face toward their destination.
All inputs are finite; a program needn't handle non-finite values.
Results may differ from a plain program's by a relative error of at most 0.000058.
Values sent between devices are 32-bit elements; how exact they have to be, the bound alone decides.
No kernel may reach another device: no remote copies, remote signals or barrier semaphores. Data moves between devices by JAX's collectives and lax.ppermute only.
A program may use at most 64 MiB of HBM per device.

v0:
```python
import jax
import jax.numpy as jnp
from jax import lax
from jax.sharding import PartitionSpec as P

CX = 2
CY = 8
NZ = 256
MOVE_MOST = 256


highest = lax.Precision.HIGHEST
step_size = 0.25
strength = 0.02


def with_halo(x, sides, width):
    for axis, dim in sides:
        peers, length = (lax.axis_size(axis), x.shape[dim])
        up = [(i, (i + 1) % peers) for i in range(peers)]
        down = [(j, i) for i, j in up]
        last = lax.slice_in_dim(x, length - width, length, axis=dim)
        first = lax.slice_in_dim(x, 0, width, axis=dim)
        before = lax.ppermute(last, axis, up)
        after = lax.ppermute(first, axis, down)
        x = jnp.concatenate([before, x, after], axis=dim)
    return x


def kernel_block(targets, sources, extent, reach_cells):
    distance = jnp.abs(targets[:, None] - sources[None, :])
    distance = jnp.minimum(distance, extent - distance)
    return jnp.exp(-distance.astype(jnp.float32) / reach_cells)


def cloud_weights(cell_block, frac_block, plane_count, row_count, depth_cells):
    index_row = jnp.arange(row_count, dtype=jnp.int32)[:, None]
    corner = (cell_block[1] * plane_count + cell_block[0])[None, :]
    hit_base = (index_row == corner).astype(jnp.float32)
    hit_east = (index_row == corner + 1).astype(jnp.float32)
    hit_north = (index_row == corner + plane_count).astype(jnp.float32)
    hit_both = (index_row == corner + plane_count + 1).astype(jnp.float32)
    west_weight = (1.0 - frac_block[0])[None, :]
    east_weight = frac_block[0][None, :]
    south_weight = (1.0 - frac_block[1])[None, :]
    north_weight = frac_block[1][None, :]
    planar = (
        hit_base * (west_weight * south_weight)
        + hit_east * (east_weight * south_weight)
        + hit_north * (west_weight * north_weight)
        + hit_both * (east_weight * north_weight)
    )
    slope_east = (hit_east - hit_base) * south_weight + (hit_both - hit_north) * north_weight
    slope_north = (hit_north - hit_base) * west_weight + (hit_both - hit_east) * east_weight
    index_depth = jnp.arange(depth_cells, dtype=jnp.int32)[:, None]
    lower_hit = (index_depth == cell_block[2][None, :]).astype(jnp.float32)
    upper_hit = (index_depth == ((cell_block[2] + 1) % depth_cells)[None, :]).astype(jnp.float32)
    vertical = lower_hit * (1.0 - frac_block[2])[None, :] + upper_hit * frac_block[2][None, :]
    slope_up = upper_hit - lower_hit
    return (planar, slope_east, slope_north, vertical, slope_up)


def particle_blocks(values):
    particle_count = values.shape[1]
    block_width = min(512, particle_count)
    return values.reshape(values.shape[0], particle_count // block_width, block_width).transpose(
        1, 0, 2
    )


def deposit(scales, cell_ids, offsets):
    layers = scales.shape[0]
    row_count = (CY + 1) * (CX + 1)

    def add_block(running, pieces):
        cell_block, frac_block, scale_block = pieces
        weights = cloud_weights(cell_block, frac_block, CX + 1, row_count, NZ)
        spread = scale_block[:, None, :] * weights[0][None]
        return (running + jnp.einsum("crb,zb->crz", spread, weights[3], precision=highest), None)

    initial = jnp.zeros((layers, row_count, NZ), jnp.float32)
    running, unused = lax.scan(
        add_block,
        initial,
        (particle_blocks(cell_ids), particle_blocks(offsets), particle_blocks(scales)),
    )
    return running.reshape(layers, CY + 1, CX + 1, NZ)


def sample_fields(fields, cell_ids, offsets, slopes):
    layers = fields.shape[0]
    row_count = fields.shape[1] * fields.shape[2]
    flattened = fields.reshape(layers * row_count, NZ)

    def one_block(pieces):
        cell_block, frac_block = pieces
        block_width = cell_block.shape[1]
        weights = cloud_weights(cell_block, frac_block, fields.shape[2], row_count, NZ)
        columns = jnp.concatenate([weights[3], weights[4]], 1) if slopes else weights[3]
        contracted = jnp.dot(
            flattened, columns, precision=highest, preferred_element_type=jnp.float32
        )
        contracted = contracted.reshape(layers, row_count, -1)
        nearby = contracted[:, :, :block_width]
        results = [jnp.sum(nearby * weights[0][None], axis=1)]
        if slopes:
            results.append(jnp.sum(nearby * weights[1][None], axis=1))
            results.append(jnp.sum(nearby * weights[2][None], axis=1))
            results.append(jnp.sum(contracted[:, :, block_width:] * weights[0][None], axis=1))
        return jnp.stack(results, 0)

    blocked = lax.map(one_block, (particle_blocks(cell_ids), particle_blocks(offsets)))
    return blocked.transpose(1, 2, 0, 3).reshape(blocked.shape[1], layers, cell_ids.shape[1])


def fold_planes(slab):
    planes = slab.shape[2]
    widened = with_halo(slab, (("gx", 2),), 2)
    return jnp.concatenate(
        [
            widened[:, :, 0:1],
            widened[:, :, 1:2] + widened[:, :, 2:3],
            widened[:, :, 3 : planes + 1],
            widened[:, :, planes + 1 : planes + 2] + widened[:, :, planes + 2 : planes + 3],
            widened[:, :, planes + 3 : planes + 4],
        ],
        axis=2,
    )


def smooth_depth(field):
    depth_cells = field.shape[-1]
    axis_cells = jnp.arange(depth_cells, dtype=jnp.int32)
    matrix = kernel_block(axis_cells, axis_cells, depth_cells, depth_cells / 16.0)
    return jnp.dot(
        field.reshape(-1, depth_cells),
        matrix,
        precision=highest,
        preferred_element_type=jnp.float32,
    ).reshape(field.shape)


def sum_lines(field):
    members = lax.axis_size("gy")
    band_rows = field.shape[1]
    own_rows = band_rows - 1
    extent = own_rows * members
    reach_cells = extent / 4.0
    anchor = lax.axis_index("gy") * own_rows
    targets = (anchor + jnp.arange(-1, own_rows + 2, dtype=jnp.int32)) % extent
    initial = jnp.zeros((field.shape[0], own_rows + 3, field.shape[2], field.shape[3]), jnp.float32)
    gathered = lax.all_gather(field, "gy", axis=1, tiled=True)
    length = gathered.shape[1]
    positions = jnp.arange(length, dtype=jnp.int32)
    sources = (positions // band_rows * own_rows + positions % band_rows) % extent
    weights = kernel_block(targets, sources, extent, reach_cells)
    return initial + jnp.einsum("ab,cbxz->caxz", weights, gathered, precision=highest)


def force_field(density):
    potential = sum_lines(smooth_depth(fold_planes(density)))
    potential = strength * potential
    centre = potential[:, 1:-1, 1:-1]
    push_east = -0.5 * (potential[:, 1:-1, 2:] - potential[:, 1:-1, :-2])
    push_north = -0.5 * (potential[:, 2:, 1:-1] - potential[:, :-2, 1:-1])
    push_up = -0.5 * (jnp.roll(centre, -1, 3) - jnp.roll(centre, 1, 3))
    return jnp.concatenate([push_east, push_north, push_up], 0)


def force_pullback(pushes, cell_ids, offsets, pull_force):
    folded = fold_planes(deposit(pull_force, cell_ids, offsets))
    across = 0.5 * (folded[0:1, :, 2:] - folded[0:1, :, :-2])
    upward = folded[2:3, :, 1:-1]
    across = across + 0.5 * (jnp.roll(upward, -1, 3) - jnp.roll(upward, 1, 3))
    line_sums = sum_lines(jnp.concatenate([across, folded[1:2, :, 1:-1]], 0))
    summed = line_sums[0:1, 1:-1] + 0.5 * (line_sums[1:2, 2:] - line_sums[1:2, :-2])
    density_pull = strength * smooth_depth(summed)
    sampled = sample_fields(jnp.concatenate([pushes, density_pull], 0), cell_ids, offsets, True)
    slopes = sampled[1:]
    return jnp.sum(slopes[:, :3] * pull_force[None], axis=1) + slopes[:, 3]


def pack_moves(destination, capacity):
    particle_count = destination.shape[0]
    grouped = jnp.argsort(destination, stable=True)
    group_size = jnp.sum(
        (destination[None, :] == jnp.arange(5, dtype=jnp.int32)[:, None]).astype(jnp.int32), axis=1
    )
    opening = jnp.cumsum(group_size) - group_size
    lane_index = jnp.arange(capacity, dtype=jnp.int32)
    chosen = jnp.stack(
        [
            grouped[jnp.minimum(opening[move_code] + lane_index, particle_count - 1)]
            for move_code in range(1, 5)
        ],
        0,
    )
    filled = lane_index[None, :] < group_size[1:5, None]
    return (chosen, filled)


def trade_pairs(outward_x, outward_y):
    widened_x = with_halo(outward_x, (("gx", 1),), 1)
    widened_y = with_halo(outward_y, (("gy", 1),), 1)
    return (widened_x[:, 0], widened_x[:, 3], widened_y[:, 0], widened_y[:, 3])


def local(
    position,
    momentum,
    cell_first,
    cell_second,
    destination,
    slot_index,
    pull_position,
    pull_momentum,
):
    particle_count = position.shape[1]
    unit_mass = jnp.ones((1, particle_count), jnp.float32)
    drift_one = position + step_size * momentum
    push_one = force_field(deposit(unit_mass, cell_first, drift_one))
    kick_one = momentum + step_size * sample_fields(push_one, cell_first, drift_one, False)[0]
    eastward = (destination == 1).astype(jnp.float32) - (destination == 2).astype(jnp.float32)
    northward = (destination == 3).astype(jnp.float32) - (destination == 4).astype(jnp.float32)
    shift_cells = jnp.stack([eastward, northward, jnp.zeros_like(eastward)], 0)
    payload = jnp.concatenate([drift_one - shift_cells, kick_one], 0)
    chosen, filled = pack_moves(destination, MOVE_MOST)
    slot_marks = jnp.where(filled, slot_index[chosen], particle_count).astype(jnp.float32)
    parcel = jnp.where(filled[None], payload[:, chosen], 0.0)
    parcel = jnp.concatenate([parcel, slot_marks[None]], 0)
    arrivals = trade_pairs(
        jnp.stack([parcel[:, 1], parcel[:, 0]], 1), jnp.stack([parcel[:, 3], parcel[:, 2]], 1)
    )
    arrivals = jnp.concatenate(arrivals, 1)
    received = arrivals[6].astype(jnp.int32)
    staying = jnp.where(destination == 0, slot_index, particle_count)
    placed = jnp.concatenate([staying, received], 0)
    arrived = (
        jnp.zeros((6, particle_count), jnp.float32)
        .at[:, placed]
        .set(jnp.concatenate([payload, arrivals[:6]], 1), mode="drop")
    )
    drift_two = arrived[:3] + step_size * arrived[3:]
    push_two = force_field(deposit(unit_mass, cell_second, drift_two))
    grad_drift_two = pull_position + force_pullback(
        push_two, cell_second, drift_two, step_size * pull_momentum
    )
    grad_kick_two = pull_momentum + step_size * grad_drift_two
    returning = jnp.concatenate([grad_drift_two, grad_kick_two], 0)
    sent_back = jnp.where(
        received[None] < particle_count,
        returning[:, jnp.minimum(received, particle_count - 1)],
        0.0,
    )
    sent_back = sent_back.reshape(6, 4, MOVE_MOST)
    homecoming = trade_pairs(sent_back[:, 0:2], sent_back[:, 2:4])
    returned = jnp.stack([homecoming[1], homecoming[0], homecoming[3], homecoming[2]], 1)
    gathered_home = jnp.where(destination[None] == 0, returning[:, slot_index], 0.0)
    home_spots = jnp.where(filled, chosen, particle_count).reshape(-1)
    gathered_home = gathered_home.at[:, home_spots].set(returned.reshape(6, -1), mode="drop")
    grad_drift_one = gathered_home[:3] + force_pullback(
        push_one, cell_first, drift_one, step_size * gathered_home[3:]
    )
    grad_momentum = gathered_home[3:] + step_size * grad_drift_one
    return (grad_drift_one, grad_momentum)


def solution(mesh):
    return jax.shard_map(
        local,
        mesh=mesh,
        in_specs=(
            P(None, ("gx", "gy")),
            P(None, ("gx", "gy")),
            P(None, ("gx", "gy")),
            P(None, ("gx", "gy")),
            P(("gx", "gy")),
            P(("gx", "gy")),
            P(None, ("gx", "gy")),
            P(None, ("gx", "gy")),
        ),
        out_specs=(P(None, ("gx", "gy")), P(None, ("gx", "gy"))),
        check_vma=False,
    )
```

profile of v0, /device:TPU:1, one launch (start us, length us, event | category | flops | bytes accessed | tf_op | source)
XLA Modules:
  0.0 329.3 jit_solution(1960830378543347206)
XLA Ops:
  1.4 1.0 maximum_subtract_fusion
  2.4 12.2 %while.91 = (s32[]{:T(128)}, f32[1,27,256]{2,1,0:T(8,128)S(1)}, s32[8,3,512]{2,1,0:T(4,128)}, f32[8,3,512]{2,1,0:T(4,128)S(1)}, s32[]{:T(128)}, /*index=5*/s32[]{:T(128)}, s32[]{}, s32[]{}) while((s32[]{:T(128)}, f32[1,27,256]{2,1,0:T(8,128)S(1)}, s32[8,3,512]{2,1,0:T(4,128)}, f32[8,3,512]{2,1,0:T(4,128)S(1)}, s32[]{:T(128)}, ...), condition=%wide.region_2.3_spmd.clone, body=%wide.region_1.2_spmd.clone.sunk | while | flops 43300868 | bytes 131215 | solution.py:82
  4.0 0.8 dynamic-slice_add_fusion.17
  7.0 0.8 dynamic-slice_add_fusion.17
  10.1 0.8 dynamic-slice_add_fusion.17
  13.1 0.8 dynamic-slice_add_fusion.17
  14.7 4.0 %collective-permute-start = (f32[1,9,2,256]{3,1,2,0:T(8,128)S(1)}, f32[1,9,2,256]{3,1,2,0:T(8,128)S(1)}, u32[]{:S(2)}, u32[]{:S(2)}) collective-permute-start(f32[1,9,2,256]{3,1,2,0:T(8,128)S(1)} %copy.330), channel_id=1, source_target_pairs={{0,8},{8,16},{16,24},{24,32},{32,40},{40,48},{48,56},{56,64},{64,7... | collective-permute-start | bytes 55304 | tf_op jit(solution)/shard_map/ppermute | solution.py:24
  18.7 7.8 %collective-permute-start.1 = (f32[1,9,2,256]{3,1,2,0:T(8,128)S(1)}, f32[1,9,2,256]{3,1,2,0:T(8,128)S(1)}, u32[]{:S(2)}, u32[]{:S(2)}) collective-permute-start(f32[1,9,2,256]{3,1,2,0:T(8,128)S(1)} %copy.334), channel_id=1, source_target_pairs={{8,0},{16,8},{24,16},{32,24},{40,32},{48,40},{56,48},{64,56},{72,6... | collective-permute-start | bytes 55304 | tf_op jit(solution)/shard_map/ppermute | solution.py:25
  28.9 5.8 %sort.17 = (s32[4096]{0:T(1024)}, s32[4096]{0:T(1024)S(1)}) sort(s32[4096]{0:T(1024)S(1)} %copy-done.3, s32[4096]{0:T(1024)S(1)} %iota.429), dimensions={0}, to_apply=%region_6.7 | sort | flops 49152 | bytes 65536 | tf_op jit(solution)/shard_map/jit(argsort)/sort | solution.py:185
  34.7 1.7 gather_fusion
  36.4 1.7 gather_fusion.1
  39.5 1.7 gather_fusion.2
  41.2 1.7 gather_fusion.3
  43.1 6.2 %gather_fusion.5 = s32[1024]{0:T(1024)S(1)} fusion(s32[4096]{0:T(1024)S(1)} %copy-done, s32[1024]{0:T(1024)S(1)} %broadcast_clamp_fusion.1), kind=kCustom, calls=%fused_computation.5 | custom fusion | bytes 12288 | tf_op jit(solution)/shard_map/gather | solution.py:228
  49.9 20.6 %all-gather = f32[72,5,256]{2,1,0:T(8,128)S(1)} all-gather(f32[9,5,256]{2,1,0:T(8,128)S(1)} %fusion.143), channel_id=2, replica_groups=mesh['gx'=64,'gy'=8] {'gy'}, dimensions={0}, use_global_device_ids=true | all-gather | bytes 414720 | tf_op jit(solution)/shard_map/all_gather | solution.py:152
  71.4 13.0 %while.88 = (s32[]{:T(128)}, f32[8,1,3,512]{3,2,1,0:T(4,128)S(1)}, s32[8,3,512]{2,1,0:T(4,128)}, f32[8,3,512]{2,1,0:T(4,128)S(1)}, f32[81,256]{1,0:T(8,128)S(1)}, /*index=5*/s32[]{:T(128)}, s32[]{:T(128)}, s32[]{}, s32[]{}) while((s32[]{:T(128)}, f32[8,1,3,512]{3,2,1,0:T(4,128)S(1)}, s32[8,3,512]{2,1,0:T(4,128)}, f32[8,3,512]{2,1,0:T(4,128)S(1)}, ...), condition=%wide.region_5.6_spmd, body=%wide.region_3.5_spmd.sunk | while | flops 128303104 | bytes 955537 | solution.py:112
  73.0 0.8 dynamic-slice_add_fusion.14
  76.3 0.8 dynamic-slice_add_fusion.14
  81.1 0.8 dynamic-slice_add_fusion.14
  85.1 2.8 gather_fusion.4
  88.1 2.1 collective-permute-start.5
  90.2 4.4 %collective-permute-start.4 = (f32[7,1,256]{2,1,0:T(1,128)S(1)}, f32[7,1,256]{2,1,0:T(1,128)S(1)}, u32[]{:S(2)}, u32[]{:S(2)}) collective-permute-start(f32[7,1,256]{2,1,0:T(1,128)S(1)} %get-tuple-element.759), channel_id=1, source_target_pairs={{0,1},{1,2},{2,3},{3,4},{4,5},{5,6},{6,7},{7,0},{8,9},{9,10},{10,1... | collective-permute-start | bytes 21512 | tf_op jit(solution)/shard_map/ppermute | solution.py:24
  94.6 4.4 %collective-permute-start.3 = (f32[7,1,256]{2,1,0:T(1,128)S(1)}, f32[7,1,256]{2,1,0:T(1,128)S(1)}, u32[]{:S(2)}, u32[]{:S(2)}) collective-permute-start(f32[7,1,256]{2,1,0:T(1,128)S(1)} %get-tuple-element.757), channel_id=1, source_target_pairs={{8,0},{16,8},{24,16},{32,24},{40,32},{48,40},{56,48},{64,56},{72,6... | collective-permute-start | bytes 21512 | tf_op jit(solution)/shard_map/ppermute | solution.py:25
  99.0 1.9 collective-permute-start.2
  101.0 6.6 %collective-permute-done.2 = f32[7,1,256]{2,1,0:T(1,128)S(1)} collective-permute-done((f32[7,1,256]{2,1,0:T(1,128)S(1)}, f32[7,1,256]{2,1,0:T(1,128)S(1)}, u32[]{:S(2)}, u32[]{:S(2)}) %collective-permute-start.2) | collective-permute-done | bytes 7200 | tf_op jit(solution)/shard_map/ppermute | solution.py:24
  107.7 2.2 copy.281
  109.9 14.1 %scatter_custom_fusion = f32[6,4096]{0,1:T(8,128)S(1)} fusion(s32[5120]{0:T(1024)S(1)} %bitcast.439, f32[5120,6]{1,0:T(8,128)} %copy.281, f32[]{:T(128)} %constant.571.clone.1), kind=kCustom, calls=%fused_computation.335 | custom fusion | bytes 98816 | tf_op jit(solution)/shard_map/scatter | solution.py:241
  124.0 2.6 fusion.253
  126.6 2.4 copy.335
  129.7 12.2 %while.92 = (s32[]{:T(128)}, f32[1,27,256]{2,1,0:T(8,128)S(1)}, s32[8,3,512]{2,1,0:T(4,128)}, f32[8,3,512]{2,1,0:T(4,128)S(1)}, s32[]{:T(128)}, /*index=5*/s32[]{:T(128)}, s32[]{}, s32[]{}) while((s32[]{:T(128)}, f32[1,27,256]{2,1,0:T(8,128)S(1)}, s32[8,3,512]{2,1,0:T(4,128)}, f32[8,3,512]{2,1,0:T(4,128)S(1)}, s32[]{:T(128)}, ...), condition=%wide.region_10.11_spmd.clone, body=%wide.region_9.10_spmd.clone.sunk | while | flops 43300868 | bytes 131215 | solution.py:82
  141.9 13.4 %while.93 = (s32[]{:T(128)}, f32[3,27,256]{2,1,0:T(8,128)S(1)}, f32[8,3,512]{2,1,0:T(4,128)S(1)}, s32[8,3,512]{2,1,0:T(4,128)}, f32[8,3,512]{2,1,0:T(4,128)S(1)}, /*index=5*/s32[]{:T(128)}, s32[]{:T(128)}, s32[]{}, s32[]{}) while((s32[]{:T(128)}, f32[3,27,256]{2,1,0:T(8,128)S(1)}, f32[8,3,512]{2,1,0:T(4,128)S(1)}, ...), condition=%wide.region_12.13_spmd.clone, body=%wide.region_11.12_spmd.clone.sunk | while | flops 128304640 | bytes 370843 | solution.py:82
  142.0 0.8 dynamic-slice_add_fusion.19
  145.3 0.8 dynamic-slice_add_fusion.19
  148.7 0.8 dynamic-slice_add_fusion.19
  150.3 0.8 dynamic-slice_add_fusion.19
  152.0 0.8 dynamic-slice_add_fusion.19
  153.7 0.8 dynamic-slice_add_fusion.19
  155.5 1.9 collective-permute-start.6
  157.4 7.6 %collective-permute-start.7 = (f32[1,9,2,256]{3,1,2,0:T(8,128)S(1)}, f32[1,9,2,256]{3,1,2,0:T(8,128)S(1)}, u32[]{:S(2)}, u32[]{:S(2)}) collective-permute-start(f32[1,9,2,256]{3,1,2,0:T(8,128)S(1)} %copy.341), channel_id=1, source_target_pairs={{8,0},{16,8},{24,16},{32,24},{40,32},{48,40},{56,48},{64,56},{72,6... | collective-permute-start | bytes 55304 | tf_op jit(solution)/shard_map/ppermute | solution.py:25
  165.0 1.9 collective-permute-start.9
  167.0 7.6 %collective-permute-start.8 = (f32[3,9,2,256]{3,1,2,0:T(8,128)S(1)}, f32[3,9,2,256]{3,1,2,0:T(8,128)S(1)}, u32[]{:S(2)}, u32[]{:S(2)}) collective-permute-start(f32[3,9,2,256]{3,1,2,0:T(8,128)S(1)} %copy.344), channel_id=1, source_target_pairs={{8,0},{16,8},{24,16},{32,24},{40,32},{48,40},{56,48},{64,56},{72,6... | collective-permute-start | bytes 165896 | tf_op jit(solution)/shard_map/ppermute | solution.py:25
  175.1 18.5 %all-gather.1 = f32[72,5,256]{2,1,0:T(8,128)S(1)} all-gather(f32[9,5,256]{2,1,0:T(8,128)S(1)} %fusion.141), channel_id=3, replica_groups=mesh['gx'=64,'gy'=8] {'gy'}, dimensions={0}, use_global_device_ids=true | all-gather | bytes 414720 | tf_op jit(solution)/shard_map/all_gather | solution.py:152
  194.6 14.8 %all_gather.14 = f32[2,72,3,256]{3,0,2,1:T(2,128)S(1)} all-gather(f32[2,9,3,256]{3,0,2,1:T(2,128)S(1)} %copy.298), channel_id=1, replica_groups=mesh['gx'=64,'gy'=8] {'gy'}, dimensions={1}, use_global_device_ids=true | all-gather | bytes 497664 | tf_op jit(solution)/shard_map/all_gather | solution.py:152
  210.4 16.8 %while.89 = (s32[]{:T(128)}, f32[8,4,4,512]{3,2,1,0:T(4,128)S(1)}, s32[8,3,512]{2,1,0:T(4,128)}, f32[8,3,512]{2,1,0:T(4,128)S(1)}, f32[108,256]{1,0:T(8,128)S(1)}, /*index=5*/s32[]{:T(128)}, s32[]{:T(128)}, s32[]{}, s32[]{}) while((s32[]{:T(128)}, f32[8,4,4,512]{3,2,1,0:T(4,128)S(1)}, s32[8,3,512]{2,1,0:T(4,128)}, ...), condition=%wide.region_18.19_spmd, body=%wide.region_13.18_spmd.sunk | while | flops 341865984 | bytes 4495505 | solution.py:112
  212.5 0.8 dynamic-slice_add_fusion.15
  216.7 0.8 dynamic-slice_add_fusion.15
  218.8 0.8 dynamic-slice_add_fusion.15
  228.2 2.8 gather_fusion.7
  231.3 2.2 collective-permute-start.10
  233.5 3.1 collective-permute-start.11
  236.6 2.6 collective-permute-start.12
  239.2 3.8 %collective-permute-start.13 = (f32[6,1,256]{2,1,0:T(1,128)S(1)}, f32[6,1,256]{2,1,0:T(1,128)S(1)}, u32[]{:S(2)}, u32[]{:S(2)}) collective-permute-start(f32[6,1,256]{2,1,0:T(1,128)S(1)} %get-tuple-element.771), channel_id=1, source_target_pairs={{0,1},{1,2},{2,3},{3,4},{4,5},{5,6},{6,7},{7,0},{8,9},{9,10},{10,1... | collective-permute-start | bytes 18440 | tf_op jit(solution)/shard_map/ppermute | solution.py:24
  243.0 14.1 %gather_fusion.6 = f32[4096,6]{1,0:T(8,128)} fusion(f32[6,4096]{0,1:T(8,128)S(1)} %copy.303, s32[4096]{0:T(1024)S(1)} %get-tuple-element.774), kind=kCustom, calls=%fused_computation.6 | custom fusion | bytes 212992 | tf_op jit(solution)/shard_map/gather | solution.py:258
  257.1 3.6 %select_bitcast_fusion = f32[6,4096]{0,1:T(8,128)S(1)} fusion(f32[4096,6]{1,0:T(8,128)} %gather_fusion.6, pred[4096]{0:T(1024)(128)(4,1)S(1)} %get-tuple-element.613), kind=kLoop, calls=%fused_computation.324 | loop fusion | flops 24576 | bytes 200704 | tf_op jit(solution)/shard_map/jit(_where)/select_n | solution.py:258
  261.0 4.1 %scatter_fusion = f32[6,4096]{0,1:T(8,128)S(1)} fusion(f32[6,4096]{0,1:T(8,128)S(1)} %select_bitcast_fusion, s32[1024]{0:T(1024)S(1)} %bitcast.440, f32[1024,6]{1,0:T(8,128)S(1)} %bitcast.355), kind=kCustom, calls=%fused_computation.9 | custom fusion | bytes 77824 | tf_op jit(solution)/shard_map/scatter | solution.py:260
  265.1 2.7 fusion.252
  267.8 2.2 copy.349
  270.1 13.4 %while.94 = (s32[]{:T(128)}, f32[3,27,256]{2,1,0:T(8,128)S(1)}, f32[8,3,512]{2,1,0:T(4,128)S(1)}, s32[8,3,512]{2,1,0:T(4,128)}, f32[8,3,512]{2,1,0:T(4,128)S(1)}, /*index=5*/s32[]{:T(128)}, s32[]{:T(128)}, s32[]{}, s32[]{}) while((s32[]{:T(128)}, f32[3,27,256]{2,1,0:T(8,128)S(1)}, f32[8,3,512]{2,1,0:T(4,128)S(1)}, ...), condition=%wide.region_22.23_spmd.clone, body=%wide.region_21.22_spmd.clone.sunk | while | flops 128304640 | bytes 370843 | solution.py:82
  270.1 0.9 dynamic-slice_add_fusion.20
  283.6 1.9 collective-permute-start.15
  285.6 7.6 %collective-permute-start.14 = (f32[3,9,2,256]{3,1,2,0:T(8,128)S(1)}, f32[3,9,2,256]{3,1,2,0:T(8,128)S(1)}, u32[]{:S(2)}, u32[]{:S(2)}) collective-permute-start(f32[3,9,2,256]{3,1,2,0:T(8,128)S(1)} %copy.352), channel_id=1, source_target_pairs={{8,0},{16,8},{24,16},{32,24},{40,32},{48,40},{56,48},{64,56},{72,6... | collective-permute-start | bytes 165896 | tf_op jit(solution)/shard_map/ppermute | solution.py:25
  294.3 1.2 collective-permute-done.14
  295.7 14.8 %all_gather.15 = f32[2,72,3,256]{3,0,2,1:T(2,128)S(1)} all-gather(f32[2,9,3,256]{3,0,2,1:T(2,128)S(1)} %copy.315), channel_id=1, replica_groups=mesh['gx'=64,'gy'=8] {'gy'}, dimensions={1}, use_global_device_ids=true | all-gather | bytes 497664 | tf_op jit(solution)/shard_map/all_gather | solution.py:152
  311.5 16.8 %while.90 = (s32[]{:T(128)}, f32[8,4,4,512]{3,2,1,0:T(4,128)S(1)}, s32[8,3,512]{2,1,0:T(4,128)}, f32[8,3,512]{2,1,0:T(4,128)S(1)}, f32[108,256]{1,0:T(8,128)S(1)}, /*index=5*/s32[]{:T(128)}, s32[]{:T(128)}, s32[]{}, s32[]{}) while((s32[]{:T(128)}, f32[8,4,4,512]{3,2,1,0:T(4,128)S(1)}, s32[8,3,512]{2,1,0:T(4,128)}, ...), condition=%wide.region_28.29_spmd, body=%wide.region_23.28_spmd.sunk | while | flops 341865984 | bytes 4495505 | solution.py:112
  (658 shorter events, 94.8 us)
Async XLA Ops:
  2.4 24.2 %copy-start.3 = (s32[4096]{0:T(1024)S(1)}, s32[4096]{0:T(1024)}, u32[]{:S(2)}) copy-start(s32[4096]{0:T(1024)} %param.26) | copy-start | bytes 49156
  14.7 34.8 %collective-permute-start = (f32[1,9,2,256]{3,1,2,0:T(8,128)S(1)}, f32[1,9,2,256]{3,1,2,0:T(8,128)S(1)}, u32[]{:S(2)}, u32[]{:S(2)}) collective-permute-start(f32[1,9,2,256]{3,1,2,0:T(8,128)S(1)} %copy.330), channel_id=1, source_target_pairs={{0,8},{8,16},{16,24},{24,32},{32,40},{40,48},{48,56},{56,64},{64,7... | collective-permute-start | bytes 55304 | tf_op jit(solution)/shard_map/ppermute | solution.py:24
  18.7 30.8 %collective-permute-start.1 = (f32[1,9,2,256]{3,1,2,0:T(8,128)S(1)}, f32[1,9,2,256]{3,1,2,0:T(8,128)S(1)}, u32[]{:S(2)}, u32[]{:S(2)}) collective-permute-start(f32[1,9,2,256]{3,1,2,0:T(8,128)S(1)} %copy.334), channel_id=1, source_target_pairs={{8,0},{16,8},{24,16},{32,24},{40,32},{48,40},{56,48},{64,56},{72,6... | collective-permute-start | bytes 55304 | tf_op jit(solution)/shard_map/ppermute | solution.py:25
  34.7 8.3 %copy-start = (s32[4096]{0:T(1024)S(1)}, s32[4096]{0:T(1024)}, u32[]{:S(2)}) copy-start(s32[4096]{0:T(1024)} %param.27) | copy-start | bytes 49156
  43.1 6.3 %copy-start.5 = (f32[3,4096]{1,0:T(4,128)S(1)}, f32[3,4096]{1,0:T(4,128)}, u32[]{:S(2)}) copy-start(f32[3,4096]{1,0:T(4,128)} %param.29) | copy-start | bytes 147460
  71.3 13.0 %copy-start.4 = (f32[3,4096]{1,0:T(4,128)S(1)}, f32[3,4096]{1,0:T(4,128)}, u32[]{:S(2)}) copy-start(f32[3,4096]{1,0:T(4,128)} %param.23) | copy-start | bytes 147460
  88.1 12.8 %collective-permute-start.5 = (f32[7,1,256]{2,1,0:T(1,128)S(1)}, f32[7,1,256]{2,1,0:T(1,128)S(1)}, u32[]{:S(2)}, u32[]{:S(2)}) collective-permute-start(f32[7,1,256]{2,1,0:T(1,128)S(1)} %get-tuple-element.758), channel_id=1, source_target_pairs={{1,0},{2,1},{3,2},{4,3},{5,4},{6,5},{7,6},{0,7},{9,8},{10,9},{11,1... | collective-permute-start | bytes 21512 | tf_op jit(solution)/shard_map/ppermute | solution.py:25
  90.2 10.8 %collective-permute-start.4 = (f32[7,1,256]{2,1,0:T(1,128)S(1)}, f32[7,1,256]{2,1,0:T(1,128)S(1)}, u32[]{:S(2)}, u32[]{:S(2)}) collective-permute-start(f32[7,1,256]{2,1,0:T(1,128)S(1)} %get-tuple-element.759), channel_id=1, source_target_pairs={{0,1},{1,2},{2,3},{3,4},{4,5},{5,6},{6,7},{7,0},{8,9},{9,10},{10,1... | collective-permute-start | bytes 21512 | tf_op jit(solution)/shard_map/ppermute | solution.py:24
  94.6 6.4 %collective-permute-start.3 = (f32[7,1,256]{2,1,0:T(1,128)S(1)}, f32[7,1,256]{2,1,0:T(1,128)S(1)}, u32[]{:S(2)}, u32[]{:S(2)}) collective-permute-start(f32[7,1,256]{2,1,0:T(1,128)S(1)} %get-tuple-element.757), channel_id=1, source_target_pairs={{8,0},{16,8},{24,16},{32,24},{40,32},{48,40},{56,48},{64,56},{72,6... | collective-permute-start | bytes 21512 | tf_op jit(solution)/shard_map/ppermute | solution.py:25
  99.0 8.6 %collective-permute-start.2 = (f32[7,1,256]{2,1,0:T(1,128)S(1)}, f32[7,1,256]{2,1,0:T(1,128)S(1)}, u32[]{:S(2)}, u32[]{:S(2)}) collective-permute-start(f32[7,1,256]{2,1,0:T(1,128)S(1)} %get-tuple-element.756), channel_id=1, source_target_pairs={{0,8},{8,16},{16,24},{24,32},{32,40},{40,48},{48,56},{56,64},{64,7... | collective-permute-start | bytes 21512 | tf_op jit(solution)/shard_map/ppermute | solution.py:24
  126.6 2.4 copy-start.2
  155.5 19.1 %collective-permute-start.6 = (f32[1,9,2,256]{3,1,2,0:T(8,128)S(1)}, f32[1,9,2,256]{3,1,2,0:T(8,128)S(1)}, u32[]{:S(2)}, u32[]{:S(2)}) collective-permute-start(f32[1,9,2,256]{3,1,2,0:T(8,128)S(1)} %copy.337), channel_id=1, source_target_pairs={{0,8},{8,16},{16,24},{24,32},{32,40},{40,48},{48,56},{56,64},{64,7... | collective-permute-start | bytes 55304 | tf_op jit(solution)/shard_map/ppermute | solution.py:24
  157.4 17.2 %collective-permute-start.7 = (f32[1,9,2,256]{3,1,2,0:T(8,128)S(1)}, f32[1,9,2,256]{3,1,2,0:T(8,128)S(1)}, u32[]{:S(2)}, u32[]{:S(2)}) collective-permute-start(f32[1,9,2,256]{3,1,2,0:T(8,128)S(1)} %copy.341), channel_id=1, source_target_pairs={{8,0},{16,8},{24,16},{32,24},{40,32},{48,40},{56,48},{64,56},{72,6... | collective-permute-start | bytes 55304 | tf_op jit(solution)/shard_map/ppermute | solution.py:25
  165.0 29.2 %collective-permute-start.9 = (f32[3,9,2,256]{3,1,2,0:T(8,128)S(1)}, f32[3,9,2,256]{3,1,2,0:T(8,128)S(1)}, u32[]{:S(2)}, u32[]{:S(2)}) collective-permute-start(f32[3,9,2,256]{3,1,2,0:T(8,128)S(1)} %copy.345), channel_id=1, source_target_pairs={{0,8},{8,16},{16,24},{24,32},{32,40},{40,48},{48,56},{56,64},{64,7... | collective-permute-start | bytes 165896 | tf_op jit(solution)/shard_map/ppermute | solution.py:24
  167.0 27.3 %collective-permute-start.8 = (f32[3,9,2,256]{3,1,2,0:T(8,128)S(1)}, f32[3,9,2,256]{3,1,2,0:T(8,128)S(1)}, u32[]{:S(2)}, u32[]{:S(2)}) collective-permute-start(f32[3,9,2,256]{3,1,2,0:T(8,128)S(1)} %copy.344), channel_id=1, source_target_pairs={{8,0},{16,8},{24,16},{32,24},{40,32},{48,40},{56,48},{64,56},{72,6... | collective-permute-start | bytes 165896 | tf_op jit(solution)/shard_map/ppermute | solution.py:25
  210.4 17.1 %copy-start.6 = (f32[3,4096]{1,0:T(4,128)S(1)}, f32[3,4096]{1,0:T(4,128)}, u32[]{:S(2)}) copy-start(f32[3,4096]{1,0:T(4,128)} %param.28) | copy-start | bytes 147460
  231.3 29.5 %collective-permute-start.10 = (f32[6,1,256]{2,1,0:T(1,128)S(1)}, f32[6,1,256]{2,1,0:T(1,128)S(1)}, u32[]{:S(2)}, u32[]{:S(2)}) collective-permute-start(f32[6,1,256]{2,1,0:T(1,128)S(1)} %get-tuple-element.770), channel_id=1, source_target_pairs={{8,0},{16,8},{24,16},{32,24},{40,32},{48,40},{56,48},{64,56},{72,6... | collective-permute-start | bytes 18440 | tf_op jit(solution)/shard_map/ppermute | solution.py:25
  233.5 27.3 %collective-permute-start.11 = (f32[6,1,256]{2,1,0:T(1,128)S(1)}, f32[6,1,256]{2,1,0:T(1,128)S(1)}, u32[]{:S(2)}, u32[]{:S(2)}) collective-permute-start(f32[6,1,256]{2,1,0:T(1,128)S(1)} %get-tuple-element.773), channel_id=1, source_target_pairs={{0,8},{8,16},{16,24},{24,32},{32,40},{40,48},{48,56},{56,64},{64,7... | collective-permute-start | bytes 18440 | tf_op jit(solution)/shard_map/ppermute | solution.py:24
  236.6 24.2 %collective-permute-start.12 = (f32[6,1,256]{2,1,0:T(1,128)S(1)}, f32[6,1,256]{2,1,0:T(1,128)S(1)}, u32[]{:S(2)}, u32[]{:S(2)}) collective-permute-start(f32[6,1,256]{2,1,0:T(1,128)S(1)} %get-tuple-element.772), channel_id=1, source_target_pairs={{1,0},{2,1},{3,2},{4,3},{5,4},{6,5},{7,6},{0,7},{9,8},{10,9},{11,1... | collective-permute-start | bytes 18440 | tf_op jit(solution)/shard_map/ppermute | solution.py:25
  239.2 21.6 %collective-permute-start.13 = (f32[6,1,256]{2,1,0:T(1,128)S(1)}, f32[6,1,256]{2,1,0:T(1,128)S(1)}, u32[]{:S(2)}, u32[]{:S(2)}) collective-permute-start(f32[6,1,256]{2,1,0:T(1,128)S(1)} %get-tuple-element.771), channel_id=1, source_target_pairs={{0,1},{1,2},{2,3},{3,4},{4,5},{5,6},{6,7},{7,0},{8,9},{9,10},{10,1... | collective-permute-start | bytes 18440 | tf_op jit(solution)/shard_map/ppermute | solution.py:24
  270.1 23.1 %copy-start.1 = (f32[3,4096]{0,1:T(8,128)S(1)}, f32[3,4096]{0,1:T(8,128)}, u32[]{:S(2)}) copy-start(f32[3,4096]{0,1:T(8,128)} %get-tuple-element.718) | copy-start | bytes 147460
  283.6 10.7 %collective-permute-start.15 = (f32[3,9,2,256]{3,1,2,0:T(8,128)S(1)}, f32[3,9,2,256]{3,1,2,0:T(8,128)S(1)}, u32[]{:S(2)}, u32[]{:S(2)}) collective-permute-start(f32[3,9,2,256]{3,1,2,0:T(8,128)S(1)} %copy.353), channel_id=1, source_target_pairs={{0,8},{8,16},{16,24},{24,32},{32,40},{40,48},{48,56},{56,64},{64,7... | collective-permute-start | bytes 165896 | tf_op jit(solution)/shard_map/ppermute | solution.py:24
  285.6 9.9 %collective-permute-start.14 = (f32[3,9,2,256]{3,1,2,0:T(8,128)S(1)}, f32[3,9,2,256]{3,1,2,0:T(8,128)S(1)}, u32[]{:S(2)}, u32[]{:S(2)}) collective-permute-start(f32[3,9,2,256]{3,1,2,0:T(8,128)S(1)} %copy.352), channel_id=1, source_target_pairs={{8,0},{16,8},{24,16},{32,24},{40,32},{48,40},{56,48},{64,56},{72,6... | collective-permute-start | bytes 165896 | tf_op jit(solution)/shard_map/ppermute | solution.py:25
where the time goes:
time: 334 us; the launch traced here: 329 us
  other arithmetic  71.2 us (21%)
  local copies, waits for them, and re-layouts  70.9 us (21%)
  blocking collectives  68.8 us (21%)
  starting transfers between devices  64.9 us (19%)
  matrix products  39.7 us (12%)
  waiting for transfers between devices  8.22 us (2%)
  loops' own time  3.7 us (1%)
    all_gather x4, blocking collectives, sum_lines(): gathered = lax.all_gather(field, 'gy', axis=1, tiled=True)  68.8 us
    add x56, other arithmetic, cloud_weights(): corner = (cell_block[1] * plane_count + cell_block[0])[None, :]  46.3 us
    ppermute x8, starting transfers between devices, with_halo(): after = lax.ppermute(first, axis, down)  41.8 us
    ppermute x8, starting transfers between devices, with_halo(): before = lax.ppermute(last, axis, up)  23 us
    dot_general x32, matrix products, add_block(): jnp.einsum('crb,zb->crz', spread, weights[3], precision=highest)  20.9 us
    dot_general x24, matrix products, one_block(): jnp.dot(flattened, columns, precision=highest, preferred_element_type=jnp...  15.9 us
    scatter x1, local copies, waits for them, and re-layouts, local(): arrived = jnp.zeros((6, particle_count), jnp.float32).at[:, placed].set(j...  14.1 us
    gather x1, local copies, waits for them, and re-layouts, local(): returning[:, slot_index]  14.1 us
  transfers between devices with their start and end apart: 16, of which 3 were waited for; matrix products, arithmetic and copies ran while one was open for 13% of the time, Pallas kernels for 0%

commit v1 on v0

--- a/solution.py
+++ b/solution.py
@@ -186,7 +186,8 @@
     group_size = jnp.sum(
         (destination[None, :] == jnp.arange(5, dtype=jnp.int32)[:, None]).astype(jnp.int32), axis=1
     )
-    opening = jnp.cumsum(group_size) - group_size
+    earlier = jnp.arange(5, dtype=jnp.int32)[None, :] < jnp.arange(5, dtype=jnp.int32)[:, None]
+    opening = jnp.sum(jnp.where(earlier, group_size[None, :], 0), axis=1)
     lane_index = jnp.arange(capacity, dtype=jnp.int32)
     chosen = jnp.stack(
         [

time: 334 us -> 334 us (level)
  no operation moved by 1% of the time
where the time goes in v1:
time: 334 us; the launch traced here: 329 us
  other arithmetic  71.1 us (21%)
  local copies, waits for them, and re-layouts  70.9 us (21%)
  blocking collectives  68.8 us (21%)
  starting transfers between devices  64.9 us (19%)
  matrix products  39.7 us (12%)
  waiting for transfers between devices  8.23 us (2%)
  loops' own time  3.7 us (1%)
    all_gather x4, blocking collectives, sum_lines(): gathered = lax.all_gather(field, 'gy', axis=1, tiled=True)  68.8 us
    add x56, other arithmetic, cloud_weights(): corner = (cell_block[1] * plane_count + cell_block[0])[None, :]  46.3 us
    ppermute x8, starting transfers between devices, with_halo(): after = lax.ppermute(first, axis, down)  41.8 us
    ppermute x8, starting transfers between devices, with_halo(): before = lax.ppermute(last, axis, up)  23 us
    dot_general x32, matrix products, add_block(): jnp.einsum('crb,zb->crz', spread, weights[3], precision=highest)  20.9 us
    dot_general x24, matrix products, one_block(): jnp.dot(flattened, columns, precision=highest, preferred_element_type=jnp...  15.9 us
    scatter x1, local copies, waits for them, and re-layouts, local(): arrived = jnp.zeros((6, particle_count), jnp.float32).at[:, placed].set(j...  14.1 us
    gather x1, local copies, waits for them, and re-layouts, local(): returning[:, slot_index]  14.1 us
  transfers between devices with their start and end apart: 16, of which 3 were waited for; matrix products, arithmetic and copies ran while one was open for 13% of the time, Pallas kernels for 0%

profile of v1, /device:TPU:1, one launch (start us, length us, event | category | flops | bytes accessed | tf_op | source)
XLA Modules:
  0.0 329.2 jit_solution(8306297615378816670)
XLA Ops:
  1.4 1.0 maximum_subtract_fusion
  2.4 12.2 %while.91 = (s32[]{:T(128)}, f32[1,27,256]{2,1,0:T(8,128)S(1)}, s32[8,3,512]{2,1,0:T(4,128)}, f32[8,3,512]{2,1,0:T(4,128)S(1)}, s32[]{:T(128)}, /*index=5*/s32[]{:T(128)}, s32[]{}, s32[]{}) while((s32[]{:T(128)}, f32[1,27,256]{2,1,0:T(8,128)S(1)}, s32[8,3,512]{2,1,0:T(4,128)}, f32[8,3,512]{2,1,0:T(4,128)S(1)}, s32[]{:T(128)}, ...), condition=%wide.region_2.3_spmd.clone, body=%wide.region_1.2_spmd.clone.sunk | while | flops 43300868 | bytes 131215 | solution.py:82
  2.5 0.8 dynamic-slice_add_fusion.17
  4.0 0.8 dynamic-slice_add_fusion.17
  5.5 0.8 dynamic-slice_add_fusion.17
  7.0 0.8 dynamic-slice_add_fusion.17
  8.5 0.8 dynamic-slice_add_fusion.17
  10.1 0.8 dynamic-slice_add_fusion.17
  11.6 0.8 dynamic-slice_add_fusion.17
  13.1 0.8 dynamic-slice_add_fusion.17
  14.7 4.0 %collective-permute-start = (f32[1,9,2,256]{3,1,2,0:T(8,128)S(1)}, f32[1,9,2,256]{3,1,2,0:T(8,128)S(1)}, u32[]{:S(2)}, u32[]{:S(2)}) collective-permute-start(f32[1,9,2,256]{3,1,2,0:T(8,128)S(1)} %copy.330), channel_id=1, source_target_pairs={{0,8},{8,16},{16,24},{24,32},{32,40},{40,48},{48,56},{56,64},{64,7... | collective-permute-start | bytes 55304 | tf_op jit(solution)/shard_map/ppermute | solution.py:24
  18.7 7.8 %collective-permute-start.1 = (f32[1,9,2,256]{3,1,2,0:T(8,128)S(1)}, f32[1,9,2,256]{3,1,2,0:T(8,128)S(1)}, u32[]{:S(2)}, u32[]{:S(2)}) collective-permute-start(f32[1,9,2,256]{3,1,2,0:T(8,128)S(1)} %copy.334), channel_id=1, source_target_pairs={{8,0},{16,8},{24,16},{32,24},{40,32},{48,40},{56,48},{64,56},{72,6... | collective-permute-start | bytes 55304 | tf_op jit(solution)/shard_map/ppermute | solution.py:25
  28.8 5.8 %sort.17 = (s32[4096]{0:T(1024)}, s32[4096]{0:T(1024)S(1)}) sort(s32[4096]{0:T(1024)S(1)} %copy-done.3, s32[4096]{0:T(1024)S(1)} %iota.435), dimensions={0}, to_apply=%region_6.7 | sort | flops 49152 | bytes 65536 | tf_op jit(solution)/shard_map/jit(argsort)/sort | solution.py:185
  34.6 1.7 gather_fusion
  36.4 1.7 gather_fusion.1
  39.4 1.7 gather_fusion.2
  41.1 1.7 gather_fusion.3
  43.0 6.2 %gather_fusion.5 = s32[1024]{0:T(1024)S(1)} fusion(s32[4096]{0:T(1024)S(1)} %copy-done, s32[1024]{0:T(1024)S(1)} %broadcast_clamp_fusion.1), kind=kCustom, calls=%fused_computation.5 | custom fusion | bytes 12288 | tf_op jit(solution)/shard_map/gather | solution.py:229
  49.8 20.6 %all-gather = f32[72,5,256]{2,1,0:T(8,128)S(1)} all-gather(f32[9,5,256]{2,1,0:T(8,128)S(1)} %fusion.143), channel_id=2, replica_groups=mesh['gx'=64,'gy'=8] {'gy'}, dimensions={0}, use_global_device_ids=true | all-gather | bytes 414720 | tf_op jit(solution)/shard_map/all_gather | solution.py:152
  71.3 12.9 %while.88 = (s32[]{:T(128)}, f32[8,1,3,512]{3,2,1,0:T(4,128)S(1)}, s32[8,3,512]{2,1,0:T(4,128)}, f32[8,3,512]{2,1,0:T(4,128)S(1)}, f32[81,256]{1,0:T(8,128)S(1)}, /*index=5*/s32[]{:T(128)}, s32[]{:T(128)}, s32[]{}, s32[]{}) while((s32[]{:T(128)}, f32[8,1,3,512]{3,2,1,0:T(4,128)S(1)}, s32[8,3,512]{2,1,0:T(4,128)}, f32[8,3,512]{2,1,0:T(4,128)S(1)}, ...), condition=%wide.region_5.6_spmd, body=%wide.region_3.5_spmd.sunk | while | flops 128303104 | bytes 955537 | solution.py:112
  71.3 0.8 dynamic-slice_add_fusion.14
  74.6 0.8 dynamic-slice_add_fusion.14
  76.2 0.8 dynamic-slice_add_fusion.14
  79.4 0.8 dynamic-slice_add_fusion.14
  85.0 2.8 gather_fusion.4
  88.0 2.1 collective-permute-start.5
  90.1 4.4 %collective-permute-start.4 = (f32[7,1,256]{2,1,0:T(1,128)S(1)}, f32[7,1,256]{2,1,0:T(1,128)S(1)}, u32[]{:S(2)}, u32[]{:S(2)}) collective-permute-start(f32[7,1,256]{2,1,0:T(1,128)S(1)} %get-tuple-element.759), channel_id=1, source_target_pairs={{0,1},{1,2},{2,3},{3,4},{4,5},{5,6},{6,7},{7,0},{8,9},{9,10},{10,1... | collective-permute-start | bytes 21512 | tf_op jit(solution)/shard_map/ppermute | solution.py:24
  94.5 4.4 %collective-permute-start.3 = (f32[7,1,256]{2,1,0:T(1,128)S(1)}, f32[7,1,256]{2,1,0:T(1,128)S(1)}, u32[]{:S(2)}, u32[]{:S(2)}) collective-permute-start(f32[7,1,256]{2,1,0:T(1,128)S(1)} %get-tuple-element.757), channel_id=1, source_target_pairs={{8,0},{16,8},{24,16},{32,24},{40,32},{48,40},{56,48},{64,56},{72,6... | collective-permute-start | bytes 21512 | tf_op jit(solution)/shard_map/ppermute | solution.py:25
  98.9 1.9 collective-permute-start.2
  100.9 6.6 %collective-permute-done.2 = f32[7,1,256]{2,1,0:T(1,128)S(1)} collective-permute-done((f32[7,1,256]{2,1,0:T(1,128)S(1)}, f32[7,1,256]{2,1,0:T(1,128)S(1)}, u32[]{:S(2)}, u32[]{:S(2)}) %collective-permute-start.2) | collective-permute-done | bytes 7200 | tf_op jit(solution)/shard_map/ppermute | solution.py:24
  107.6 2.2 copy.281
  109.9 14.1 %scatter_custom_fusion = f32[6,4096]{0,1:T(8,128)S(1)} fusion(s32[5120]{0:T(1024)S(1)} %bitcast.436, f32[5120,6]{1,0:T(8,128)} %copy.281, f32[]{:T(128)} %constant.568.clone.1), kind=kCustom, calls=%fused_computation.335 | custom fusion | bytes 98816 | tf_op jit(solution)/shard_map/scatter | solution.py:242
  123.9 2.6 fusion.253
  126.6 2.4 copy.335
  129.6 12.2 %while.92 = (s32[]{:T(128)}, f32[1,27,256]{2,1,0:T(8,128)S(1)}, s32[8,3,512]{2,1,0:T(4,128)}, f32[8,3,512]{2,1,0:T(4,128)S(1)}, s32[]{:T(128)}, /*index=5*/s32[]{:T(128)}, s32[]{}, s32[]{}) while((s32[]{:T(128)}, f32[1,27,256]{2,1,0:T(8,128)S(1)}, s32[8,3,512]{2,1,0:T(4,128)}, f32[8,3,512]{2,1,0:T(4,128)S(1)}, s32[]{:T(128)}, ...), condition=%wide.region_10.11_spmd.clone, body=%wide.region_9.10_spmd.clone.sunk | while | flops 43300868 | bytes 131215 | solution.py:82
  141.9 13.4 %while.93 = (s32[]{:T(128)}, f32[3,27,256]{2,1,0:T(8,128)S(1)}, f32[8,3,512]{2,1,0:T(4,128)S(1)}, s32[8,3,512]{2,1,0:T(4,128)}, f32[8,3,512]{2,1,0:T(4,128)S(1)}, /*index=5*/s32[]{:T(128)}, s32[]{:T(128)}, s32[]{}, s32[]{}) while((s32[]{:T(128)}, f32[3,27,256]{2,1,0:T(8,128)S(1)}, f32[8,3,512]{2,1,0:T(4,128)S(1)}, ...), condition=%wide.region_12.13_spmd.clone, body=%wide.region_11.12_spmd.clone.sunk | while | flops 128304640 | bytes 370843 | solution.py:82
  141.9 0.8 dynamic-slice_add_fusion.19
  150.3 0.8 dynamic-slice_add_fusion.19
  153.6 0.8 dynamic-slice_add_fusion.19
  155.4 1.9 collective-permute-start.6
  157.4 7.6 %collective-permute-start.7 = (f32[1,9,2,256]{3,1,2,0:T(8,128)S(1)}, f32[1,9,2,256]{3,1,2,0:T(8,128)S(1)}, u32[]{:S(2)}, u32[]{:S(2)}) collective-permute-start(f32[1,9,2,256]{3,1,2,0:T(8,128)S(1)} %copy.341), channel_id=1, source_target_pairs={{8,0},{16,8},{24,16},{32,24},{40,32},{48,40},{56,48},{64,56},{72,6... | collective-permute-start | bytes 55304 | tf_op jit(solution)/shard_map/ppermute | solution.py:25
  165.0 1.9 collective-permute-start.9
  166.9 7.6 %collective-permute-start.8 = (f32[3,9,2,256]{3,1,2,0:T(8,128)S(1)}, f32[3,9,2,256]{3,1,2,0:T(8,128)S(1)}, u32[]{:S(2)}, u32[]{:S(2)}) collective-permute-start(f32[3,9,2,256]{3,1,2,0:T(8,128)S(1)} %copy.344), channel_id=1, source_target_pairs={{8,0},{16,8},{24,16},{32,24},{40,32},{48,40},{56,48},{64,56},{72,6... | collective-permute-start | bytes 165896 | tf_op jit(solution)/shard_map/ppermute | solution.py:25
  175.0 18.5 %all-gather.1 = f32[72,5,256]{2,1,0:T(8,128)S(1)} all-gather(f32[9,5,256]{2,1,0:T(8,128)S(1)} %fusion.141), channel_id=3, replica_groups=mesh['gx'=64,'gy'=8] {'gy'}, dimensions={0}, use_global_device_ids=true | all-gather | bytes 414720 | tf_op jit(solution)/shard_map/all_gather | solution.py:152
  194.5 14.8 %all_gather.14 = f32[2,72,3,256]{3,0,2,1:T(2,128)S(1)} all-gather(f32[2,9,3,256]{3,0,2,1:T(2,128)S(1)} %copy.298), channel_id=1, replica_groups=mesh['gx'=64,'gy'=8] {'gy'}, dimensions={1}, use_global_device_ids=true | all-gather | bytes 497664 | tf_op jit(solution)/shard_map/all_gather | solution.py:152
  210.3 16.8 %while.89 = (s32[]{:T(128)}, f32[8,4,4,512]{3,2,1,0:T(4,128)S(1)}, s32[8,3,512]{2,1,0:T(4,128)}, f32[8,3,512]{2,1,0:T(4,128)S(1)}, f32[108,256]{1,0:T(8,128)S(1)}, /*index=5*/s32[]{:T(128)}, s32[]{:T(128)}, s32[]{}, s32[]{}) while((s32[]{:T(128)}, f32[8,4,4,512]{3,2,1,0:T(4,128)S(1)}, s32[8,3,512]{2,1,0:T(4,128)}, ...), condition=%wide.region_18.19_spmd, body=%wide.region_13.18_spmd.sunk | while | flops 341865984 | bytes 4495505 | solution.py:112
  212.4 0.8 dynamic-slice_add_fusion.15
  228.1 2.8 gather_fusion.7
  231.2 2.2 collective-permute-start.10
  233.4 3.1 collective-permute-start.11
  236.5 2.6 collective-permute-start.12
  239.1 3.8 %collective-permute-start.13 = (f32[6,1,256]{2,1,0:T(1,128)S(1)}, f32[6,1,256]{2,1,0:T(1,128)S(1)}, u32[]{:S(2)}, u32[]{:S(2)}) collective-permute-start(f32[6,1,256]{2,1,0:T(1,128)S(1)} %get-tuple-element.771), channel_id=1, source_target_pairs={{0,1},{1,2},{2,3},{3,4},{4,5},{5,6},{6,7},{7,0},{8,9},{9,10},{10,1... | collective-permute-start | bytes 18440 | tf_op jit(solution)/shard_map/ppermute | solution.py:24
  243.0 14.1 %gather_fusion.6 = f32[4096,6]{1,0:T(8,128)} fusion(f32[6,4096]{0,1:T(8,128)S(1)} %copy.303, s32[4096]{0:T(1024)S(1)} %get-tuple-element.774), kind=kCustom, calls=%fused_computation.6 | custom fusion | bytes 212992 | tf_op jit(solution)/shard_map/gather | solution.py:259
  257.0 3.6 %select_bitcast_fusion = f32[6,4096]{0,1:T(8,128)S(1)} fusion(f32[4096,6]{1,0:T(8,128)} %gather_fusion.6, pred[4096]{0:T(1024)(128)(4,1)S(1)} %get-tuple-element.613), kind=kLoop, calls=%fused_computation.324 | loop fusion | flops 24576 | bytes 200704 | tf_op jit(solution)/shard_map/jit(_where)/select_n | solution.py:259
  260.9 4.1 %scatter_fusion = f32[6,4096]{0,1:T(8,128)S(1)} fusion(f32[6,4096]{0,1:T(8,128)S(1)} %select_bitcast_fusion, s32[1024]{0:T(1024)S(1)} %bitcast.437, f32[1024,6]{1,0:T(8,128)S(1)} %bitcast.352), kind=kCustom, calls=%fused_computation.9 | custom fusion | bytes 77824 | tf_op jit(solution)/shard_map/scatter | solution.py:261
  265.0 2.7 fusion.252
  267.7 2.2 copy.349
  270.0 13.4 %while.94 = (s32[]{:T(128)}, f32[3,27,256]{2,1,0:T(8,128)S(1)}, f32[8,3,512]{2,1,0:T(4,128)S(1)}, s32[8,3,512]{2,1,0:T(4,128)}, f32[8,3,512]{2,1,0:T(4,128)S(1)}, /*index=5*/s32[]{:T(128)}, s32[]{:T(128)}, s32[]{}, s32[]{}) while((s32[]{:T(128)}, f32[3,27,256]{2,1,0:T(8,128)S(1)}, f32[8,3,512]{2,1,0:T(4,128)S(1)}, ...), condition=%wide.region_22.23_spmd.clone, body=%wide.region_21.22_spmd.clone.sunk | while | flops 128304640 | bytes 370843 | solution.py:82
  270.0 0.9 dynamic-slice_add_fusion.20
  283.5 1.9 collective-permute-start.15
  285.5 7.6 %collective-permute-start.14 = (f32[3,9,2,256]{3,1,2,0:T(8,128)S(1)}, f32[3,9,2,256]{3,1,2,0:T(8,128)S(1)}, u32[]{:S(2)}, u32[]{:S(2)}) collective-permute-start(f32[3,9,2,256]{3,1,2,0:T(8,128)S(1)} %copy.352), channel_id=1, source_target_pairs={{8,0},{16,8},{24,16},{32,24},{40,32},{48,40},{56,48},{64,56},{72,6... | collective-permute-start | bytes 165896 | tf_op jit(solution)/shard_map/ppermute | solution.py:25
  294.2 1.2 collective-permute-done.14
  295.7 14.8 %all_gather.15 = f32[2,72,3,256]{3,0,2,1:T(2,128)S(1)} all-gather(f32[2,9,3,256]{3,0,2,1:T(2,128)S(1)} %copy.315), channel_id=1, replica_groups=mesh['gx'=64,'gy'=8] {'gy'}, dimensions={1}, use_global_device_ids=true | all-gather | bytes 497664 | tf_op jit(solution)/shard_map/all_gather | solution.py:152
  311.4 16.8 %while.90 = (s32[]{:T(128)}, f32[8,4,4,512]{3,2,1,0:T(4,128)S(1)}, s32[8,3,512]{2,1,0:T(4,128)}, f32[8,3,512]{2,1,0:T(4,128)S(1)}, f32[108,256]{1,0:T(8,128)S(1)}, /*index=5*/s32[]{:T(128)}, s32[]{:T(128)}, s32[]{}, s32[]{}) while((s32[]{:T(128)}, f32[8,4,4,512]{3,2,1,0:T(4,128)S(1)}, s32[8,3,512]{2,1,0:T(4,128)}, ...), condition=%wide.region_28.29_spmd, body=%wide.region_23.28_spmd.sunk | while | flops 341865984 | bytes 4495505 | solution.py:112
  (657 shorter events, 94.8 us)
Async XLA Ops:
  2.4 24.2 %copy-start.3 = (s32[4096]{0:T(1024)S(1)}, s32[4096]{0:T(1024)}, u32[]{:S(2)}) copy-start(s32[4096]{0:T(1024)} %param.26) | copy-start | bytes 49156
  14.7 34.7 %collective-permute-start = (f32[1,9,2,256]{3,1,2,0:T(8,128)S(1)}, f32[1,9,2,256]{3,1,2,0:T(8,128)S(1)}, u32[]{:S(2)}, u32[]{:S(2)}) collective-permute-start(f32[1,9,2,256]{3,1,2,0:T(8,128)S(1)} %copy.330), channel_id=1, source_target_pairs={{0,8},{8,16},{16,24},{24,32},{32,40},{40,48},{48,56},{56,64},{64,7... | collective-permute-start | bytes 55304 | tf_op jit(solution)/shard_map/ppermute | solution.py:24
  18.7 30.7 %collective-permute-start.1 = (f32[1,9,2,256]{3,1,2,0:T(8,128)S(1)}, f32[1,9,2,256]{3,1,2,0:T(8,128)S(1)}, u32[]{:S(2)}, u32[]{:S(2)}) collective-permute-start(f32[1,9,2,256]{3,1,2,0:T(8,128)S(1)} %copy.334), channel_id=1, source_target_pairs={{8,0},{16,8},{24,16},{32,24},{40,32},{48,40},{56,48},{64,56},{72,6... | collective-permute-start | bytes 55304 | tf_op jit(solution)/shard_map/ppermute | solution.py:25
  34.6 8.3 %copy-start = (s32[4096]{0:T(1024)S(1)}, s32[4096]{0:T(1024)}, u32[]{:S(2)}) copy-start(s32[4096]{0:T(1024)} %param.27) | copy-start | bytes 49156
  43.0 6.3 %copy-start.5 = (f32[3,4096]{1,0:T(4,128)S(1)}, f32[3,4096]{1,0:T(4,128)}, u32[]{:S(2)}) copy-start(f32[3,4096]{1,0:T(4,128)} %param.29) | copy-start | bytes 147460
  71.3 13.0 %copy-start.4 = (f32[3,4096]{1,0:T(4,128)S(1)}, f32[3,4096]{1,0:T(4,128)}, u32[]{:S(2)}) copy-start(f32[3,4096]{1,0:T(4,128)} %param.23) | copy-start | bytes 147460
  88.0 12.8 %collective-permute-start.5 = (f32[7,1,256]{2,1,0:T(1,128)S(1)}, f32[7,1,256]{2,1,0:T(1,128)S(1)}, u32[]{:S(2)}, u32[]{:S(2)}) collective-permute-start(f32[7,1,256]{2,1,0:T(1,128)S(1)} %get-tuple-element.758), channel_id=1, source_target_pairs={{1,0},{2,1},{3,2},{4,3},{5,4},{6,5},{7,6},{0,7},{9,8},{10,9},{11,1... | collective-permute-start | bytes 21512 | tf_op jit(solution)/shard_map/ppermute | solution.py:25
  90.1 10.8 %collective-permute-start.4 = (f32[7,1,256]{2,1,0:T(1,128)S(1)}, f32[7,1,256]{2,1,0:T(1,128)S(1)}, u32[]{:S(2)}, u32[]{:S(2)}) collective-permute-start(f32[7,1,256]{2,1,0:T(1,128)S(1)} %get-tuple-element.759), channel_id=1, source_target_pairs={{0,1},{1,2},{2,3},{3,4},{4,5},{5,6},{6,7},{7,0},{8,9},{9,10},{10,1... | collective-permute-start | bytes 21512 | tf_op jit(solution)/shard_map/ppermute | solution.py:24
  94.5 6.4 %collective-permute-start.3 = (f32[7,1,256]{2,1,0:T(1,128)S(1)}, f32[7,1,256]{2,1,0:T(1,128)S(1)}, u32[]{:S(2)}, u32[]{:S(2)}) collective-permute-start(f32[7,1,256]{2,1,0:T(1,128)S(1)} %get-tuple-element.757), channel_id=1, source_target_pairs={{8,0},{16,8},{24,16},{32,24},{40,32},{48,40},{56,48},{64,56},{72,6... | collective-permute-start | bytes 21512 | tf_op jit(solution)/shard_map/ppermute | solution.py:25
  98.9 8.6 %collective-permute-start.2 = (f32[7,1,256]{2,1,0:T(1,128)S(1)}, f32[7,1,256]{2,1,0:T(1,128)S(1)}, u32[]{:S(2)}, u32[]{:S(2)}) collective-permute-start(f32[7,1,256]{2,1,0:T(1,128)S(1)} %get-tuple-element.756), channel_id=1, source_target_pairs={{0,8},{8,16},{16,24},{24,32},{32,40},{40,48},{48,56},{56,64},{64,7... | collective-permute-start | bytes 21512 | tf_op jit(solution)/shard_map/ppermute | solution.py:24
  126.6 2.4 copy-start.2
  155.4 19.1 %collective-permute-start.6 = (f32[1,9,2,256]{3,1,2,0:T(8,128)S(1)}, f32[1,9,2,256]{3,1,2,0:T(8,128)S(1)}, u32[]{:S(2)}, u32[]{:S(2)}) collective-permute-start(f32[1,9,2,256]{3,1,2,0:T(8,128)S(1)} %copy.337), channel_id=1, source_target_pairs={{0,8},{8,16},{16,24},{24,32},{32,40},{40,48},{48,56},{56,64},{64,7... | collective-permute-start | bytes 55304 | tf_op jit(solution)/shard_map/ppermute | solution.py:24
  157.4 17.2 %collective-permute-start.7 = (f32[1,9,2,256]{3,1,2,0:T(8,128)S(1)}, f32[1,9,2,256]{3,1,2,0:T(8,128)S(1)}, u32[]{:S(2)}, u32[]{:S(2)}) collective-permute-start(f32[1,9,2,256]{3,1,2,0:T(8,128)S(1)} %copy.341), channel_id=1, source_target_pairs={{8,0},{16,8},{24,16},{32,24},{40,32},{48,40},{56,48},{64,56},{72,6... | collective-permute-start | bytes 55304 | tf_op jit(solution)/shard_map/ppermute | solution.py:25
  165.0 29.2 %collective-permute-start.9 = (f32[3,9,2,256]{3,1,2,0:T(8,128)S(1)}, f32[3,9,2,256]{3,1,2,0:T(8,128)S(1)}, u32[]{:S(2)}, u32[]{:S(2)}) collective-permute-start(f32[3,9,2,256]{3,1,2,0:T(8,128)S(1)} %copy.345), channel_id=1, source_target_pairs={{0,8},{8,16},{16,24},{24,32},{32,40},{40,48},{48,56},{56,64},{64,7... | collective-permute-start | bytes 165896 | tf_op jit(solution)/shard_map/ppermute | solution.py:24
  166.9 27.3 %collective-permute-start.8 = (f32[3,9,2,256]{3,1,2,0:T(8,128)S(1)}, f32[3,9,2,256]{3,1,2,0:T(8,128)S(1)}, u32[]{:S(2)}, u32[]{:S(2)}) collective-permute-start(f32[3,9,2,256]{3,1,2,0:T(8,128)S(1)} %copy.344), channel_id=1, source_target_pairs={{8,0},{16,8},{24,16},{32,24},{40,32},{48,40},{56,48},{64,56},{72,6... | collective-permute-start | bytes 165896 | tf_op jit(solution)/shard_map/ppermute | solution.py:25
  210.3 17.1 %copy-start.6 = (f32[3,4096]{1,0:T(4,128)S(1)}, f32[3,4096]{1,0:T(4,128)}, u32[]{:S(2)}) copy-start(f32[3,4096]{1,0:T(4,128)} %param.28) | copy-start | bytes 147460
  231.2 29.5 %collective-permute-start.10 = (f32[6,1,256]{2,1,0:T(1,128)S(1)}, f32[6,1,256]{2,1,0:T(1,128)S(1)}, u32[]{:S(2)}, u32[]{:S(2)}) collective-permute-start(f32[6,1,256]{2,1,0:T(1,128)S(1)} %get-tuple-element.770), channel_id=1, source_target_pairs={{8,0},{16,8},{24,16},{32,24},{40,32},{48,40},{56,48},{64,56},{72,6... | collective-permute-start | bytes 18440 | tf_op jit(solution)/shard_map/ppermute | solution.py:25
  233.4 27.3 %collective-permute-start.11 = (f32[6,1,256]{2,1,0:T(1,128)S(1)}, f32[6,1,256]{2,1,0:T(1,128)S(1)}, u32[]{:S(2)}, u32[]{:S(2)}) collective-permute-start(f32[6,1,256]{2,1,0:T(1,128)S(1)} %get-tuple-element.773), channel_id=1, source_target_pairs={{0,8},{8,16},{16,24},{24,32},{32,40},{40,48},{48,56},{56,64},{64,7... | collective-permute-start | bytes 18440 | tf_op jit(solution)/shard_map/ppermute | solution.py:24
  236.5 24.2 %collective-permute-start.12 = (f32[6,1,256]{2,1,0:T(1,128)S(1)}, f32[6,1,256]{2,1,0:T(1,128)S(1)}, u32[]{:S(2)}, u32[]{:S(2)}) collective-permute-start(f32[6,1,256]{2,1,0:T(1,128)S(1)} %get-tuple-element.772), channel_id=1, source_target_pairs={{1,0},{2,1},{3,2},{4,3},{5,4},{6,5},{7,6},{0,7},{9,8},{10,9},{11,1... | collective-permute-start | bytes 18440 | tf_op jit(solution)/shard_map/ppermute | solution.py:25
  239.1 21.6 %collective-permute-start.13 = (f32[6,1,256]{2,1,0:T(1,128)S(1)}, f32[6,1,256]{2,1,0:T(1,128)S(1)}, u32[]{:S(2)}, u32[]{:S(2)}) collective-permute-start(f32[6,1,256]{2,1,0:T(1,128)S(1)} %get-tuple-element.771), channel_id=1, source_target_pairs={{0,1},{1,2},{2,3},{3,4},{4,5},{5,6},{6,7},{7,0},{8,9},{9,10},{10,1... | collective-permute-start | bytes 18440 | tf_op jit(solution)/shard_map/ppermute | solution.py:24
  270.0 23.1 %copy-start.1 = (f32[3,4096]{0,1:T(8,128)S(1)}, f32[3,4096]{0,1:T(8,128)}, u32[]{:S(2)}) copy-start(f32[3,4096]{0,1:T(8,128)} %get-tuple-element.718) | copy-start | bytes 147460
  283.5 10.7 %collective-permute-start.15 = (f32[3,9,2,256]{3,1,2,0:T(8,128)S(1)}, f32[3,9,2,256]{3,1,2,0:T(8,128)S(1)}, u32[]{:S(2)}, u32[]{:S(2)}) collective-permute-start(f32[3,9,2,256]{3,1,2,0:T(8,128)S(1)} %copy.353), channel_id=1, source_target_pairs={{0,8},{8,16},{16,24},{24,32},{32,40},{40,48},{48,56},{56,64},{64,7... | collective-permute-start | bytes 165896 | tf_op jit(solution)/shard_map/ppermute | solution.py:24
  285.5 9.9 %collective-permute-start.14 = (f32[3,9,2,256]{3,1,2,0:T(8,128)S(1)}, f32[3,9,2,256]{3,1,2,0:T(8,128)S(1)}, u32[]{:S(2)}, u32[]{:S(2)}) collective-permute-start(f32[3,9,2,256]{3,1,2,0:T(8,128)S(1)} %copy.352), channel_id=1, source_target_pairs={{8,0},{16,8},{24,16},{32,24},{40,32},{48,40},{56,48},{64,56},{72,6... | collective-permute-start | bytes 165896 | tf_op jit(solution)/shard_map/ppermute | solution.py:25

commit v2 on v0

v2 whole, which is shorter than its diff:
```python
import functools

import jax
import jax.numpy as jnp
from jax import lax
from jax.experimental import pallas as pl
from jax.experimental.pallas import tpu as pltpu
from jax.sharding import PartitionSpec as P

CX = 2
CY = 8
NZ = 256
NQ = 4096
BLK = 256
ROWS = 16
TABLES = 5
STEP = 0.25
STRENGTH = 0.02
F32 = jnp.float32
BF16 = jnp.bfloat16
highest = lax.Precision.HIGHEST
VMEM_LIMIT = 48 * 1024 * 1024


def shape(*dims, dtype=F32):
    return jax.ShapeDtypeStruct(dims, dtype)


def call(body, outs, scratch=()):
    return pl.pallas_call(
        body,
        out_shape=outs,
        scratch_shapes=list(scratch),
        compiler_params=pltpu.CompilerParams(vmem_limit_bytes=VMEM_LIMIT),
    )


def split(x):
    high = x.astype(BF16)
    return high, (x - high.astype(F32)).astype(BF16)


def one_hot(index):
    rows = lax.broadcasted_iota(jnp.int32, (256, index.shape[1]), 0)
    return jnp.where(rows == index, 1.0, 0.0).astype(BF16)


def spread_onto(values, hot):
    return lax.dot_general(values, hot, (((1,), (1,)), ((), ())), preferred_element_type=F32)


def pick_from(table, hot):
    return jnp.dot(table, hot, preferred_element_type=F32)


def next_z(x):
    return pltpu.roll(x, NZ - 1, 1)


def prev_z(x):
    return pltpu.roll(x, 1, 1)


def diff_z(x):
    return 0.5 * (next_z(x) - prev_z(x))


def diff_row(x):
    return 0.5 * (pltpu.roll(x, ROWS - 1, 0) - pltpu.roll(x, 1, 0))


def axis_hits(rows, pitch, padded, cell_x, cell_y):
    index = lax.broadcasted_iota(jnp.int32, (padded, cell_x.shape[1]), 0)
    row_x = index // pitch
    row_y = index - row_x * pitch
    away_x = row_x - cell_x
    away_y = row_y - cell_y
    return away_x == 0, away_x == 1, away_y == 0, away_y == 1


def weights_of(hits, frac_x, frac_y):
    low_x, high_x, low_y, high_y = hits
    along_x = jnp.where(low_x, 1.0 - frac_x, jnp.where(high_x, frac_x, 0.0))
    along_y = jnp.where(low_y, 1.0 - frac_y, jnp.where(high_y, frac_y, 0.0))
    return along_x, along_y


def slopes_of(hits):
    low_x, high_x, low_y, high_y = hits
    along_x = jnp.where(low_x, -1.0, jnp.where(high_x, 1.0, 0.0))
    along_y = jnp.where(low_y, -1.0, jnp.where(high_y, 1.0, 0.0))
    return along_x, along_y


def row3(ref, at, first=0):
    return [ref[first + k : first + k + 1, at] for k in range(3)]


def line_matrix(me):
    target = lax.broadcasted_iota(jnp.int32, (ROWS, 8 * ROWS), 0)
    column = lax.broadcasted_iota(jnp.int32, (ROWS, 8 * ROWS), 1)
    device = column // ROWS
    source = column - device * ROWS
    away = (CY * (me - device) + target - source + 128) & 63
    away = jnp.minimum(away, 64 - away)
    return STRENGTH * jnp.exp(away.astype(F32) * (-1.0 / 16.0))


def depth_matrix():
    target = lax.broadcasted_iota(jnp.int32, (NZ, NZ), 0)
    source = lax.broadcasted_iota(jnp.int32, (NZ, NZ), 1)
    away = jnp.abs(target - source)
    away = jnp.minimum(away, NZ - away)
    return jnp.exp(away.astype(F32) * (-1.0 / 16.0))


def product(a, b):
    a_high, a_low = split(a)
    b_high, b_low = split(b)
    dot = functools.partial(jnp.dot, preferred_element_type=F32)
    return dot(a_high, b_high) + (dot(a_high, b_low) + dot(a_low, b_high))


def smooth(me, gathered, planes, kept):
    lines = line_matrix(me)
    for p in range(planes):
        source = gathered[:, p * ROWS : (p + 1) * ROWS, :].reshape(8 * ROWS, NZ)
        kept[p * ROWS : (p + 1) * ROWS, :] = product(lines, source)
    kept[0 : planes * ROWS, :] = product(kept[0 : planes * ROWS, :], depth_matrix())


def deposit_first_body(pos, mom, cell, pull_pos, pull_mom, own, up, down, acc):
    acc[...] = jnp.zeros_like(acc)

    def block(b, carry):
        at = pl.ds(pl.multiple_of(b * BLK, BLK), BLK)
        frac = [p + STEP * m for p, m in zip(row3(pos, at), row3(mom, at))]
        cells = row3(cell, at)
        along_x, along_y = weights_of(axis_hits(27, CY + 1, 32, cells[0], cells[1]), frac[0], frac[1])
        planar = along_x * along_y
        below = split(planar * (1.0 - frac[2]))
        above = split(planar * frac[2])
        hot = one_hot(cells[2])
        high = jnp.concatenate([below[0], above[0]], 0)
        low = jnp.concatenate([below[1], above[1]], 0)
        acc[...] += spread_onto(high, hot) + spread_onto(low, hot)
        return carry

    lax.fori_loop(0, NQ // BLK, block, 0, unroll=2)
    density = acc[0:32, :] + prev_z(acc[32:64, :])
    own[...] = jnp.zeros_like(own)
    for x in range(3):
        own[x * ROWS + 2 : x * ROWS + 11, :] = density[x * 9 : x * 9 + 9, :]
    up[0:32, :] = own[16:48, :]
    down[0:32, :] = own[0:32, :]
    for k in range(6):
        source = pull_pos if k < 3 else pull_mom
        for c in range(16):
            line = source[k % 3 : k % 3 + 1, c * 256 : (c + 1) * 256]
            at_row = 32 + k * 16 + c
            up[at_row : at_row + 1, :] = line
            down[at_row : at_row + 1, :] = line


def fold_first_body(own, left, right, pulls, out):
    out[0:16, :] = left[0:16, :]
    out[16:32, :] = own[0:16, :] + left[16:32, :]
    out[32:48, :] = own[16:32, :]
    out[48:64, :] = own[32:48, :] + right[0:16, :]
    out[64:80, :] = right[16:32, :]
    out[80:176, :] = pulls[32:128, :]


def step_body(
    place,
    pos,
    mom,
    cell,
    dest,
    slot,
    gathered,
    left,
    right,
    own,
    up,
    down,
    drift,
    pulls,
    field_high,
    field_low,
    kept,
    pack,
    table_high,
    table_low,
    acc,
    planes,
):
    me = place[0]
    smooth(me, gathered, 5, kept)
    pack[...] = jnp.zeros_like(pack)
    for x in range(3):
        mid = (x + 1) * ROWS
        east = kept[mid + 18 : mid + 27, :]
        west = kept[mid - 14 : mid - 5, :]
        pack[x * 9 : x * 9 + 9, :] = -0.5 * (east - west)
        north = kept[mid + 3 : mid + 12, :]
        south = kept[mid + 1 : mid + 10, :]
        pack[32 + x * 9 : 32 + x * 9 + 9, :] = -0.5 * (north - south)
        pack[64 + x * 9 : 64 + x * 9 + 9, :] = -diff_z(kept[mid : mid + 16, :])[2:11, :]
    for s in range(2):
        values = pack[...] if s == 0 else next_z(pack[...])
        high, low = split(values)
        field_high[s * 96 : (s + 1) * 96, :] = high
        field_low[s * 96 : (s + 1) * 96, :] = low
    ahead = lax.rem(me + 1, 8)
    behind = lax.rem(me + 7, 8)
    for t in range(TABLES):
        for k in range(6):
            first = 80 + k * 16
            if t == 0:
                values = gathered[me, first : first + 16, :]
            elif t == 1:
                values = right[first - 48 : first - 32, :]
            elif t == 2:
                values = left[first - 48 : first - 32, :]
            elif t == 3:
                values = gathered[ahead, first : first + 16, :]
            else:
                values = gathered[behind, first : first + 16, :]
            high, low = split(values)
            row = k * 80 + t * 16
            table_high[row : row + 16, :] = high
            table_low[row : row + 16, :] = low
    acc[...] = jnp.zeros_like(acc)

    def block(b, carry):
        at = pl.ds(pl.multiple_of(b * BLK, BLK), BLK)
        momentum = row3(mom, at)
        frac = [p + STEP * m for p, m in zip(row3(pos, at), momentum)]
        cells = row3(cell, at)
        moved = dest[:, at]
        where_to = slot[:, at]
        hot = one_hot(cells[2])
        along_x, along_y = weights_of(axis_hits(27, CY + 1, 32, cells[0], cells[1]), frac[0], frac[1])
        planar = along_x * along_y
        sampled = pick_from(field_high[...], hot) + pick_from(field_low[...], hot)
        below = planar * (1.0 - frac[2])
        above = planar * frac[2]
        force = [
            jnp.sum(
                below * sampled[d * 32 : d * 32 + 32, :] + above * sampled[96 + d * 32 : 128 + d * 32, :],
                axis=0,
                keepdims=True,
            )
            for d in range(3)
        ]
        to_x = jnp.where(moved == 1, 1, jnp.where(moved == 2, -1, 0))
        to_y = jnp.where(moved == 3, 1, jnp.where(moved == 4, -1, 0))
        shift = [to_x.astype(F32), to_y.astype(F32), 0.0]
        second = [frac[d] - shift[d] + STEP * (momentum[d] + STEP * force[d]) for d in range(3)]
        for d in range(3):
            drift[d : d + 1, at] = second[d]
        hot_slot = one_hot(where_to & 255)
        taken = pick_from(table_high[...], hot_slot) + pick_from(table_low[...], hot_slot)
        chosen = moved * 16 + lax.shift_right_logical(where_to, 8)
        here = lax.broadcasted_iota(jnp.int32, (80, BLK), 0) == chosen
        home = [
            jnp.sum(jnp.where(here, taken[k * 80 : k * 80 + 80, :], 0.0), axis=0, keepdims=True)
            for k in range(6)
        ]
        for k in range(6):
            pulls[k : k + 1, at] = home[k]
        along_x, along_y = weights_of(
            axis_hits(55, CY + 3, 64, cells[0] + to_x + 1, cells[1] + to_y + 1), second[0], second[1]
        )
        planar = along_x * along_y
        below = planar * (1.0 - second[2])
        above = planar * second[2]
        for c in range(4):
            scale = 1.0 if c == 0 else STEP * home[2 + c]
            high_b, low_b = split(below if c == 0 else below * scale)
            high_a, low_a = split(above if c == 0 else above * scale)
            high = jnp.concatenate([high_b, high_a], 0)
            low = jnp.concatenate([low_b, low_a], 0)
            acc[c * 128 : c * 128 + 128, :] += spread_onto(high, hot) + spread_onto(low, hot)
        return carry

    lax.fori_loop(0, NQ // BLK, block, 0)
    planes[...] = jnp.zeros_like(planes)
    for c in range(4):
        total = acc[c * 128 : c * 128 + 64, :] + prev_z(acc[c * 128 + 64 : c * 128 + 128, :])
        for x in range(5):
            planes[c, x, 1:12, :] = total[x * 11 : x * 11 + 11, :]
    for x in range(5):
        planes[2, x] = diff_row(planes[2, x]) + diff_z(planes[3, x])
    for c in range(3):
        for x in range(3):
            own[(c * 3 + x) * 16 : (c * 3 + x) * 16 + 16, :] = planes[c, x + 1]
        for x in range(2):
            up[(c * 2 + x) * 16 : (c * 2 + x) * 16 + 16, :] = planes[c, x + 3]
            down[(c * 2 + x) * 16 : (c * 2 + x) * 16 + 16, :] = planes[c, x]


def fold_body(channels, own, left, right, out):
    for c in range(channels):
        mine, theirs = c * 48, c * 32
        out[mine : mine + 16, :] = own[mine : mine + 16, :] + left[theirs : theirs + 16, :]
        out[mine + 16 : mine + 32, :] = (
            own[mine + 16 : mine + 32, :]
            + left[theirs + 16 : theirs + 32, :]
            + right[theirs : theirs + 16, :]
        )
        out[mine + 32 : mine + 48, :] = own[mine + 32 : mine + 48, :] + right[theirs + 16 : theirs + 32, :]


def lines_body(place, gathered, own, up, down):
    smooth(place[0], gathered, 9, own)
    for c in range(2):
        up[c * 32 : c * 32 + 32, :] = own[c * 48 : c * 48 + 32, :]
        down[c * 32 : c * 32 + 32, :] = own[c * 48 + 16 : c * 48 + 48, :]
    up[64:80, :] = own[112:128, :]
    down[64:80, :] = own[112:128, :]


def back_body(
    pos,
    mom,
    cell,
    dest,
    drift,
    pulls,
    mine,
    left,
    right,
    own,
    up,
    down,
    grads,
    wide,
    pack,
    field_high,
    field_low,
    acc,
    planes,
):
    for c in range(2):
        wide[c, 0:32, :] = left[c * 32 : c * 32 + 32, :]
        wide[c, 32:80, :] = mine[c * 48 : c * 48 + 48, :]
        wide[c, 80:112, :] = right[c * 32 : c * 32 + 32, :]
    wide[2, 16:32, :] = left[64:80, :]
    wide[2, 32:80, :] = mine[96:144, :]
    wide[2, 80:96, :] = right[64:80, :]
    pack[...] = jnp.zeros_like(pack)
    for x in range(5):
        mid = (x + 1) * 16
        first = x * 11
        pack[first : first + 11, :] = -0.5 * (wide[0, mid + 17 : mid + 28, :] - wide[0, mid - 15 : mid - 4, :])
        pack[64 + first : 75 + first, :] = -0.5 * (
            wide[0, mid + 2 : mid + 13, :] - wide[0, mid : mid + 11, :]
        )
        pack[128 + first : 139 + first, :] = -diff_z(wide[0, mid : mid + 16, :])[1:12, :]
        pack[192 + first : 203 + first, :] = (
            0.5 * (wide[1, mid + 17 : mid + 28, :] - wide[1, mid - 15 : mid - 4, :])
            + wide[2, mid + 1 : mid + 12, :]
        )
    for s in range(2):
        values = pack[...] if s == 0 else next_z(pack[...])
        high, low = split(values)
        field_high[s * 256 : (s + 1) * 256, :] = high
        field_low[s * 256 : (s + 1) * 256, :] = low
    acc[...] = jnp.zeros_like(acc)

    def block(b, carry):
        at = pl.ds(pl.multiple_of(b * BLK, BLK), BLK)
        cells = row3(cell, at)
        moved = dest[:, at]
        hot = one_hot(cells[2])
        second = row3(drift, at)
        pull_position = row3(pulls, at)
        pull_momentum = row3(pulls, at, 3)
        to_x = jnp.where(moved == 1, 1, jnp.where(moved == 2, -1, 0))
        to_y = jnp.where(moved == 3, 1, jnp.where(moved == 4, -1, 0))
        hits = axis_hits(55, CY + 3, 64, cells[0] + to_x + 1, cells[1] + to_y + 1)
        along_x, along_y = weights_of(hits, second[0], second[1])
        slope_x, slope_y = slopes_of(hits)
        sampled = pick_from(field_high[...], hot) + pick_from(field_low[...], hot)
        sides = []
        for s in range(2):
            mixed = sampled[s * 256 + 192 : s * 256 + 256, :]
            for d in range(3):
                mixed = mixed + (STEP * pull_momentum[d]) * sampled[s * 256 + d * 64 : s * 256 + d * 64 + 64, :]
            sides.append(mixed)
        level = sides[0] + second[2] * (sides[1] - sides[0])
        rise = sides[1] - sides[0]
        slopes = [
            jnp.sum(slope_x * (along_y * level), axis=0, keepdims=True),
            jnp.sum(slope_y * (along_x * level), axis=0, keepdims=True),
            jnp.sum(along_x * (along_y * rise), axis=0, keepdims=True),
        ]
        grad_drift = [pull_position[d] + slopes[d] for d in range(3)]
        grad_kick = [pull_momentum[d] + STEP * grad_drift[d] for d in range(3)]
        for d in range(3):
            grads[d : d + 1, at] = grad_drift[d]
            grads[d + 3 : d + 4, at] = grad_kick[d]
        frac = [p + STEP * m for p, m in zip(row3(pos, at), row3(mom, at))]
        along_x, along_y = weights_of(axis_hits(27, CY + 1, 32, cells[0], cells[1]), frac[0], frac[1])
        planar = along_x * along_y
        below = planar * (1.0 - frac[2])
        above = planar * frac[2]
        for c in range(3):
            scale = STEP * grad_kick[c]
            high_b, low_b = split(below * scale)
            high_a, low_a = split(above * scale)
            high = jnp.concatenate([high_b, high_a], 0)
            low = jnp.concatenate([low_b, low_a], 0)
            acc[c * 64 : c * 64 + 64, :] += spread_onto(high, hot) + spread_onto(low, hot)
        return carry

    lax.fori_loop(0, NQ // BLK, block, 0)
    planes[...] = jnp.zeros_like(planes)
    for c in range(3):
        total = acc[c * 64 : c * 64 + 32, :] + prev_z(acc[c * 64 + 32 : c * 64 + 64, :])
        for x in range(3):
            planes[c, x + 2, 2:11, :] = total[x * 9 : x * 9 + 9, :]
    for x in range(5):
        spread = 0.5 * (planes[0, x + 2] - planes[0, x])
        if 1 <= x <= 3:
            spread = spread + diff_row(planes[1, x + 1]) + diff_z(planes[2, x + 1])
        if 1 <= x <= 3:
            own[(x - 1) * 16 : x * 16, :] = spread
        if x >= 3:
            up[(x - 3) * 16 : (x - 2) * 16, :] = spread
        if x <= 1:
            down[x * 16 : (x + 1) * 16, :] = spread


def last_body(
    place, pos, mom, cell, grads, field_high, field_low, gathered, grad_pos, grad_mom, kept, pack, high, low
):
    smooth(place[0], gathered, 3, kept)
    pack[...] = jnp.zeros_like(pack)
    for x in range(3):
        pack[x * 9 : x * 9 + 9, :] = kept[x * 16 + 2 : x * 16 + 11, :]
    high[0:192, :] = field_high[...]
    low[0:192, :] = field_low[...]
    high[192:224, :], low[192:224, :] = split(pack[...])
    high[224:256, :], low[224:256, :] = split(next_z(pack[...]))

    def block(b, carry):
        at = pl.ds(pl.multiple_of(b * BLK, BLK), BLK)
        frac = [p + STEP * m for p, m in zip(row3(pos, at), row3(mom, at))]
        cells = row3(cell, at)
        hot = one_hot(cells[2])
        hits = axis_hits(27, CY + 1, 32, cells[0], cells[1])
        along_x, along_y = weights_of(hits, frac[0], frac[1])
        slope_x, slope_y = slopes_of(hits)
        grad_drift = row3(grads, at)
        grad_kick = row3(grads, at, 3)
        sampled = pick_from(high[...], hot) + pick_from(low[...], hot)
        sides = []
        for s in range(2):
            mixed = sampled[192 + s * 32 : 224 + s * 32, :]
            for d in range(3):
                mixed = mixed + (STEP * grad_kick[d]) * sampled[s * 96 + d * 32 : s * 96 + d * 32 + 32, :]
            sides.append(mixed)
        level = sides[0] + frac[2] * (sides[1] - sides[0])
        rise = sides[1] - sides[0]
        slopes = [
            jnp.sum(slope_x * (along_y * level), axis=0, keepdims=True),
            jnp.sum(slope_y * (along_x * level), axis=0, keepdims=True),
            jnp.sum(along_x * (along_y * rise), axis=0, keepdims=True),
        ]
        for d in range(3):
            total = grad_drift[d] + slopes[d]
            grad_pos[d : d + 1, at] = total
            grad_mom[d : d + 1, at] = grad_kick[d] + STEP * total
        return carry

    lax.fori_loop(0, NQ // BLK, block, 0, unroll=2)


def swap_x(up, down):
    peers = lax.axis_size("gx")
    forward = [(i, (i + 1) % peers) for i in range(peers)]
    backward = [((i + 1) % peers, i) for i in range(peers)]
    return lax.ppermute(up, "gx", forward), lax.ppermute(down, "gx", backward)


def gather_y(x):
    return lax.all_gather(x, "gy", axis=0, tiled=False)


def local(pos, mom, cell, cell_second, dest, slot, pull_pos, pull_mom):
    place = lax.axis_index("gy").astype(jnp.int32).reshape(1)
    dest = dest.reshape(1, NQ)
    slot = slot.reshape(1, NQ)
    scalar = pl.BlockSpec(memory_space=pltpu.SMEM)
    vmem = pl.BlockSpec(memory_space=pltpu.VMEM)

    def call_at(body, outs, scratch, operands):
        return pl.pallas_call(
            body,
            out_shape=outs,
            in_specs=[scalar] + [vmem] * operands,
            scratch_shapes=list(scratch),
            compiler_params=pltpu.CompilerParams(vmem_limit_bytes=VMEM_LIMIT),
        )

    own, up, down = call(
        deposit_first_body, (shape(48, NZ), shape(128, NZ), shape(128, NZ)), [pltpu.VMEM((64, NZ), F32)]
    )(pos, mom, cell, pull_pos, pull_mom)
    left, right = swap_x(up, down)
    gathered = gather_y(call(fold_first_body, shape(176, NZ))(own, left, right, up))
    own, up, down, drift, pulls, field_high, field_low = call_at(
        step_body,
        (
            shape(144, NZ),
            shape(96, NZ),
            shape(96, NZ),
            shape(3, NQ),
            shape(6, NQ),
            shape(192, NZ, dtype=BF16),
            shape(192, NZ, dtype=BF16),
        ),
        [
            pltpu.VMEM((80, NZ), F32),
            pltpu.VMEM((96, NZ), F32),
            pltpu.VMEM((480, NZ), BF16),
            pltpu.VMEM((480, NZ), BF16),
            pltpu.VMEM((512, NZ), F32),
            pltpu.VMEM((4, 5, ROWS, NZ), F32),
        ],
        8,
    )(place, pos, mom, cell, dest, slot, gathered, left, right)
    left, right = swap_x(up, down)
    gathered = gather_y(call(functools.partial(fold_body, 3), shape(144, NZ))(own, left, right))
    mine, up, down = call_at(lines_body, (shape(144, NZ), shape(80, NZ), shape(80, NZ)), [], 1)(
        place, gathered
    )
    left, right = swap_x(up, down)
    own, up, down, grads = call(
        back_body,
        (shape(48, NZ), shape(32, NZ), shape(32, NZ), shape(6, NQ)),
        [
            pltpu.VMEM((3, 112, NZ), F32),
            pltpu.VMEM((256, NZ), F32),
            pltpu.VMEM((512, NZ), BF16),
            pltpu.VMEM((512, NZ), BF16),
            pltpu.VMEM((192, NZ), F32),
            pltpu.VMEM((3, 7, ROWS, NZ), F32),
        ],
    )(pos, mom, cell, dest, drift, pulls, mine, left, right)
    left, right = swap_x(up, down)
    gathered = gather_y(call(functools.partial(fold_body, 1), shape(48, NZ))(own, left, right))
    return call_at(
        last_body,
        (shape(3, NQ), shape(3, NQ)),
        [
            pltpu.VMEM((48, NZ), F32),
            pltpu.VMEM((32, NZ), F32),
            pltpu.VMEM((256, NZ), BF16),
            pltpu.VMEM((256, NZ), BF16),
        ],
        7,
    )(place, pos, mom, cell, grads, field_high, field_low, gathered)


def solution(mesh):
    both = ("gx", "gy")
    return jax.shard_map(
        local,
        mesh=mesh,
        in_specs=(P(None, both), P(None, both), P(None, both), P(None, both), P(both), P(both), P(None, both), P(None, both)),
        out_specs=(P(None, both), P(None, both)),
        check_vma=False,
    )
```

time: 334 us -> 195 us (0.58); the launches traced: 329 us -> 195 us
  other arithmetic: 71.2 us -> 0 us
  waiting for transfers between devices: 8.22 us -> 76.4 us
  local copies, waits for them, and re-layouts: 70.9 us -> 10.8 us
  blocking collectives: 68.8 us -> 17.1 us
  matrix products: 39.7 us -> 0 us
  Pallas kernels: 0 us -> 35.2 us
  starting transfers between devices: 64.9 us -> 40.8 us
  between operations: 1.93 us -> 14.2 us
  loops' own time: 3.7 us -> 0 us
    all_gather x0 -> x2, waiting for transfers between devices: none -> 64.3 us  [gather_y(): return lax.all_gather(x, 'gy', axis=0, tiled=False)]
    add x174 -> x0, other arithmetic: 51.8 us -> none  [the longest x56 46.3 us: cloud_weights(): corner = (cell_block[1] * plane_count + cell_block[0])[None, :]]
    all_gather x4 -> x1, blocking collectives: 68.8 us -> 17.1 us  [gather_y(): return lax.all_gather(x, 'gy', axis=0, tiled=False)]
    dot_general x64 -> x0, matrix products: 39.7 us -> none  [the longest x32 20.9 us: add_block(): jnp.einsum('crb,zb->crz', spread, weights[3], precision=highest)]
    pallas_call x0 -> x8, Pallas kernels: none -> 35.2 us  [the longest x1 13.7 us: local(): call_at(step_body, (shape(144, NZ), shape(96, NZ), shape(96, NZ), shape(3...]
    gather x11 -> x0, local copies, waits for them, and re-layouts: 33.1 us -> none  [the longest x1 14.1 us: local(): returning[:, slot_index]]
    ppermute x16 -> x8, starting transfers between devices: 64.9 us -> 40.7 us  [swap_x(): return (lax.ppermute(up, 'gx', forward), lax.ppermute(down, 'gx', backward))]
    scatter x2 -> x0, local copies, waits for them, and re-layouts: 18.2 us -> none  [the longest x1 14.1 us: local(): arrived = jnp.zeros((6, particle_count), jnp.float32).at[:, placed].set(j...]
  transfers between devices with their start and end apart: 16 -> 10, of which waited for: 3 -> 9; matrix products, arithmetic and copies ran while one was open for 13% -> 0% of each run, Pallas kernels for 0% -> 0%
where the time goes in v2:
time: 195 us
  waiting for transfers between devices  76.4 us (39%)
  starting transfers between devices  40.8 us (21%)
  Pallas kernels  35.2 us (18%)
  blocking collectives  17.1 us (9%)
  between operations  14.2 us (7%)
  local copies, waits for them, and re-layouts  10.8 us (6%)
    all_gather x2, waiting for transfers between devices, gather_y(): return lax.all_gather(x, 'gy', axis=0, tiled=False)  64.3 us
    ppermute x8, starting transfers between devices, swap_x(): return (lax.ppermute(up, 'gx', forward), lax.ppermute(down, 'gx', backward))  40.7 us
    all_gather x1, blocking collectives, gather_y(): return lax.all_gather(x, 'gy', axis=0, tiled=False)  17.1 us
    pallas_call x1, Pallas kernels, local(): call_at(step_body, (shape(144, NZ), shape(96, NZ), shape(96, NZ), shape(3...  13.7 us
    pallas_call x1, Pallas kernels, local(): call(back_body, (shape(48, NZ), shape(32, NZ), shape(32, NZ), shape(6, NQ...  12.6 us
    ppermute x8, waiting for transfers between devices, swap_x(): return (lax.ppermute(up, 'gx', forward), lax.ppermute(down, 'gx', backward))  12.1 us
    unnamed x32, local copies, waits for them, and re-layouts  10.8 us
    pallas_call x1, Pallas kernels, local(): call_at(last_body, (shape(3, NQ), shape(3, NQ)), [pltpu.VMEM((48, NZ), F3...  4.24 us
  transfers between devices with their start and end apart: 10, of which 9 were waited for; matrix products, arithmetic and copies ran while one was open for 0% of the time, Pallas kernels for 0%

profile of v2, /device:TPU:1, one launch (start us, length us, event | category | flops | bytes accessed | tf_op | source)
XLA Modules:
  0.0 194.6 jit_solution(17412688119046376135)
XLA Ops:
  7.2 0.0 all-gather.6.cloned.1.call-start
  7.2 0.0 copy-start.2
  7.2 0.8 copy-done.2
  8.1 0.0 copy-start.5
  8.1 0.8 copy-done.5
  8.9 0.0 copy-start.8
  8.9 0.8 copy-done.8
  9.7 0.0 copy-start.13
  9.7 0.8 copy-done.13
  10.6 0.0 copy-start.14
  10.6 0.8 copy-done.14
  11.4 2.8 %shard_map.86 = (f32[48,256]{1,0:T(8,128)S(1)}, f32[128,256]{1,0:T(8,128)S(1)}, f32[128,256]{1,0:T(8,128)S(1)}) custom-call(f32[3,4096]{1,0:T(4,128)S(1)} %copy-done.2, f32[3,4096]{1,0:T(4,128)S(1)} %copy-done.5, s32[3,4096]{1,0:T(4,128)S(1)} %copy-done.8, f32[3,4096]{1,0:T(4,128)S(1)} %copy-done.13, f32[3,4096]{1,0:T(4,128)S(1)} %copy-done.14), custom_call_target="tpu_custom_call" | custom-call | tf_op jit(solution)/shard_map/pallas_call | solution.py:509
  14.2 9.9 %collective-permute-start.1 = (f32[128,256]{1,0:T(8,128)S(1)}, f32[128,256]{1,0:T(8,128)S(1)}, u32[]{:S(2)}, u32[]{:S(2)}) collective-permute-start(f32[128,256]{1,0:T(8,128)S(1)} %get-tuple-element.21), channel_id=1, source_target_pairs={{8,0},{16,8},{24,16},{32,24},{40,32},{48,40},{56,48},{64,56},{72,6... | collective-permute-start | bytes 393224 | tf_op jit(solution)/shard_map/ppermute | solution.py:486
  24.1 1.9 collective-permute-start
  26.0 0.2 collective-permute-done.1.right
  26.2 7.8 %collective-permute-done.left = f32[128,256]{1,0:T(8,128)S(1)} collective-permute-done((f32[128,256]{1,0:T(8,128)S(1)}, f32[128,256]{1,0:T(8,128)S(1)}, u32[]{:S(2)}, u32[]{:S(2)}) %collective-permute-start) | collective-permute-done | bytes 131104 | tf_op jit(solution)/shard_map/ppermute | solution.py:486
  34.0 0.7 shard_map.87
  34.7 0.0 all-gather.6.cloned.1.call-update
  34.7 0.0 all-gather.8.cloned.1.call-start
  34.8 32.8 %all-gather.6.cloned.1.call-done = f32[1408,256]{1,0:T(8,128)} async-done(((f32[176,256]{1,0:T(8,128)}), f32[1408,256]{1,0:T(8,128)}) %all-gather.6.cloned.1.call-update) | async-done | bytes 1441808 | tf_op jit(solution)/shard_map/all_gather | solution.py:490
  67.6 0.0 copy-start
  67.6 1.4 copy-done
  69.0 0.0 copy-start.3
  69.0 0.8 copy-done.3
  69.8 0.0 copy-start.6
  69.8 0.8 copy-done.6
  70.7 0.0 copy-start.9
  70.7 0.8 copy-done.9
  71.5 0.0 copy-start.11
  71.5 0.7 copy-done.11
  72.2 0.0 copy-start.15
  72.2 0.7 copy-done.15
  72.9 0.0 copy-start.4
  72.9 0.0 copy-start.7
  72.9 0.0 copy-start.10
  72.9 0.0 copy-start.12
  73.0 13.7 %shard_map.88 = (f32[144,256]{1,0:T(8,128)S(1)}, f32[96,256]{1,0:T(8,128)S(1)}, f32[96,256]{1,0:T(8,128)S(1)}, f32[3,4096]{1,0:T(4,128)S(1)}, f32[6,4096]{1,0:T(...) custom-call(s32[1]{0:T(128)} %bitcast.place, f32[3,4096]{1,0:T(4,128)S(1)} %copy-done.3, ...), custom_call_target="tpu_custom_call" | custom-call | tf_op jit(solution)/shard_map/pallas_call | solution.py:514
  86.6 4.2 %collective-permute-start.2 = (f32[96,256]{1,0:T(8,128)S(1)}, f32[96,256]{1,0:T(8,128)S(1)}, u32[]{:S(2)}, u32[]{:S(2)}) collective-permute-start(f32[96,256]{1,0:T(8,128)S(1)} %get-tuple-element.25), channel_id=1, source_target_pairs={{0,8},{8,16},{16,24},{24,32},{32,40},{40,48},{48,56},{56,64},{64,7... | collective-permute-start | bytes 294920 | tf_op jit(solution)/shard_map/ppermute | solution.py:486
  90.9 5.3 %collective-permute-start.3 = (f32[96,256]{1,0:T(8,128)S(1)}, f32[96,256]{1,0:T(8,128)S(1)}, u32[]{:S(2)}, u32[]{:S(2)}) collective-permute-start(f32[96,256]{1,0:T(8,128)S(1)} %get-tuple-element.26), channel_id=1, source_target_pairs={{8,0},{16,8},{24,16},{32,24},{40,32},{48,40},{56,48},{64,56},{72,6... | collective-permute-start | bytes 294920 | tf_op jit(solution)/shard_map/ppermute | solution.py:486
  96.2 0.7 collective-permute-done.2.left
  96.9 0.9 collective-permute-done.3.right
  97.8 0.7 shard_map.89
  98.5 0.0 all-gather.8.cloned.1.call-update
  98.5 31.5 %all-gather.8.cloned.1.call-done = f32[1152,256]{1,0:T(8,128)} async-done(((f32[144,256]{1,0:T(8,128)}), f32[1152,256]{1,0:T(8,128)}) %all-gather.8.cloned.1.call-update) | async-done | bytes 1179664 | tf_op jit(solution)/shard_map/all_gather | solution.py:490
  130.0 0.0 copy-start.1
  130.0 1.3 copy-done.1
  131.3 0.6 shard_map.90
  131.9 3.7 %collective-permute-start.4 = (f32[80,256]{1,0:T(8,128)S(1)}, f32[80,256]{1,0:T(8,128)S(1)}, u32[]{:S(2)}, u32[]{:S(2)}) collective-permute-start(f32[80,256]{1,0:T(8,128)S(1)} %get-tuple-element.28), channel_id=1, source_target_pairs={{0,8},{8,16},{16,24},{24,32},{32,40},{40,48},{48,56},{56,64},{64,7... | collective-permute-start | bytes 245768 | tf_op jit(solution)/shard_map/ppermute | solution.py:486
  135.6 5.8 %collective-permute-start.5 = (f32[80,256]{1,0:T(8,128)S(1)}, f32[80,256]{1,0:T(8,128)S(1)}, u32[]{:S(2)}, u32[]{:S(2)}) collective-permute-start(f32[80,256]{1,0:T(8,128)S(1)} %get-tuple-element.29), channel_id=1, source_target_pairs={{8,0},{16,8},{24,16},{32,24},{40,32},{48,40},{56,48},{64,56},{72,6... | collective-permute-start | bytes 245768 | tf_op jit(solution)/shard_map/ppermute | solution.py:486
  141.4 0.4 collective-permute-done.4.left
  141.8 1.1 collective-permute-done.5.right
  142.9 0.0 copy-done.4
  142.9 0.0 copy-done.7
  142.9 0.0 copy-done.10
  142.9 0.0 copy-done.12
  142.9 12.6 %shard_map.91 = (f32[48,256]{1,0:T(8,128)S(1)}, f32[32,256]{1,0:T(8,128)S(1)}, f32[32,256]{1,0:T(8,128)S(1)}, f32[6,4096]{1,0:T(8,128)S(1)}) custom-call(f32[3,4096]{1,0:T(4,128)S(1)} %copy-done.4, f32[3,4096]{1,0:T(4,128)S(1)} %copy-done.7, s32[3,4096]{1,0:T(4,128)S(1)} %copy-done.10, s32[1,4096]{1,0:T(1,128)S(1)} %bitcast.10, ...), custom_call_target="tpu_custom_call" | custom-call | tf_op jit(solution)/shard_map/pallas_call | solution.py:541
  155.4 1.9 collective-permute-start.6
  157.4 7.9 %collective-permute-start.7 = (f32[32,256]{1,0:T(8,128)S(1)}, f32[32,256]{1,0:T(8,128)S(1)}, u32[]{:S(2)}, u32[]{:S(2)}) collective-permute-start(f32[32,256]{1,0:T(8,128)S(1)} %get-tuple-element.35), channel_id=1, source_target_pairs={{8,0},{16,8},{24,16},{32,24},{40,32},{48,40},{56,48},{64,56},{72,6... | collective-permute-start | bytes 98312 | tf_op jit(solution)/shard_map/ppermute | solution.py:486
  165.3 0.0 collective-permute-done.6.left
  165.3 1.0 collective-permute-done.7.right
  166.3 17.1 %all-gather.2 = f32[384,256]{1,0:T(8,128)S(1)} all-gather(f32[48,256]{1,0:T(8,128)S(1)} %shard_map.92), channel_id=4, replica_groups=mesh['gx'=64,'gy'=8] {'gy'}, dimensions={0}, use_global_device_ids=true | all-gather | bytes 442368 | tf_op jit(solution)/shard_map/all_gather | solution.py:490
  183.5 4.2 %shard_map.93 = (f32[3,4096]{1,0:T(4,128)}, f32[3,4096]{1,0:T(4,128)}) custom-call(s32[1]{0:T(128)} %bitcast.place, f32[3,4096]{1,0:T(4,128)S(1)} %copy-done.4, f32[3,4096]{1,0:T(4,128)S(1)} %copy-done.7, s32[3,4096]{1,0:T(4,128)S(1)} %copy-done.10, f32[6,4096]{1,0:T(8,128)S(1)} %get-tuple-element.30.grads, ...), custom_call_target="tpu_custom_call" | custom-call | tf_op jit(solution)/shard_map/pallas_call | solution.py:555
  (1 shorter events, 0.0 us)
Async XLA Ops:
  7.2 60.5 %all-gather.6.cloned.1.call-start = ((), (), s32[]{:S(2)}) async-start(), calls=%async_computation | async-start | bytes 1622016 | tf_op jit(solution)/shard_map/all_gather | solution.py:490
  7.2 0.8 copy-start.2
  8.1 0.8 copy-start.5
  8.9 0.8 copy-start.8
  9.7 0.8 copy-start.13
  10.6 0.8 copy-start.14
  14.2 12.1 %collective-permute-start.1 = (f32[128,256]{1,0:T(8,128)S(1)}, f32[128,256]{1,0:T(8,128)S(1)}, u32[]{:S(2)}, u32[]{:S(2)}) collective-permute-start(f32[128,256]{1,0:T(8,128)S(1)} %get-tuple-element.21), channel_id=1, source_target_pairs={{8,0},{16,8},{24,16},{32,24},{40,32},{48,40},{56,48},{64,56},{72,6... | collective-permute-start | bytes 393224 | tf_op jit(solution)/shard_map/ppermute | solution.py:486
  24.1 9.9 %collective-permute-start = (f32[128,256]{1,0:T(8,128)S(1)}, f32[128,256]{1,0:T(8,128)S(1)}, u32[]{:S(2)}, u32[]{:S(2)}) collective-permute-start(f32[128,256]{1,0:T(8,128)S(1)} %get-tuple-element.20.pulls), channel_id=1, source_target_pairs={{0,8},{8,16},{16,24},{24,32},{32,40},{40,48},{48,56},{56,64},{64,7... | collective-permute-start | bytes 393224 | tf_op jit(solution)/shard_map/ppermute | solution.py:486
  34.7 95.3 %all-gather.8.cloned.1.call-start = ((), (), s32[]{:S(2)}) async-start(), calls=%async_computation.1 | async-start | bytes 1327104 | tf_op jit(solution)/shard_map/all_gather | solution.py:490
  67.6 1.4 copy-start
  69.0 0.8 copy-start.3
  69.8 0.8 copy-start.6
  70.7 0.8 copy-start.9
  71.5 0.7 copy-start.11
  72.2 0.7 copy-start.15
  72.9 69.9 %copy-start.4 = (f32[3,4096]{1,0:T(4,128)S(1)}, f32[3,4096]{1,0:T(4,128)}, u32[]{:S(2)}) copy-start(f32[3,4096]{1,0:T(4,128)} %pos.7) | copy-start | bytes 147460
  72.9 69.9 %copy-start.7 = (f32[3,4096]{1,0:T(4,128)S(1)}, f32[3,4096]{1,0:T(4,128)}, u32[]{:S(2)}) copy-start(f32[3,4096]{1,0:T(4,128)} %mom.7) | copy-start | bytes 147460
  72.9 69.9 %copy-start.10 = (s32[3,4096]{1,0:T(4,128)S(1)}, s32[3,4096]{1,0:T(4,128)}, u32[]{:S(2)}) copy-start(s32[3,4096]{1,0:T(4,128)} %cell.7) | copy-start | bytes 147460
  72.9 69.9 %copy-start.12 = (s32[4096]{0:T(1024)S(1)}, s32[4096]{0:T(1024)}, u32[]{:S(2)}) copy-start(s32[4096]{0:T(1024)} %param.11) | copy-start | bytes 49156
  86.6 10.3 %collective-permute-start.2 = (f32[96,256]{1,0:T(8,128)S(1)}, f32[96,256]{1,0:T(8,128)S(1)}, u32[]{:S(2)}, u32[]{:S(2)}) collective-permute-start(f32[96,256]{1,0:T(8,128)S(1)} %get-tuple-element.25), channel_id=1, source_target_pairs={{0,8},{8,16},{16,24},{24,32},{32,40},{40,48},{48,56},{56,64},{64,7... | collective-permute-start | bytes 294920 | tf_op jit(solution)/shard_map/ppermute | solution.py:486
  90.9 6.9 %collective-permute-start.3 = (f32[96,256]{1,0:T(8,128)S(1)}, f32[96,256]{1,0:T(8,128)S(1)}, u32[]{:S(2)}, u32[]{:S(2)}) collective-permute-start(f32[96,256]{1,0:T(8,128)S(1)} %get-tuple-element.26), channel_id=1, source_target_pairs={{8,0},{16,8},{24,16},{32,24},{40,32},{48,40},{56,48},{64,56},{72,6... | collective-permute-start | bytes 294920 | tf_op jit(solution)/shard_map/ppermute | solution.py:486
  130.0 1.3 copy-start.1
  131.9 9.9 %collective-permute-start.4 = (f32[80,256]{1,0:T(8,128)S(1)}, f32[80,256]{1,0:T(8,128)S(1)}, u32[]{:S(2)}, u32[]{:S(2)}) collective-permute-start(f32[80,256]{1,0:T(8,128)S(1)} %get-tuple-element.28), channel_id=1, source_target_pairs={{0,8},{8,16},{16,24},{24,32},{32,40},{40,48},{48,56},{56,64},{64,7... | collective-permute-start | bytes 245768 | tf_op jit(solution)/shard_map/ppermute | solution.py:486
  135.6 7.3 %collective-permute-start.5 = (f32[80,256]{1,0:T(8,128)S(1)}, f32[80,256]{1,0:T(8,128)S(1)}, u32[]{:S(2)}, u32[]{:S(2)}) collective-permute-start(f32[80,256]{1,0:T(8,128)S(1)} %get-tuple-element.29), channel_id=1, source_target_pairs={{8,0},{16,8},{24,16},{32,24},{40,32},{48,40},{56,48},{64,56},{72,6... | collective-permute-start | bytes 245768 | tf_op jit(solution)/shard_map/ppermute | solution.py:486
  155.4 9.9 %collective-permute-start.6 = (f32[32,256]{1,0:T(8,128)S(1)}, f32[32,256]{1,0:T(8,128)S(1)}, u32[]{:S(2)}, u32[]{:S(2)}) collective-permute-start(f32[32,256]{1,0:T(8,128)S(1)} %get-tuple-element.34), channel_id=1, source_target_pairs={{0,8},{8,16},{16,24},{24,32},{32,40},{40,48},{48,56},{56,64},{64,7... | collective-permute-start | bytes 98312 | tf_op jit(solution)/shard_map/ppermute | solution.py:486
  157.4 8.9 %collective-permute-start.7 = (f32[32,256]{1,0:T(8,128)S(1)}, f32[32,256]{1,0:T(8,128)S(1)}, u32[]{:S(2)}, u32[]{:S(2)}) collective-permute-start(f32[32,256]{1,0:T(8,128)S(1)} %get-tuple-element.35), channel_id=1, source_target_pairs={{8,0},{16,8},{24,16},{32,24},{40,32},{48,40},{56,48},{64,56},{72,6... | collective-permute-start | bytes 98312 | tf_op jit(solution)/shard_map/ppermute | solution.py:486
Sparse Core Ops, SparseCore 0:
  34.9 32.7 all-gather.5
  98.6 31.3 all-gather.7

commit v3 on v2

v3 whole, which is shorter than its diff:
```python
import functools

import jax
import jax.numpy as jnp
from jax import lax
from jax.experimental import pallas as pl
from jax.experimental.pallas import tpu as pltpu
from jax.sharding import PartitionSpec as P

CX = 2
CY = 8
NZ = 256
NQ = 4096
BLK = 4096
ROWS = 16
TABLES = 5
STEP = 0.25
STRENGTH = 0.02
F32 = jnp.float32
BF16 = jnp.bfloat16
highest = lax.Precision.HIGHEST
VMEM_LIMIT = 24 * 1024 * 1024


def shape(*dims, dtype=F32):
    return jax.ShapeDtypeStruct(dims, dtype)


def call(body, outs, scratch=()):
    return pl.pallas_call(
        body,
        out_shape=outs,
        scratch_shapes=list(scratch),
        compiler_params=pltpu.CompilerParams(vmem_limit_bytes=VMEM_LIMIT),
    )


def split(x):
    high = x.astype(BF16)
    return high, (x - high.astype(F32)).astype(BF16)


def one_hot(index):
    rows = lax.broadcasted_iota(jnp.int32, (256, index.shape[1]), 0)
    return jnp.where(rows == index, 1.0, 0.0).astype(BF16)


def one_hot_columns(index):
    width = index.shape[1]
    down = jnp.transpose(jnp.broadcast_to(index, (8, width)))[:, 0:1]
    columns = lax.broadcasted_iota(jnp.int32, (width, 256), 1)
    return jnp.where(columns == down, 1.0, 0.0).astype(BF16)


MODE_S = "rows"
MODE_D = "nt"


def put_split(ref, first, values):
    rows = values.shape[0]
    high, low = split(values)
    half = ref.shape[0] // 2
    ref[first : first + rows, :] = high
    ref[half + first : half + first + rows, :] = low


def halves(x):
    half = x.shape[0] // 2
    return x[:half] + x[half:]


def pick_from(table, hot):
    return halves(jnp.dot(table[...], hot, preferred_element_type=F32))


def spread_onto(values, index):
    if MODE_D == "nt":
        return halves(
            lax.dot_general(
                values[...], one_hot(index), (((1,), (1,)), ((), ())), preferred_element_type=F32
            )
        )
    return halves(jnp.dot(values[...], one_hot_columns(index), preferred_element_type=F32))


def next_z(x):
    return pltpu.roll(x, NZ - 1, 1)


def prev_z(x):
    return pltpu.roll(x, 1, 1)


def diff_z(x):
    return 0.5 * (next_z(x) - prev_z(x))


def diff_row(x):
    return 0.5 * (pltpu.roll(x, ROWS - 1, 0) - pltpu.roll(x, 1, 0))


def axis_hits(rows, pitch, padded, cell_x, cell_y):
    index = lax.broadcasted_iota(jnp.int32, (padded, cell_x.shape[1]), 0)
    row_x = index // pitch
    row_y = index - row_x * pitch
    away_x = row_x - cell_x
    away_y = row_y - cell_y
    return away_x == 0, away_x == 1, away_y == 0, away_y == 1


def weights_of(hits, frac_x, frac_y):
    low_x, high_x, low_y, high_y = hits
    along_x = jnp.where(low_x, 1.0 - frac_x, jnp.where(high_x, frac_x, 0.0))
    along_y = jnp.where(low_y, 1.0 - frac_y, jnp.where(high_y, frac_y, 0.0))
    return along_x, along_y


def slopes_of(hits):
    low_x, high_x, low_y, high_y = hits
    along_x = jnp.where(low_x, -1.0, jnp.where(high_x, 1.0, 0.0))
    along_y = jnp.where(low_y, -1.0, jnp.where(high_y, 1.0, 0.0))
    return along_x, along_y


def row3(ref, at, first=0):
    return [ref[first + k : first + k + 1, at] for k in range(3)]


def line_matrix(me, window, offset, rows, first_y):
    target = lax.broadcasted_iota(jnp.int32, (ROWS, 8 * window), 0)
    column = lax.broadcasted_iota(jnp.int32, (ROWS, 8 * window), 1)
    device = column // window
    source = column - device * window - offset
    away = (CY * (me - device) + target - 2 - source - first_y + 128) & 63
    away = jnp.minimum(away, 64 - away)
    weight = STRENGTH * jnp.exp(away.astype(F32) * (-1.0 / 16.0))
    return jnp.where((source >= 0) & (source < rows), weight, 0.0)


def depth_body(out):
    target = lax.broadcasted_iota(jnp.int32, (NZ, NZ), 0)
    source = lax.broadcasted_iota(jnp.int32, (NZ, NZ), 1)
    away = jnp.abs(target - source)
    away = jnp.minimum(away, NZ - away)
    put_split(out, 0, jnp.exp(away.astype(F32) * (-1.0 / 16.0)))


def product(a, b_high, b_low):
    a_high, a_low = split(a)
    dot = functools.partial(jnp.dot, preferred_element_type=F32)
    return dot(a_high, b_high) + (dot(a_high, b_low) + dot(a_low, b_high))


def smooth(me, depth, gathered, planes, rows, first_y, window, kept):
    for p in range(planes):
        first = min(p * rows // 8 * 8, gathered.shape[1] - window)
        lines = line_matrix(me, window, p * rows - first, rows, first_y)
        source = gathered[:, first : first + window, :].reshape(8 * window, NZ)
        kept[p * ROWS : (p + 1) * ROWS, :] = product(lines, *split(source))
    kept[0 : planes * ROWS, :] = product(
        kept[0 : planes * ROWS, :], depth[0:NZ, :], depth[NZ : 2 * NZ, :]
    )


def select_pulls(table, where_to, moved):
    taken = pick_from(table, one_hot(where_to & 255))
    chosen = moved * 16 + lax.shift_right_logical(where_to, 8)
    here = lax.broadcasted_iota(jnp.int32, (80, where_to.shape[1]), 0) == chosen
    return [
        jnp.sum(jnp.where(here, taken[k * 80 : k * 80 + 80, :], 0.0), axis=0, keepdims=True) for k in range(3)
    ]


def deposit_first_body(
    pos, mom, cell, dest, slot, pull_pos, pull_mom, own, up, down, state, labels, held, ints, lone, sems, lhs, acc
):
    copies = [
        pltpu.make_async_copy(pos, held.at[0], sems.at[0]),
        pltpu.make_async_copy(mom, held.at[1], sems.at[1]),
        pltpu.make_async_copy(cell, ints, sems.at[2]),
        pltpu.make_async_copy(dest, lone.at[0], sems.at[3]),
        pltpu.make_async_copy(slot, lone.at[1], sems.at[4]),
        pltpu.make_async_copy(pull_pos, held.at[2], sems.at[5]),
        pltpu.make_async_copy(pull_mom, held.at[3], sems.at[6]),
    ]
    for copy in copies:
        copy.start()
    own[...] = jnp.zeros_like(own)
    acc[...] = jnp.zeros_like(acc)
    for copy in copies:
        copy.wait()
    state[0:3, :] = held[0] + STEP * held[1]
    state[3:6, :] = held[1]
    labels[0:3, :] = ints[...]
    labels[3:4, :] = lone[0]
    labels[4:5, :] = lone[1]

    def block(b, carry):
        at = pl.ds(pl.multiple_of(b * BLK, BLK), BLK)
        frac = row3(state, at)
        cells = row3(labels, at)
        along_x, along_y = weights_of(axis_hits(27, CY + 1, 32, cells[0], cells[1]), frac[0], frac[1])
        planar = along_x * along_y
        put_split(lhs, 0, planar * (1.0 - frac[2]))
        put_split(lhs, 32, planar * frac[2])
        acc[...] += spread_onto(lhs, cells[2])
        return carry

    lax.fori_loop(0, NQ // BLK, block, 0)
    density = acc[0:32, :] + prev_z(acc[32:64, :])
    for x in range(3):
        own[x * ROWS + 2 : x * ROWS + 11, :] = density[x * 9 : x * 9 + 9, :]
    up[0:32, :] = own[16:48, :]
    down[0:32, :] = own[0:32, :]
    for k in range(6):
        source = held.at[2 + k // 3]
        for c in range(16):
            line = source[k % 3 : k % 3 + 1, c * 256 : (c + 1) * 256]
            at_row = 32 + k * 16 + c
            up[at_row : at_row + 1, :] = line
            down[at_row : at_row + 1, :] = line


def fold_first_body(own, left, right, out):
    rows = slice(2, 11)
    out[0:9, :] = left[0:16, :][rows]
    out[9:18, :] = (own[0:16, :] + left[16:32, :])[rows]
    out[18:27, :] = own[16:32, :][rows]
    out[27:36, :] = (own[32:48, :] + right[0:16, :])[rows]
    out[36:45, :] = right[16:32, :][rows]
    out[45:48, :] = jnp.zeros((3, NZ), F32)


def step_body(
    place,
    state,
    labels,
    depth,
    gathered,
    mine,
    left,
    right,
    below,
    above,
    own,
    up,
    down,
    drift,
    pulls,
    fields,
    kept,
    pack,
    table,
    lhs,
    acc,
    planes,
):
    smooth(place[0], depth, gathered, 5, 9, 0, 16, kept)
    pack[...] = jnp.zeros_like(pack)
    for x in range(3):
        mid = (x + 1) * ROWS
        east = kept[mid + 18 : mid + 27, :]
        west = kept[mid - 14 : mid - 5, :]
        pack[x * 9 : x * 9 + 9, :] = -0.5 * (east - west)
        north = kept[mid + 3 : mid + 12, :]
        south = kept[mid + 1 : mid + 10, :]
        pack[32 + x * 9 : 32 + x * 9 + 9, :] = -0.5 * (north - south)
        pack[64 + x * 9 : 64 + x * 9 + 9, :] = -diff_z(kept[mid : mid + 16, :])[2:11, :]
    put_split(fields, 0, pack[...])
    put_split(fields, 96, next_z(pack[...]))
    fill_table(table, 80, (mine, right, left, above, below))
    acc[...] = jnp.zeros_like(acc)

    def block(b, carry):
        at = pl.ds(pl.multiple_of(b * BLK, BLK), BLK)
        frac = row3(state, at)
        momentum = row3(state, at, 3)
        cells = row3(labels, at)
        moved = labels[3:4, at]
        where_to = labels[4:5, at]
        along_x, along_y = weights_of(axis_hits(27, CY + 1, 32, cells[0], cells[1]), frac[0], frac[1])
        planar = along_x * along_y
        sampled = pick_from(fields, one_hot(cells[2]))
        lower = planar * (1.0 - frac[2])
        upper = planar * frac[2]
        force = [
            jnp.sum(
                lower * sampled[d * 32 : d * 32 + 32, :] + upper * sampled[96 + d * 32 : 128 + d * 32, :],
                axis=0,
                keepdims=True,
            )
            for d in range(3)
        ]
        to_x = jnp.where(moved == 1, 1, jnp.where(moved == 2, -1, 0))
        to_y = jnp.where(moved == 3, 1, jnp.where(moved == 4, -1, 0))
        shift = [to_x.astype(F32), to_y.astype(F32), 0.0]
        second = [frac[d] - shift[d] + STEP * (momentum[d] + STEP * force[d]) for d in range(3)]
        home = select_pulls(table, where_to, moved)
        for d in range(3):
            drift[d : d + 1, at] = second[d]
            pulls[d : d + 1, at] = home[d]
        along_x, along_y = weights_of(
            axis_hits(55, CY + 3, 64, cells[0] + to_x + 1, cells[1] + to_y + 1), second[0], second[1]
        )
        planar = along_x * along_y
        upper = planar * second[2]
        lower = planar - upper
        for c in range(4):
            scale = None if c == 0 else STEP * home[c - 1]
            put_split(lhs, c * 128, lower if c == 0 else lower * scale)
            put_split(lhs, c * 128 + 64, upper if c == 0 else upper * scale)
        acc[...] += spread_onto(lhs, cells[2])
        return carry

    lax.fori_loop(0, NQ // BLK, block, 0)
    planes[...] = jnp.zeros_like(planes)
    for c in range(4):
        total = acc[c * 128 : c * 128 + 64, :] + prev_z(acc[c * 128 + 64 : c * 128 + 128, :])
        for x in range(5):
            planes[c, x, 1:12, :] = total[x * 11 : x * 11 + 11, :]
    for x in range(5):
        planes[2, x] = diff_row(planes[2, x]) + diff_z(planes[3, x])
    for c in range(3):
        for x in range(3):
            own[(c * 3 + x) * 16 : (c * 3 + x) * 16 + 16, :] = planes[c, x + 1]
        for x in range(2):
            up[(c * 2 + x) * 16 : (c * 2 + x) * 16 + 16, :] = planes[c, x + 3]
            down[(c * 2 + x) * 16 : (c * 2 + x) * 16 + 16, :] = planes[c, x]


def fill_table(table, first, sources):
    for k in range(3):
        for t, source in enumerate(sources):
            put_split(table, k * 80 + t * 16, source[first + k * 16 : first + k * 16 + 16, :])


def pulls_body(labels, mine, left, right, below, above, pulls, table):
    fill_table(table, 32, (mine, right, left, above, below))

    def block(b, carry):
        at = pl.ds(pl.multiple_of(b * BLK, BLK), BLK)
        home = select_pulls(table, labels[4:5, at], labels[3:4, at])
        for d in range(3):
            pulls[d : d + 1, at] = home[d]
        return carry

    lax.fori_loop(0, NQ // BLK, block, 0)


def fold_body(channels, own, left, right, out):
    rows = out.shape[0] // (channels * 3)
    spare = out.shape[0] - channels * 3 * rows
    if spare:
        out[channels * 3 * rows :, :] = jnp.zeros((spare, NZ), F32)
    for c in range(channels):
        mine, theirs, to = c * 48, c * 32, c * 3 * rows
        first = own[mine : mine + 16, :] + left[theirs : theirs + 16, :]
        second = (
            own[mine + 16 : mine + 32, :]
            + left[theirs + 16 : theirs + 32, :]
            + right[theirs : theirs + 16, :]
        )
        third = own[mine + 32 : mine + 48, :] + right[theirs + 16 : theirs + 32, :]
        for n, values in enumerate((first, second, third)):
            out[to + n * rows : to + (n + 1) * rows, :] = values[0:rows]


def lines_body(place, depth, gathered, own, up, down):
    smooth(place[0], depth, gathered, 9, 13, -2, 24, own)
    for c in range(2):
        up[c * 32 : c * 32 + 32, :] = own[c * 48 : c * 48 + 32, :]
        down[c * 32 : c * 32 + 32, :] = own[c * 48 + 16 : c * 48 + 48, :]
    up[64:80, :] = own[112:128, :]
    down[64:80, :] = own[112:128, :]


def back_body(
    state, labels, drift, pulls, pulls_pos, mine, left, right, own, up, down, grads, wide, pack, fields, lhs, acc, planes
):
    for c in range(2):
        wide[c, 0:32, :] = left[c * 32 : c * 32 + 32, :]
        wide[c, 32:80, :] = mine[c * 48 : c * 48 + 48, :]
        wide[c, 80:112, :] = right[c * 32 : c * 32 + 32, :]
    wide[2, 16:32, :] = left[64:80, :]
    wide[2, 32:80, :] = mine[96:144, :]
    wide[2, 80:96, :] = right[64:80, :]
    pack[...] = jnp.zeros_like(pack)
    for x in range(5):
        mid = (x + 1) * 16
        first = x * 11
        pack[first : first + 11, :] = -0.5 * (wide[0, mid + 17 : mid + 28, :] - wide[0, mid - 15 : mid - 4, :])
        pack[64 + first : 75 + first, :] = -0.5 * (
            wide[0, mid + 2 : mid + 13, :] - wide[0, mid : mid + 11, :]
        )
        pack[128 + first : 139 + first, :] = -diff_z(wide[0, mid : mid + 16, :])[1:12, :]
        pack[192 + first : 203 + first, :] = (
            0.5 * (wide[1, mid + 17 : mid + 28, :] - wide[1, mid - 15 : mid - 4, :])
            + wide[2, mid + 1 : mid + 12, :]
        )
    put_split(fields, 0, pack[...])
    put_split(fields, 256, next_z(pack[...]))
    acc[...] = jnp.zeros_like(acc)

    def block(b, carry):
        at = pl.ds(pl.multiple_of(b * BLK, BLK), BLK)
        cells = row3(labels, at)
        moved = labels[3:4, at]
        second = row3(drift, at)
        pull_position = row3(pulls_pos, at)
        pull_momentum = row3(pulls, at)
        to_x = jnp.where(moved == 1, 1, jnp.where(moved == 2, -1, 0))
        to_y = jnp.where(moved == 3, 1, jnp.where(moved == 4, -1, 0))
        hits = axis_hits(55, CY + 3, 64, cells[0] + to_x + 1, cells[1] + to_y + 1)
        along_x, along_y = weights_of(hits, second[0], second[1])
        slope_x, slope_y = slopes_of(hits)
        sampled = pick_from(fields, one_hot(cells[2]))
        sides = []
        for s in range(2):
            mixed = sampled[s * 256 + 192 : s * 256 + 256, :]
            for d in range(3):
                mixed = mixed + (STEP * pull_momentum[d]) * sampled[s * 256 + d * 64 : s * 256 + d * 64 + 64, :]
            sides.append(mixed)
        level = sides[0] + second[2] * (sides[1] - sides[0])
        rise = sides[1] - sides[0]
        slopes = [
            jnp.sum(slope_x * (along_y * level), axis=0, keepdims=True),
            jnp.sum(slope_y * (along_x * level), axis=0, keepdims=True),
            jnp.sum(along_x * (along_y * rise), axis=0, keepdims=True),
        ]
        grad_drift = [pull_position[d] + slopes[d] for d in range(3)]
        grad_kick = [pull_momentum[d] + STEP * grad_drift[d] for d in range(3)]
        for d in range(3):
            grads[d : d + 1, at] = grad_drift[d]
            grads[d + 3 : d + 4, at] = grad_kick[d]
        frac = row3(state, at)
        along_x, along_y = weights_of(axis_hits(27, CY + 1, 32, cells[0], cells[1]), frac[0], frac[1])
        planar = along_x * along_y
        above = planar * frac[2]
        below = planar - above
        for c in range(3):
            scale = STEP * grad_kick[c]
            put_split(lhs, c * 64, below * scale)
            put_split(lhs, c * 64 + 32, above * scale)
        acc[...] += spread_onto(lhs, cells[2])
        return carry

    lax.fori_loop(0, NQ // BLK, block, 0)
    planes[...] = jnp.zeros_like(planes)
    for c in range(3):
        total = acc[c * 64 : c * 64 + 32, :] + prev_z(acc[c * 64 + 32 : c * 64 + 64, :])
        for x in range(3):
            planes[c, x + 2, 2:11, :] = total[x * 9 : x * 9 + 9, :]
    for x in range(5):
        spread = 0.5 * (planes[0, x + 2] - planes[0, x])
        if 1 <= x <= 3:
            spread = spread + diff_row(planes[1, x + 1]) + diff_z(planes[2, x + 1])
        if 1 <= x <= 3:
            own[(x - 1) * 16 : x * 16, :] = spread
        if x >= 3:
            up[(x - 3) * 16 : (x - 2) * 16, :] = spread
        if x <= 1:
            down[x * 16 : (x + 1) * 16, :] = spread


def last_body(place, state, labels, depth, grads, fields, gathered, grad_pos, grad_mom, kept, pack, own_field):
    smooth(place[0], depth, gathered, 3, 16, -2, 16, kept)
    pack[...] = jnp.zeros_like(pack)
    for x in range(3):
        pack[x * 9 : x * 9 + 9, :] = kept[x * 16 + 2 : x * 16 + 11, :]
    put_split(own_field, 0, pack[...])
    put_split(own_field, 32, next_z(pack[...]))

    def block(b, carry):
        at = pl.ds(pl.multiple_of(b * BLK, BLK), BLK)
        frac = row3(state, at)
        cells = row3(labels, at)
        hot = one_hot(cells[2])
        hits = axis_hits(27, CY + 1, 32, cells[0], cells[1])
        along_x, along_y = weights_of(hits, frac[0], frac[1])
        slope_x, slope_y = slopes_of(hits)
        grad_drift = row3(grads, at)
        grad_kick = row3(grads, at, 3)
        sampled = pick_from(fields, hot)
        pulled = pick_from(own_field, hot)
        sides = []
        for s in range(2):
            mixed = pulled[s * 32 : s * 32 + 32, :]
            for d in range(3):
                mixed = mixed + (STEP * grad_kick[d]) * sampled[s * 96 + d * 32 : s * 96 + d * 32 + 32, :]
            sides.append(mixed)
        level = sides[0] + frac[2] * (sides[1] - sides[0])
        rise = sides[1] - sides[0]
        slopes = [
            jnp.sum(slope_x * (along_y * level), axis=0, keepdims=True),
            jnp.sum(slope_y * (along_x * level), axis=0, keepdims=True),
            jnp.sum(along_x * (along_y * rise), axis=0, keepdims=True),
        ]
        for d in range(3):
            total = grad_drift[d] + slopes[d]
            grad_pos[d : d + 1, at] = total
            grad_mom[d : d + 1, at] = grad_kick[d] + STEP * total
        return carry

    lax.fori_loop(0, NQ // BLK, block, 0)


def swap(up, down, axis):
    peers = lax.axis_size(axis)
    forward = [(i, (i + 1) % peers) for i in range(peers)]
    backward = [((i + 1) % peers, i) for i in range(peers)]
    return lax.ppermute(up, axis, forward), lax.ppermute(down, axis, backward)


def gather_y(x):
    return lax.all_gather(x, "gy", axis=0, tiled=False)


def local(pos, mom, cell, cell_second, dest, slot, pull_pos, pull_mom):
    place = lax.axis_index("gy").astype(jnp.int32).reshape(1)
    dest = dest.reshape(1, NQ)
    slot = slot.reshape(1, NQ)
    scalar = pl.BlockSpec(memory_space=pltpu.SMEM)
    vmem = pl.BlockSpec(memory_space=pltpu.VMEM)

    def call_at(body, outs, scratch, operands):
        return pl.pallas_call(
            body,
            out_shape=outs,
            in_specs=[scalar] + [vmem] * operands,
            scratch_shapes=list(scratch),
            compiler_params=pltpu.CompilerParams(vmem_limit_bytes=VMEM_LIMIT),
        )

    depth = pl.pallas_call(
        depth_body,
        out_shape=shape(2 * NZ, NZ, dtype=BF16),
        compiler_params=pltpu.CompilerParams(vmem_limit_bytes=VMEM_LIMIT),
        cost_estimate=pl.CostEstimate(flops=10**9, bytes_accessed=10**7, transcendentals=10**6),
    )()
    in_hbm = [
        pltpu.with_memory_space_constraint(x, pltpu.HBM)
        for x in (pos, mom, cell, dest, slot, pull_pos, pull_mom)
    ]
    own, up, down, state, labels = pl.pallas_call(
        deposit_first_body,
        out_shape=(
            shape(48, NZ),
            shape(128, NZ),
            shape(128, NZ),
            shape(6, NQ),
            shape(5, NQ, dtype=jnp.int32),
        ),
        in_specs=[pl.BlockSpec(memory_space=pltpu.HBM)] * 7,
        scratch_shapes=[
            pltpu.VMEM((4, 3, NQ), F32),
            pltpu.VMEM((3, NQ), jnp.int32),
            pltpu.VMEM((2, 1, NQ), jnp.int32),
            pltpu.SemaphoreType.DMA((7,)),
            pltpu.VMEM((128, BLK), BF16),
            pltpu.VMEM((64, NZ), F32),
        ],
        compiler_params=pltpu.CompilerParams(vmem_limit_bytes=VMEM_LIMIT),
    )(*in_hbm)
    mine, (left, right) = up, swap(up, down, "gx")
    below, above = swap(up, up, "gy")
    first_left, first_right = left, right
    gathered = gather_y(call(fold_first_body, shape(48, NZ))(own, left, right))
    own, up, down, drift, pulls, fields = call_at(
        step_body,
        (
            shape(144, NZ),
            shape(96, NZ),
            shape(96, NZ),
            shape(3, NQ),
            shape(3, NQ),
            shape(384, NZ, dtype=BF16),
        ),
        [
            pltpu.VMEM((80, NZ), F32),
            pltpu.VMEM((96, NZ), F32),
            pltpu.VMEM((480, NZ), BF16),
            pltpu.VMEM((1024, BLK), BF16),
            pltpu.VMEM((512, NZ), F32),
            pltpu.VMEM((4, 5, ROWS, NZ), F32),
        ],
        9,
    )(place, state, labels, depth, gathered, mine, left, right, below, above)
    left, right = swap(up, down, "gx")
    gathered = gather_y(call(functools.partial(fold_body, 3), shape(120, NZ))(own, left, right))
    own, up, down = call_at(lines_body, (shape(144, NZ), shape(80, NZ), shape(80, NZ)), [], 2)(
        place, depth, gathered
    )
    left, right = swap(up, down, "gx")
    pulls_pos = call(pulls_body, shape(3, NQ), [pltpu.VMEM((480, NZ), BF16)])(
        labels, mine, first_left, first_right, below, above
    )
    own, up, down, grads = call(
        back_body,
        (shape(48, NZ), shape(32, NZ), shape(32, NZ), shape(6, NQ)),
        [
            pltpu.VMEM((3, 112, NZ), F32),
            pltpu.VMEM((256, NZ), F32),
            pltpu.VMEM((1024, NZ), BF16),
            pltpu.VMEM((384, BLK), BF16),
            pltpu.VMEM((192, NZ), F32),
            pltpu.VMEM((3, 7, ROWS, NZ), F32),
        ],
    )(state, labels, drift, pulls, pulls_pos, own, left, right)
    left, right = swap(up, down, "gx")
    gathered = gather_y(call(functools.partial(fold_body, 1), shape(48, NZ))(own, left, right))
    return call_at(
        last_body,
        (shape(3, NQ), shape(3, NQ)),
        [pltpu.VMEM((48, NZ), F32), pltpu.VMEM((32, NZ), F32), pltpu.VMEM((128, NZ), BF16)],
        6,
    )(place, state, labels, depth, grads, fields, gathered)


def solution(mesh):
    both = ("gx", "gy")
    return jax.shard_map(
        local,
        mesh=mesh,
        in_specs=(P(None, both), P(None, both), P(None, both), P(None, both), P(both), P(both), P(None, both), P(None, both)),
        out_specs=(P(None, both), P(None, both)),
        check_vma=False,
    )
```

time: 195 us -> 128 us (0.66)
  waiting for transfers between devices: 76.4 us -> 2.79 us
  blocking collectives: 17.1 us -> 54 us
  Pallas kernels: 35.2 us -> 17.5 us
  between operations: 14.2 us -> 0.8 us
  local copies, waits for them, and re-layouts: 10.8 us -> 0 us
  starting transfers between devices: 40.8 us -> 50.7 us
    all_gather x2 -> x0, waiting for transfers between devices: 64.3 us -> none  [gather_y(): return lax.all_gather(x, 'gy', axis=0, tiled=False)]
    all_gather x1 -> x3, blocking collectives: 17.1 us -> 54 us  [gather_y(): return lax.all_gather(x, 'gy', axis=0, tiled=False)]
    unnamed x32 -> x0, local copies, waits for them, and re-layouts: 10.8 us -> none
    ppermute x8 -> x10, starting transfers between devices: 40.7 us -> 50.7 us  [swap(): return (lax.ppermute(up, axis, forward), lax.ppermute(down, axis, backward))]
    ppermute x8 -> x10, waiting for transfers between devices: 12.1 us -> 2.79 us  [swap(): return (lax.ppermute(up, axis, forward), lax.ppermute(down, axis, backward))]
    pallas_call x1, Pallas kernels: 12.6 us -> 4.44 us  [local(): call(back_body, (shape(48, NZ), shape(32, NZ), shape(32, NZ), shape(6, NQ...]
    pallas_call x1, Pallas kernels: 13.7 us -> 5.9 us  [local(): call_at(step_body, (shape(144, NZ), shape(96, NZ), shape(96, NZ), shape(3...]
    pallas_call x4 -> x6, Pallas kernels: 4.71 us -> 4.44 us  [the longest x1 2.21 us: local(): pl.pallas_call(deposit_first_body, out_shape=(shape(48, NZ), shape(128, N...]
  transfers between devices with their start and end apart: 10 -> 10, of which waited for: 9 -> 4; matrix products, arithmetic and copies ran while one was open for 0% -> 0% of each run, Pallas kernels for 0% -> 1%
where the time goes in v3:
time: 128 us; the launch traced here: 126 us
  blocking collectives  54 us (42%)
  starting transfers between devices  50.7 us (40%)
  Pallas kernels  17.5 us (14%)
  waiting for transfers between devices  2.79 us (2%)
    all_gather x3, blocking collectives, gather_y(): return lax.all_gather(x, 'gy', axis=0, tiled=False)  54 us
    ppermute x10, starting transfers between devices, swap(): return (lax.ppermute(up, axis, forward), lax.ppermute(down, axis, backward))  50.7 us
    pallas_call x1, Pallas kernels, local(): call_at(step_body, (shape(144, NZ), shape(96, NZ), shape(96, NZ), shape(3...  5.9 us
    pallas_call x1, Pallas kernels, local(): call(back_body, (shape(48, NZ), shape(32, NZ), shape(32, NZ), shape(6, NQ...  4.44 us
    ppermute x10, waiting for transfers between devices, swap(): return (lax.ppermute(up, axis, forward), lax.ppermute(down, axis, backward))  2.79 us
    pallas_call x1, Pallas kernels, local(): call_at(last_body, (shape(3, NQ), shape(3, NQ)), [pltpu.VMEM((48, NZ), F3...  2.74 us
  transfers between devices with their start and end apart: 10, of which 4 were waited for; matrix products, arithmetic and copies ran while one was open for 0% of the time, Pallas kernels for 1%

profile of v3, /device:TPU:1, one launch (start us, length us, event | category | flops | bytes accessed | tf_op | source)
XLA Modules:
  0.0 125.8 jit_solution(17757399124690778617)
XLA Ops:
  0.6 2.2 %shard_map.86 = (f32[48,256]{1,0:T(8,128)S(1)}, f32[128,256]{1,0:T(8,128)S(1)}, f32[128,256]{1,0:T(8,128)S(1)}, f32[6,4096]{1,0:T(8,128)S(1)}, s32[5,4096]{1,0:T(8,128)S(1)}) custom-call(f32[3,4096]{1,0:T(4,128)} %pos.1, f32[3,4096]{1,0:T(4,128)} %mom.1, s32[3,4096]{1,0:T(4,128)} %cell.1, s32[1,4096]{1,0:T(1,128)} %bitcast.9, s32[1,4096]{1,0:T(1,128)} %bitcast.10, ...), custom_call_target="tpu_custom_call" | custom-call | tf_op jit(solution)/shard_map/pallas_call | solution.py:544
  2.8 4.0 %collective-permute-start = (f32[128,256]{1,0:T(8,128)S(1)}, f32[128,256]{1,0:T(8,128)S(1)}, u32[]{:S(2)}, u32[]{:S(2)}) collective-permute-start(f32[128,256]{1,0:T(8,128)S(1)} %get-tuple-element.23.mine), channel_id=1, source_target_pairs={{0,8},{8,16},{16,24},{24,32},{32,40},{40,48},{48,56},{56,64},{64,7... | collective-permute-start | bytes 393224 | tf_op jit(solution)/shard_map/ppermute | solution.py:511
  6.9 7.8 %collective-permute-start.1 = (f32[128,256]{1,0:T(8,128)S(1)}, f32[128,256]{1,0:T(8,128)S(1)}, u32[]{:S(2)}, u32[]{:S(2)}) collective-permute-start(f32[128,256]{1,0:T(8,128)S(1)} %get-tuple-element.24), channel_id=1, source_target_pairs={{8,0},{16,8},{24,16},{32,24},{40,32},{48,40},{56,48},{64,56},{72,6... | collective-permute-start | bytes 393224 | tf_op jit(solution)/shard_map/ppermute | solution.py:511
  14.7 6.6 %collective-permute-start.2 = (f32[128,256]{1,0:T(8,128)S(1)}, f32[128,256]{1,0:T(8,128)S(1)}, u32[]{:S(2)}, u32[]{:S(2)}) collective-permute-start(f32[128,256]{1,0:T(8,128)S(1)} %get-tuple-element.23.mine), channel_id=1, source_target_pairs={{0,1},{1,2},{2,3},{3,4},{4,5},{5,6},{6,7},{7,0},{8,9},{9,10},{10,1... | collective-permute-start | bytes 393224 | tf_op jit(solution)/shard_map/ppermute | solution.py:511
  21.4 2.3 %collective-permute-start.3 = (f32[128,256]{1,0:T(8,128)S(1)}, f32[128,256]{1,0:T(8,128)S(1)}, u32[]{:S(2)}, u32[]{:S(2)}) collective-permute-start(f32[128,256]{1,0:T(8,128)S(1)} %get-tuple-element.23.mine), channel_id=1, source_target_pairs={{1,0},{2,1},{3,2},{4,3},{5,4},{6,5},{7,6},{0,7},{9,8},{10,9},{11,1... | collective-permute-start | bytes 393224 | tf_op jit(solution)/shard_map/ppermute | solution.py:511
  23.7 0.1 shard_map.87.depth
  23.8 0.0 collective-permute-done.left
  23.8 0.0 collective-permute-done.1.right
  23.8 19.1 %all-gather = f32[384,256]{1,0:T(8,128)S(1)} all-gather(f32[48,256]{1,0:T(8,128)S(1)} %shard_map.88), channel_id=2, replica_groups=mesh['gx'=64,'gy'=8] {'gy'}, dimensions={0}, use_global_device_ids=true | all-gather | bytes 442368 | tf_op jit(solution)/shard_map/all_gather | solution.py:515
  42.9 0.0 collective-permute-done.2.below
  42.9 0.0 collective-permute-done.3.above
  42.9 5.9 %shard_map.89 = (f32[144,256]{1,0:T(8,128)S(1)}, f32[96,256]{1,0:T(8,128)S(1)}, f32[96,256]{1,0:T(8,128)S(1)}, f32[3,4096]{1,0:T(4,128)S(1)}, f32[3,4096]{1,0:T(4,128)S(1)}, /*index=5*/bf16[384,256]{1,0:T(8,128)(2,1)S(1)}) custom-call(s32[1]{0:T(128)} %bitcast.place, f32[6,4096]{1,0:T(8,128)S(1)} %get-tuple-element.20.state, ...), custom_call_target="tpu_custom_call" | custom-call | tf_op jit(solution)/shard_map/pallas_call | solution.py:568
  48.8 1.9 %collective-permute-start.4 = (f32[96,256]{1,0:T(8,128)S(1)}, f32[96,256]{1,0:T(8,128)S(1)}, u32[]{:S(2)}, u32[]{:S(2)}) collective-permute-start(f32[96,256]{1,0:T(8,128)S(1)} %get-tuple-element.28), channel_id=1, source_target_pairs={{0,8},{8,16},{16,24},{24,32},{32,40},{40,48},{48,56},{56,64},{64,7... | collective-permute-start | bytes 294920 | tf_op jit(solution)/shard_map/ppermute | solution.py:511
  50.7 7.6 %collective-permute-start.5 = (f32[96,256]{1,0:T(8,128)S(1)}, f32[96,256]{1,0:T(8,128)S(1)}, u32[]{:S(2)}, u32[]{:S(2)}) collective-permute-start(f32[96,256]{1,0:T(8,128)S(1)} %get-tuple-element.29), channel_id=1, source_target_pairs={{8,0},{16,8},{24,16},{32,24},{40,32},{48,40},{56,48},{64,56},{72,6... | collective-permute-start | bytes 294920 | tf_op jit(solution)/shard_map/ppermute | solution.py:511
  58.3 0.8 collective-permute-done.4.left
  59.1 0.8 collective-permute-done.5.right
  59.9 18.2 %all-gather.1 = f32[960,256]{1,0:T(8,128)S(1)} all-gather(f32[120,256]{1,0:T(8,128)S(1)} %shard_map.91), channel_id=3, replica_groups=mesh['gx'=64,'gy'=8] {'gy'}, dimensions={0}, use_global_device_ids=true | all-gather | bytes 1105920 | tf_op jit(solution)/shard_map/all_gather | solution.py:515
  78.1 0.8 shard_map.92
  78.9 1.9 %collective-permute-start.6 = (f32[80,256]{1,0:T(8,128)S(1)}, f32[80,256]{1,0:T(8,128)S(1)}, u32[]{:S(2)}, u32[]{:S(2)}) collective-permute-start(f32[80,256]{1,0:T(8,128)S(1)} %get-tuple-element.31), channel_id=1, source_target_pairs={{0,8},{8,16},{16,24},{24,32},{32,40},{40,48},{48,56},{56,64},{64,7... | collective-permute-start | bytes 245768 | tf_op jit(solution)/shard_map/ppermute | solution.py:511
  80.8 8.2 %collective-permute-start.7 = (f32[80,256]{1,0:T(8,128)S(1)}, f32[80,256]{1,0:T(8,128)S(1)}, u32[]{:S(2)}, u32[]{:S(2)}) collective-permute-start(f32[80,256]{1,0:T(8,128)S(1)} %get-tuple-element.32), channel_id=1, source_target_pairs={{8,0},{16,8},{24,16},{32,24},{40,32},{48,40},{56,48},{64,56},{72,6... | collective-permute-start | bytes 245768 | tf_op jit(solution)/shard_map/ppermute | solution.py:511
  89.1 1.3 %shard_map.90.pulls_pos = f32[3,4096]{1,0:T(4,128)S(1)} custom-call(s32[5,4096]{1,0:T(8,128)S(1)} %get-tuple-element.21.labels, f32[128,256]{1,0:T(8,128)S(1)} %get-tuple-element.23.mine, f32[128,256]{1,0:T(8,128)S(1)} %collective-permute-done.left, f32[128,256]{1,0:T(8,128)S(1)} %collective-permute-done.1.right, ...), custom_call_target="tpu_custom_call" | custom-call | tf_op jit(solution)/shard_map/pallas_call | solution.py:594
  90.4 0.0 collective-permute-done.6.left
  90.4 0.2 collective-permute-done.7.right
  90.6 4.4 %shard_map.93 = (f32[48,256]{1,0:T(8,128)S(1)}, f32[32,256]{1,0:T(8,128)S(1)}, f32[32,256]{1,0:T(8,128)S(1)}, f32[6,4096]{1,0:T(8,128)S(1)}) custom-call(f32[6,4096]{1,0:T(8,128)S(1)} %get-tuple-element.20.state, s32[5,4096]{1,0:T(8,128)S(1)} %get-tuple-element.21.labels, f32[3,4096]{1,0:T(4,128)S(1)} %get-tuple-element.25.drift, ...), custom_call_target="tpu_custom_call" | custom-call | tf_op jit(solution)/shard_map/pallas_call | solution.py:597
  95.0 1.9 %collective-permute-start.8 = (f32[32,256]{1,0:T(8,128)S(1)}, f32[32,256]{1,0:T(8,128)S(1)}, u32[]{:S(2)}, u32[]{:S(2)}) collective-permute-start(f32[32,256]{1,0:T(8,128)S(1)} %get-tuple-element.36), channel_id=1, source_target_pairs={{0,8},{8,16},{16,24},{24,32},{32,40},{40,48},{48,56},{56,64},{64,7... | collective-permute-start | bytes 98312 | tf_op jit(solution)/shard_map/ppermute | solution.py:511
  97.0 8.3 %collective-permute-start.9 = (f32[32,256]{1,0:T(8,128)S(1)}, f32[32,256]{1,0:T(8,128)S(1)}, u32[]{:S(2)}, u32[]{:S(2)}) collective-permute-start(f32[32,256]{1,0:T(8,128)S(1)} %get-tuple-element.37), channel_id=1, source_target_pairs={{8,0},{16,8},{24,16},{32,24},{40,32},{48,40},{56,48},{64,56},{72,6... | collective-permute-start | bytes 98312 | tf_op jit(solution)/shard_map/ppermute | solution.py:511
  105.3 0.0 collective-permute-done.8.left
  105.3 1.0 collective-permute-done.9.right
  106.3 16.7 %all-gather.2 = f32[384,256]{1,0:T(8,128)S(1)} all-gather(f32[48,256]{1,0:T(8,128)S(1)} %shard_map.94), channel_id=4, replica_groups=mesh['gx'=64,'gy'=8] {'gy'}, dimensions={0}, use_global_device_ids=true | all-gather | bytes 442368 | tf_op jit(solution)/shard_map/all_gather | solution.py:515
  123.0 2.7 %shard_map.95 = (f32[3,4096]{1,0:T(4,128)}, f32[3,4096]{1,0:T(4,128)}) custom-call(s32[1]{0:T(128)} %bitcast.place, f32[6,4096]{1,0:T(8,128)S(1)} %get-tuple-element.20.state, s32[5,4096]{1,0:T(8,128)S(1)} %get-tuple-element.21.labels, bf16[512,256]{1,0:T(8,128)(2,1)S(1)} %shard_map.87.depth, f32[6,4096]{1,0:T(8,128)S(1)} %get-tuple-element.33.grads, ...), custom_call_target="tpu_custom_call" | custom-call | tf_op jit(solution)/shard_map/pallas_call | solution.py:611
  (3 shorter events, 0.0 us)
Async XLA Ops:
  2.8 20.9 %collective-permute-start = (f32[128,256]{1,0:T(8,128)S(1)}, f32[128,256]{1,0:T(8,128)S(1)}, u32[]{:S(2)}, u32[]{:S(2)}) collective-permute-start(f32[128,256]{1,0:T(8,128)S(1)} %get-tuple-element.23.mine), channel_id=1, source_target_pairs={{0,8},{8,16},{16,24},{24,32},{32,40},{40,48},{48,56},{56,64},{64,7... | collective-permute-start | bytes 393224 | tf_op jit(solution)/shard_map/ppermute | solution.py:511
  6.9 16.9 %collective-permute-start.1 = (f32[128,256]{1,0:T(8,128)S(1)}, f32[128,256]{1,0:T(8,128)S(1)}, u32[]{:S(2)}, u32[]{:S(2)}) collective-permute-start(f32[128,256]{1,0:T(8,128)S(1)} %get-tuple-element.24), channel_id=1, source_target_pairs={{8,0},{16,8},{24,16},{32,24},{40,32},{48,40},{56,48},{64,56},{72,6... | collective-permute-start | bytes 393224 | tf_op jit(solution)/shard_map/ppermute | solution.py:511
  14.7 28.2 %collective-permute-start.2 = (f32[128,256]{1,0:T(8,128)S(1)}, f32[128,256]{1,0:T(8,128)S(1)}, u32[]{:S(2)}, u32[]{:S(2)}) collective-permute-start(f32[128,256]{1,0:T(8,128)S(1)} %get-tuple-element.23.mine), channel_id=1, source_target_pairs={{0,1},{1,2},{2,3},{3,4},{4,5},{5,6},{6,7},{7,0},{8,9},{9,10},{10,1... | collective-permute-start | bytes 393224 | tf_op jit(solution)/shard_map/ppermute | solution.py:511
  21.4 21.5 %collective-permute-start.3 = (f32[128,256]{1,0:T(8,128)S(1)}, f32[128,256]{1,0:T(8,128)S(1)}, u32[]{:S(2)}, u32[]{:S(2)}) collective-permute-start(f32[128,256]{1,0:T(8,128)S(1)} %get-tuple-element.23.mine), channel_id=1, source_target_pairs={{1,0},{2,1},{3,2},{4,3},{5,4},{6,5},{7,6},{0,7},{9,8},{10,9},{11,1... | collective-permute-start | bytes 393224 | tf_op jit(solution)/shard_map/ppermute | solution.py:511
  48.8 10.3 %collective-permute-start.4 = (f32[96,256]{1,0:T(8,128)S(1)}, f32[96,256]{1,0:T(8,128)S(1)}, u32[]{:S(2)}, u32[]{:S(2)}) collective-permute-start(f32[96,256]{1,0:T(8,128)S(1)} %get-tuple-element.28), channel_id=1, source_target_pairs={{0,8},{8,16},{16,24},{24,32},{32,40},{40,48},{48,56},{56,64},{64,7... | collective-permute-start | bytes 294920 | tf_op jit(solution)/shard_map/ppermute | solution.py:511
  50.7 9.2 %collective-permute-start.5 = (f32[96,256]{1,0:T(8,128)S(1)}, f32[96,256]{1,0:T(8,128)S(1)}, u32[]{:S(2)}, u32[]{:S(2)}) collective-permute-start(f32[96,256]{1,0:T(8,128)S(1)} %get-tuple-element.29), channel_id=1, source_target_pairs={{8,0},{16,8},{24,16},{32,24},{40,32},{48,40},{56,48},{64,56},{72,6... | collective-permute-start | bytes 294920 | tf_op jit(solution)/shard_map/ppermute | solution.py:511
  78.9 11.5 %collective-permute-start.6 = (f32[80,256]{1,0:T(8,128)S(1)}, f32[80,256]{1,0:T(8,128)S(1)}, u32[]{:S(2)}, u32[]{:S(2)}) collective-permute-start(f32[80,256]{1,0:T(8,128)S(1)} %get-tuple-element.31), channel_id=1, source_target_pairs={{0,8},{8,16},{16,24},{24,32},{32,40},{40,48},{48,56},{56,64},{64,7... | collective-permute-start | bytes 245768 | tf_op jit(solution)/shard_map/ppermute | solution.py:511
  80.8 9.7 %collective-permute-start.7 = (f32[80,256]{1,0:T(8,128)S(1)}, f32[80,256]{1,0:T(8,128)S(1)}, u32[]{:S(2)}, u32[]{:S(2)}) collective-permute-start(f32[80,256]{1,0:T(8,128)S(1)} %get-tuple-element.32), channel_id=1, source_target_pairs={{8,0},{16,8},{24,16},{32,24},{40,32},{48,40},{56,48},{64,56},{72,6... | collective-permute-start | bytes 245768 | tf_op jit(solution)/shard_map/ppermute | solution.py:511
  95.0 10.3 %collective-permute-start.8 = (f32[32,256]{1,0:T(8,128)S(1)}, f32[32,256]{1,0:T(8,128)S(1)}, u32[]{:S(2)}, u32[]{:S(2)}) collective-permute-start(f32[32,256]{1,0:T(8,128)S(1)} %get-tuple-element.36), channel_id=1, source_target_pairs={{0,8},{8,16},{16,24},{24,32},{32,40},{40,48},{48,56},{56,64},{64,7... | collective-permute-start | bytes 98312 | tf_op jit(solution)/shard_map/ppermute | solution.py:511
  97.0 9.3 %collective-permute-start.9 = (f32[32,256]{1,0:T(8,128)S(1)}, f32[32,256]{1,0:T(8,128)S(1)}, u32[]{:S(2)}, u32[]{:S(2)}) collective-permute-start(f32[32,256]{1,0:T(8,128)S(1)} %get-tuple-element.37), channel_id=1, source_target_pairs={{8,0},{16,8},{24,16},{32,24},{40,32},{48,40},{56,48},{64,56},{72,6... | collective-permute-start | bytes 98312 | tf_op jit(solution)/shard_map/ppermute | solution.py:511

commit v4 on v3

--- a/solution.py
+++ b/solution.py
@@ -19,6 +19,8 @@
 F32 = jnp.float32
 BF16 = jnp.bfloat16
 highest = lax.Precision.HIGHEST
+SECOND_SPANS = [(11 * p, 11, -1) for p in range(6)] + [(66 + 13 * p, 13, -2) for p in range(3)]
+REPLIES = 105
 VMEM_LIMIT = 24 * 1024 * 1024
 
 
@@ -73,14 +75,10 @@
     return halves(jnp.dot(table[...], hot, preferred_element_type=F32))
 
 
-def spread_onto(values, index):
-    if MODE_D == "nt":
-        return halves(
-            lax.dot_general(
-                values[...], one_hot(index), (((1,), (1,)), ((), ())), preferred_element_type=F32
-            )
-        )
-    return halves(jnp.dot(values[...], one_hot_columns(index), preferred_element_type=F32))
+def spread_onto(values, hot):
+    return halves(
+        lax.dot_general(values[...], hot, (((1,), (1,)), ((), ())), preferred_element_type=F32)
+    )
 
 
 def next_z(x):
@@ -100,12 +98,10 @@
 
 
 def axis_hits(rows, pitch, padded, cell_x, cell_y):
-    index = lax.broadcasted_iota(jnp.int32, (padded, cell_x.shape[1]), 0)
+    index = lax.broadcasted_iota(jnp.int32, (padded, 1), 0)
     row_x = index // pitch
     row_y = index - row_x * pitch
-    away_x = row_x - cell_x
-    away_y = row_y - cell_y
-    return away_x == 0, away_x == 1, away_y == 0, away_y == 1
+    return row_x == cell_x, row_x - 1 == cell_x, row_y == cell_y, row_y - 1 == cell_y
 
 
 def weights_of(hits, frac_x, frac_y):
@@ -151,28 +147,79 @@
     return dot(a_high, b_high) + (dot(a_high, b_low) + dot(a_low, b_high))
 
 
-def smooth(me, depth, gathered, planes, rows, first_y, window, kept):
-    for p in range(planes):
-        first = min(p * rows // 8 * 8, gathered.shape[1] - window)
-        lines = line_matrix(me, window, p * rows - first, rows, first_y)
+def smooth(me, depth, gathered, spans, window, kept):
+    for p, (start, rows, first_y) in enumerate(spans):
+        first = min(start // 8 * 8, gathered.shape[1] - window)
+        lines = line_matrix(me, window, start - first, rows, first_y)
         source = gathered[:, first : first + window, :].reshape(8 * window, NZ)
         kept[p * ROWS : (p + 1) * ROWS, :] = product(lines, *split(source))
-    kept[0 : planes * ROWS, :] = product(
-        kept[0 : planes * ROWS, :], depth[0:NZ, :], depth[NZ : 2 * NZ, :]
+    kept[0 : len(spans) * ROWS, :] = product(
+        kept[0 : len(spans) * ROWS, :], depth[0:NZ, :], depth[NZ : 2 * NZ, :]
     )
 
 
 def select_pulls(table, where_to, moved):
     taken = pick_from(table, one_hot(where_to & 255))
+    rows = taken.shape[0] // 3
     chosen = moved * 16 + lax.shift_right_logical(where_to, 8)
-    here = lax.broadcasted_iota(jnp.int32, (80, where_to.shape[1]), 0) == chosen
+    here = lax.broadcasted_iota(jnp.int32, (rows, where_to.shape[1]), 0) == chosen
     return [
-        jnp.sum(jnp.where(here, taken[k * 80 : k * 80 + 80, :], 0.0), axis=0, keepdims=True) for k in range(3)
+        jnp.sum(jnp.where(here, taken[k * rows : k * rows + rows, :], 0.0), axis=0, keepdims=True)
+        for k in range(3)
     ]
 
 
+def requests_body(labels, wanted, ranks, marks, lists):
+    for c in range(16):
+        part = labels[3:4, c * 256 : (c + 1) * 256]
+        marks[c : c + 1, :] = jnp.where(part == 3, 1.0, 0.0)
+        marks[16 + c : 17 + c, :] = jnp.where(part == 4, 1.0, 0.0)
+    row = lax.broadcasted_iota(jnp.int32, (256, 256), 0)
+    column = lax.broadcasted_iota(jnp.int32, (256, 256), 1)
+    earlier = jnp.where(row < column, 1.0, 0.0).astype(BF16)
+    within = jnp.dot(marks[...].astype(BF16), earlier, preferred_element_type=F32)
+    totals = jnp.broadcast_to(jnp.sum(marks[...], axis=1, keepdims=True), (32, 256))
+    row = lax.broadcasted_iota(jnp.int32, (32, 32), 0)
+    column = lax.broadcasted_iota(jnp.int32, (32, 32), 1)
+    earlier = jnp.where((column < row) & (row // 16 == column // 16), 1.0, 0.0).astype(BF16)
+    marks[...] = within + jnp.dot(earlier, totals.astype(BF16), preferred_element_type=F32)
+    for c in range(16):
+        part = labels[3:4, c * 256 : (c + 1) * 256]
+        place = jnp.where(part == 3, marks[c : c + 1, :], jnp.where(part == 4, marks[16 + c : 17 + c, :], -1.0))
+        ranks[0:1, c * 256 : (c + 1) * 256] = place.astype(jnp.int32)
+    moved = labels[3:4, :]
+    where_to = labels[4:5, :]
+    upper = lax.shift_right_logical(where_to, 8).astype(F32)
+    lower = (where_to & 255).astype(F32)
+    lists[...] = jnp.zeros_like(lists)
+    lists[0:1, :] = jnp.where(moved == 3, upper, 0.0)
+    lists[1:2, :] = jnp.where(moved == 3, lower, 0.0)
+    lists[2:3, :] = jnp.where(moved == 4, upper, 0.0)
+    lists[3:4, :] = jnp.where(moved == 4, lower, 0.0)
+    placed = lax.dot_general(
+        lists[...].astype(BF16), one_hot(ranks[...]), (((1,), (1,)), ((), ())), preferred_element_type=F32
+    )
+    wanted[...] = jnp.zeros_like(wanted)
+    wanted[0:1, :] = placed[0:1, :] * 256.0 + placed[1:2, :]
+    wanted[1:2, :] = placed[2:3, :] * 256.0 + placed[3:4, :]
+
+
+def replies_body(place, gathered, lent, out, table):
+    put_split(table, 0, lent[...])
+    out[...] = jnp.zeros_like(out)
+    for n, side in enumerate((lax.rem(place[0] + 7, 8), lax.rem(place[0] + 1, 8))):
+        wanted = gathered[side, 45 + n : 46 + n, :].astype(jnp.int32)
+        taken = pick_from(table, one_hot(wanted & 255))
+        here = lax.broadcasted_iota(jnp.int32, (16, 256), 0) == lax.shift_right_logical(wanted, 8)
+        for k in range(3):
+            row = n * 3 + k
+            out[row : row + 1, :] = jnp.sum(
+                jnp.where(here, taken[k * 16 : k * 16 + 16, :], 0.0), axis=0, keepdims=True
+            )
+
+
 def deposit_first_body(
-    pos, mom, cell, dest, slot, pull_pos, pull_mom, own, up, down, state, labels, held, ints, lone, sems, lhs, acc
+    pos, mom, cell, dest, slot, pull_pos, pull_mom, own, up, down, lent, state, labels, hot, held, ints, lone, sems, lhs, acc
 ):
     copies = [
         pltpu.make_async_copy(pos, held.at[0], sems.at[0]),
@@ -194,6 +241,7 @@
     labels[0:3, :] = ints[...]
     labels[3:4, :] = lone[0]
     labels[4:5, :] = lone[1]
+    hot[...] = one_hot(ints[2:3, :])
 
     def block(b, carry):
         at = pl.ds(pl.multiple_of(b * BLK, BLK), BLK)
@@ -203,7 +251,7 @@
         planar = along_x * along_y
         put_split(lhs, 0, planar * (1.0 - frac[2]))
         put_split(lhs, 32, planar * frac[2])
-        acc[...] += spread_onto(lhs, cells[2])
+        acc[...] += spread_onto(lhs, hot[...])
         return carry
 
     lax.fori_loop(0, NQ // BLK, block, 0)
@@ -219,29 +267,31 @@
             at_row = 32 + k * 16 + c
             up[at_row : at_row + 1, :] = line
             down[at_row : at_row + 1, :] = line
-
-
-def fold_first_body(own, left, right, out):
+            if k < 3:
+                lent[at_row - 32 : at_row - 31, :] = line
+
+
+def fold_first_body(own, left, right, pulls, wanted, out):
     rows = slice(2, 11)
     out[0:9, :] = left[0:16, :][rows]
     out[9:18, :] = (own[0:16, :] + left[16:32, :])[rows]
     out[18:27, :] = own[16:32, :][rows]
     out[27:36, :] = (own[32:48, :] + right[0:16, :])[rows]
     out[36:45, :] = right[16:32, :][rows]
-    out[45:48, :] = jnp.zeros((3, NZ), F32)
+    out[45:48, :] = wanted[0:3, :]
+    out[48:96, :] = pulls[80:128, :]
 
 
 def step_body(
     place,
     state,
     labels,
+    hot,
     depth,
     gathered,
     mine,
     left,
     right,
-    below,
-    above,
     own,
     up,
     down,
@@ -255,7 +305,7 @@
     acc,
     planes,
 ):
-    smooth(place[0], depth, gathered, 5, 9, 0, 16, kept)
+    smooth(place[0], depth, gathered, [(9 * p, 9, 0) for p in range(5)], 16, kept)
     pack[...] = jnp.zeros_like(pack)
     for x in range(3):
         mid = (x + 1) * ROWS
@@ -268,7 +318,15 @@
         pack[64 + x * 9 : 64 + x * 9 + 9, :] = -diff_z(kept[mid : mid + 16, :])[2:11, :]
     put_split(fields, 0, pack[...])
     put_split(fields, 96, next_z(pack[...]))
-    fill_table(table, 80, (mine, right, left, above, below))
+    ahead = lax.rem(place[0] + 1, 8)
+    behind = lax.rem(place[0] + 7, 8)
+
+    def rows_of(device):
+        return lambda row: gathered[device, 48 + row : 64 + row, :]
+
+    fill_table(
+        table, [rows_at(mine, 80), rows_at(right, 80), rows_at(left, 80), rows_of(ahead), rows_of(behind)]
+    )
     acc[...] = jnp.zeros_like(acc)
 
     def block(b, carry):
@@ -280,7 +338,7 @@
         where_to = labels[4:5, at]
         along_x, along_y = weights_of(axis_hits(27, CY + 1, 32, cells[0], cells[1]), frac[0], frac[1])
         planar = along_x * along_y
-        sampled = pick_from(fields, one_hot(cells[2]))
+        sampled = pick_from(fields, hot[...])
         lower = planar * (1.0 - frac[2])
         upper = planar * frac[2]
         force = [
@@ -309,7 +367,7 @@
             scale = None if c == 0 else STEP * home[c - 1]
             put_split(lhs, c * 128, lower if c == 0 else lower * scale)
             put_split(lhs, c * 128 + 64, upper if c == 0 else upper * scale)
-        acc[...] += spread_onto(lhs, cells[2])
+        acc[...] += spread_onto(lhs, hot[...])
         return carry
 
     lax.fori_loop(0, NQ // BLK, block, 0)
@@ -328,45 +386,55 @@
             down[(c * 2 + x) * 16 : (c * 2 + x) * 16 + 16, :] = planes[c, x]
 
 
-def fill_table(table, first, sources):
+def fill_table(table, sources):
     for k in range(3):
         for t, source in enumerate(sources):
-            put_split(table, k * 80 + t * 16, source[first + k * 16 : first + k * 16 + 16, :])
-
-
-def pulls_body(labels, mine, left, right, below, above, pulls, table):
-    fill_table(table, 32, (mine, right, left, above, below))
-
-    def block(b, carry):
-        at = pl.ds(pl.multiple_of(b * BLK, BLK), BLK)
-        home = select_pulls(table, labels[4:5, at], labels[3:4, at])
-        for d in range(3):
-            pulls[d : d + 1, at] = home[d]
-        return carry
-
-    lax.fori_loop(0, NQ // BLK, block, 0)
-
-
-def fold_body(channels, own, left, right, out):
-    rows = out.shape[0] // (channels * 3)
-    spare = out.shape[0] - channels * 3 * rows
-    if spare:
-        out[channels * 3 * rows :, :] = jnp.zeros((spare, NZ), F32)
-    for c in range(channels):
-        mine, theirs, to = c * 48, c * 32, c * 3 * rows
-        first = own[mine : mine + 16, :] + left[theirs : theirs + 16, :]
-        second = (
-            own[mine + 16 : mine + 32, :]
-            + left[theirs + 16 : theirs + 32, :]
-            + right[theirs : theirs + 16, :]
-        )
-        third = own[mine + 32 : mine + 48, :] + right[theirs + 16 : theirs + 32, :]
-        for n, values in enumerate((first, second, third)):
-            out[to + n * rows : to + (n + 1) * rows, :] = values[0:rows]
+            put_split(table, (k * len(sources) + t) * 16, source(k * 16))
+
+
+def rows_at(ref, first):
+    return lambda row: ref[first + row : first + row + 16, :]
+
+
+def pulls_body(place, labels, ranks, mine, left, right, gathered, pulls, table, lists, replied):
+    fill_table(table, [rows_at(mine, 0), rows_at(right, 32), rows_at(left, 32)])
+    moved = labels[3:4, :]
+    home = select_pulls(table, labels[4:5, :], moved)
+    lists[...] = jnp.zeros_like(lists)
+    lists[0:3, :] = gathered[lax.rem(place[0] + 1, 8), REPLIES : REPLIES + 3, :]
+    lists[3:6, :] = gathered[lax.rem(place[0] + 7, 8), REPLIES + 3 : REPLIES + 6, :]
+    put_split(replied, 0, lists[...])
+    taken = pick_from(replied, one_hot(ranks[...]))
+    for d in range(3):
+        from_y = jnp.where(moved == 3, taken[d : d + 1, :], jnp.where(moved == 4, taken[d + 3 : d + 4, :], 0.0))
+        pulls[d : d + 1, :] = home[d] + from_y
+
+
+def fold_planes(own, left, right, channel):
+    mine, theirs = channel * 48, channel * 32
+    first = own[mine : mine + 16, :] + left[theirs : theirs + 16, :]
+    second = (
+        own[mine + 16 : mine + 32, :] + left[theirs + 16 : theirs + 32, :] + right[theirs : theirs + 16, :]
+    )
+    third = own[mine + 32 : mine + 48, :] + right[theirs + 16 : theirs + 32, :]
+    return first, second, third
+
+
+def fold_second_body(own, left, right, replies, out):
+    for c in range(3):
+        for n, values in enumerate(fold_planes(own, left, right, c)):
+            start, rows, first_y = SECOND_SPANS[c * 3 + n]
+            out[start : start + rows, :] = values[first_y + 2 : first_y + 2 + rows]
+    out[REPLIES : REPLIES + 7, :] = replies[0:7, :]
+
+
+def fold_third_body(own, left, right, out):
+    for n, values in enumerate(fold_planes(own, left, right, 0)):
+        out[n * 16 : n * 16 + 16, :] = values
 
 
 def lines_body(place, depth, gathered, own, up, down):
-    smooth(place[0], depth, gathered, 9, 13, -2, 24, own)
+    smooth(place[0], depth, gathered, SECOND_SPANS, 24, own)
     for c in range(2):
         up[c * 32 : c * 32 + 32, :] = own[c * 48 : c * 48 + 32, :]
         down[c * 32 : c * 32 + 32, :] = own[c * 48 + 16 : c * 48 + 48, :]
@@ -375,7 +443,7 @@
 
 
 def back_body(
-    state, labels, drift, pulls, pulls_pos, mine, left, right, own, up, down, grads, wide, pack, fields, lhs, acc, planes
+    state, labels, hot, drift, pulls, pulls_pos, mine, left, right, own, up, down, grads, wide, pack, fields, lhs, acc, planes
 ):
     for c in range(2):
         wide[c, 0:32, :] = left[c * 32 : c * 32 + 32, :]
@@ -413,7 +481,7 @@
         hits = axis_hits(55, CY + 3, 64, cells[0] + to_x + 1, cells[1] + to_y + 1)
         along_x, along_y = weights_of(hits, second[0], second[1])
         slope_x, slope_y = slopes_of(hits)
-        sampled = pick_from(fields, one_hot(cells[2]))
+        sampled = pick_from(fields, hot[...])
         sides = []
         for s in range(2):
             mixed = sampled[s * 256 + 192 : s * 256 + 256, :]
@@ -441,7 +509,7 @@
             scale = STEP * grad_kick[c]
             put_split(lhs, c * 64, below * scale)
             put_split(lhs, c * 64 + 32, above * scale)
-        acc[...] += spread_onto(lhs, cells[2])
+        acc[...] += spread_onto(lhs, hot[...])
         return carry
 
     lax.fori_loop(0, NQ // BLK, block, 0)
@@ -462,46 +530,51 @@
             down[x * 16 : (x + 1) * 16, :] = spread
 
 
-def last_body(place, state, labels, depth, grads, fields, gathered, grad_pos, grad_mom, kept, pack, own_field):
-    smooth(place[0], depth, gathered, 3, 16, -2, 16, kept)
+def mix_slopes(hits, frac, sides):
+    along_x, along_y = weights_of(hits, frac[0], frac[1])
+    slope_x, slope_y = slopes_of(hits)
+    rise = sides[1] - sides[0]
+    level = sides[0] + frac[2] * rise
+    return [
+        jnp.sum(slope_x * (along_y * level), axis=0, keepdims=True),
+        jnp.sum(slope_y * (along_x * level), axis=0, keepdims=True),
+        jnp.sum(along_x * (along_y * rise), axis=0, keepdims=True),
+    ]
+
+
+def push_body(state, labels, hot, grads, fields, out):
+    frac = row3(state, slice(None))
+    cells = row3(labels, slice(None))
+    grad_kick = row3(grads, slice(None), 3)
+    sampled = pick_from(fields, hot[...])
+    sides = []
+    for s in range(2):
+        mixed = (STEP * grad_kick[0]) * sampled[s * 96 : s * 96 + 32, :]
+        for d in range(1, 3):
+            mixed = mixed + (STEP * grad_kick[d]) * sampled[s * 96 + d * 32 : s * 96 + d * 32 + 32, :]
+        sides.append(mixed)
+    slopes = mix_slopes(axis_hits(27, CY + 1, 32, cells[0], cells[1]), frac, sides)
+    for d in range(3):
+        out[d : d + 1, :] = grads[d : d + 1, :] + slopes[d]
+
+
+def last_body(place, state, labels, hot, depth, grads, partial, gathered, grad_pos, grad_mom, kept, pack, own_field):
+    smooth(place[0], depth, gathered, [(16 * p, 16, -2) for p in range(3)], 16, kept)
     pack[...] = jnp.zeros_like(pack)
     for x in range(3):
         pack[x * 9 : x * 9 + 9, :] = kept[x * 16 + 2 : x * 16 + 11, :]
     put_split(own_field, 0, pack[...])
     put_split(own_field, 32, next_z(pack[...]))
-
-    def block(b, carry):
-        at = pl.ds(pl.multiple_of(b * BLK, BLK), BLK)
-        frac = row3(state, at)
-        cells = row3(labels, at)
-        hot = one_hot(cells[2])
-        hits = axis_hits(27, CY + 1, 32, cells[0], cells[1])
-        along_x, along_y = weights_of(hits, frac[0], frac[1])
-        slope_x, slope_y = slopes_of(hits)
-        grad_drift = row3(grads, at)
-        grad_kick = row3(grads, at, 3)
-        sampled = pick_from(fields, hot)
-        pulled = pick_from(own_field, hot)
-        sides = []
-        for s in range(2):
-            mixed = pulled[s * 32 : s * 32 + 32, :]
-            for d in range(3):
-                mixed = mixed + (STEP * grad_kick[d]) * sampled[s * 96 + d * 32 : s * 96 + d * 32 + 32, :]
-            sides.append(mixed)
-        level = sides[0] + frac[2] * (sides[1] - sides[0])
-        rise = sides[1] - sides[0]
-        slopes = [
-            jnp.sum(slope_x * (along_y * level), axis=0, keepdims=True),
-            jnp.sum(slope_y * (along_x * level), axis=0, keepdims=True),
-            jnp.sum(along_x * (along_y * rise), axis=0, keepdims=True),
-        ]
-        for d in range(3):
-            total = grad_drift[d] + slopes[d]
-            grad_pos[d : d + 1, at] = total
-            grad_mom[d : d + 1, at] = grad_kick[d] + STEP * total
-        return carry
-
-    lax.fori_loop(0, NQ // BLK, block, 0)
+    frac = row3(state, slice(None))
+    cells = row3(labels, slice(None))
+    sampled = pick_from(own_field, hot[...])
+    slopes = mix_slopes(
+        axis_hits(27, CY + 1, 32, cells[0], cells[1]), frac, [sampled[0:32, :], sampled[32:64, :]]
+    )
+    for d in range(3):
+        total = partial[d : d + 1, :] + slopes[d]
+        grad_pos[d : d + 1, :] = total
+        grad_mom[d : d + 1, :] = grads[d + 3 : d + 4, :] + STEP * total
 
 
 def swap(up, down, axis):
@@ -541,14 +614,16 @@
         pltpu.with_memory_space_constraint(x, pltpu.HBM)
         for x in (pos, mom, cell, dest, slot, pull_pos, pull_mom)
     ]
-    own, up, down, state, labels = pl.pallas_call(
+    own, up, down, lent, state, labels, hot = pl.pallas_call(
         deposit_first_body,
         out_shape=(
             shape(48, NZ),
             shape(128, NZ),
             shape(128, NZ),
+            shape(48, NZ),
             shape(6, NQ),
             shape(5, NQ, dtype=jnp.int32),
+            shape(NZ, NQ, dtype=BF16),
         ),
         in_specs=[pl.BlockSpec(memory_space=pltpu.HBM)] * 7,
         scratch_shapes=[
@@ -562,9 +637,14 @@
         compiler_params=pltpu.CompilerParams(vmem_limit_bytes=VMEM_LIMIT),
     )(*in_hbm)
     mine, (left, right) = up, swap(up, down, "gx")
-    below, above = swap(up, up, "gy")
     first_left, first_right = left, right
-    gathered = gather_y(call(fold_first_body, shape(48, NZ))(own, left, right))
+    wanted, ranks = call(
+        requests_body,
+        (shape(8, NZ), shape(1, NQ, dtype=jnp.int32)),
+        [pltpu.VMEM((32, NZ), F32), pltpu.VMEM((16, NQ), F32)],
+    )(labels)
+    gathered = gather_y(call(fold_first_body, shape(96, NZ))(own, left, right, up, wanted))
+    replies = call_at(replies_body, shape(8, NZ), [pltpu.VMEM((96, NZ), BF16)], 2)(place, gathered, lent)
     own, up, down, drift, pulls, fields = call_at(
         step_body,
         (
@@ -583,17 +663,20 @@
             pltpu.VMEM((512, NZ), F32),
             pltpu.VMEM((4, 5, ROWS, NZ), F32),
         ],
-        9,
-    )(place, state, labels, depth, gathered, mine, left, right, below, above)
+        8,
+    )(place, state, labels, hot, depth, gathered, mine, left, right)
     left, right = swap(up, down, "gx")
-    gathered = gather_y(call(functools.partial(fold_body, 3), shape(120, NZ))(own, left, right))
+    gathered = gather_y(call(fold_second_body, shape(112, NZ))(own, left, right, replies))
     own, up, down = call_at(lines_body, (shape(144, NZ), shape(80, NZ), shape(80, NZ)), [], 2)(
         place, depth, gathered
     )
     left, right = swap(up, down, "gx")
-    pulls_pos = call(pulls_body, shape(3, NQ), [pltpu.VMEM((480, NZ), BF16)])(
-        labels, mine, first_left, first_right, below, above
-    )
+    pulls_pos = call_at(
+        pulls_body,
+        shape(3, NQ),
+        [pltpu.VMEM((288, NZ), BF16), pltpu.VMEM((16, NZ), F32), pltpu.VMEM((32, NZ), BF16)],
+        6,
+    )(place, labels, ranks, lent, first_left, first_right, gathered)
     own, up, down, grads = call(
         back_body,
         (shape(48, NZ), shape(32, NZ), shape(32, NZ), shape(6, NQ)),
@@ -605,15 +688,16 @@
             pltpu.VMEM((192, NZ), F32),
             pltpu.VMEM((3, 7, ROWS, NZ), F32),
         ],
-    )(state, labels, drift, pulls, pulls_pos, own, left, right)
+    )(state, labels, hot, drift, pulls, pulls_pos, own, left, right)
     left, right = swap(up, down, "gx")
-    gathered = gather_y(call(functools.partial(fold_body, 1), shape(48, NZ))(own, left, right))
+    gathered = gather_y(call(fold_third_body, shape(48, NZ))(own, left, right))
+    partial = call(push_body, shape(3, NQ))(state, labels, hot, grads, fields)
     return call_at(
         last_body,
         (shape(3, NQ), shape(3, NQ)),
         [pltpu.VMEM((48, NZ), F32), pltpu.VMEM((32, NZ), F32), pltpu.VMEM((128, NZ), BF16)],
-        6,
-    )(place, state, labels, depth, grads, fields, gathered)
+        7,
+    )(place, state, labels, hot, depth, grads, partial, gathered)
 
 
 def solution(mesh):

time: 128 us -> 122 us (0.953); the launches traced: 126 us -> 121 us
  starting transfers between devices: 50.7 us -> 42 us
  blocking collectives: 54 us -> 56.9 us
  Pallas kernels: 17.5 us -> 19.1 us
    ppermute x10 -> x8, starting transfers between devices: 50.7 us -> 42 us  [swap(): return (lax.ppermute(up, axis, forward), lax.ppermute(down, axis, backward))]
    all_gather x3, blocking collectives: 54 us -> 56.9 us  [gather_y(): return lax.all_gather(x, 'gy', axis=0, tiled=False)]
    pallas_call x4 -> x7, Pallas kernels: 1.35 us -> 4.04 us  [the longest x1 1.78 us: local(): call_at(pulls_body, shape(3, NQ), [pltpu.VMEM((288, NZ), BF16), pltpu.VME...]
    ppermute x10 -> x8, waiting for transfers between devices: 2.79 us -> 2.68 us  [swap(): return (lax.ppermute(up, axis, forward), lax.ppermute(down, axis, backward))]
  transfers between devices with their start and end apart: 10 -> 8, of which waited for: 4 -> 3; matrix products, arithmetic and copies ran while one was open for 0% -> 0% of each run, Pallas kernels for 1% -> 3%
where the time goes in v4:
time: 122 us; the launch traced here: 121 us
  blocking collectives  56.9 us (47%)
  starting transfers between devices  42 us (34%)
  Pallas kernels  19.1 us (16%)
  waiting for transfers between devices  2.68 us (2%)
    all_gather x3, blocking collectives, gather_y(): return lax.all_gather(x, 'gy', axis=0, tiled=False)  56.9 us
    ppermute x8, starting transfers between devices, swap(): return (lax.ppermute(up, axis, forward), lax.ppermute(down, axis, backward))  42 us
    pallas_call x1, Pallas kernels, local(): call_at(step_body, (shape(144, NZ), shape(96, NZ), shape(96, NZ), shape(3...  5.54 us
    pallas_call x1, Pallas kernels, local(): call(back_body, (shape(48, NZ), shape(32, NZ), shape(32, NZ), shape(6, NQ...  4.29 us
    ppermute x8, waiting for transfers between devices, swap(): return (lax.ppermute(up, axis, forward), lax.ppermute(down, axis, backward))  2.68 us
    pallas_call x1, Pallas kernels, local(): pl.pallas_call(deposit_first_body, out_shape=(shape(48, NZ), shape(128, N...  2.44 us
  transfers between devices with their start and end apart: 8, of which 3 were waited for; matrix products, arithmetic and copies ran while one was open for 0% of the time, Pallas kernels for 3%

profile of v4, /device:TPU:1, one launch (start us, length us, event | category | flops | bytes accessed | tf_op | source)
XLA Modules:
  0.0 121.5 jit_solution(4991271006431819879)
XLA Ops:
  0.6 2.4 %shard_map.86 = (f32[48,256]{1,0:T(8,128)S(1)}, f32[128,256]{1,0:T(8,128)S(1)}, f32[128,256]{1,0:T(8,128)S(1)}, f32[48,256]{1,0:T(8,128)S(1)}, f32[6,4096]{1,0:T...) custom-call(f32[3,4096]{1,0:T(4,128)} %pos.1, f32[3,4096]{1,0:T(4,128)} %mom.1, s32[3,4096]{1,0:T(4,128)} %cell.1, ...), custom_call_target="tpu_custom_call" | custom-call | tf_op jit(solution)/shard_map/pallas_call | solution.py:617
  3.1 4.0 %collective-permute-start = (f32[128,256]{1,0:T(8,128)S(1)}, f32[128,256]{1,0:T(8,128)S(1)}, u32[]{:S(2)}, u32[]{:S(2)}) collective-permute-start(f32[128,256]{1,0:T(8,128)S(1)} %get-tuple-element.28.pulls.mine), channel_id=1, source_target_pairs={{0,8},{8,16},{16,24},{24,32},{32,40},{40,48},{48,56},{56,64},{64,7... | collective-permute-start | bytes 393224 | tf_op jit(solution)/shard_map/ppermute | solution.py:584
  7.1 7.8 %collective-permute-start.1 = (f32[128,256]{1,0:T(8,128)S(1)}, f32[128,256]{1,0:T(8,128)S(1)}, u32[]{:S(2)}, u32[]{:S(2)}) collective-permute-start(f32[128,256]{1,0:T(8,128)S(1)} %get-tuple-element.29), channel_id=1, source_target_pairs={{8,0},{16,8},{24,16},{32,24},{40,32},{48,40},{56,48},{64,56},{72,6... | collective-permute-start | bytes 393224 | tf_op jit(solution)/shard_map/ppermute | solution.py:584
  15.0 0.9 shard_map.88
  15.9 0.1 shard_map.87.depth
  16.0 0.0 collective-permute-done.left
  16.0 0.9 collective-permute-done.1.right
  16.9 22.5 %all-gather = f32[768,256]{1,0:T(8,128)S(1)} all-gather(f32[96,256]{1,0:T(8,128)S(1)} %shard_map.89), channel_id=2, replica_groups=mesh['gx'=64,'gy'=8] {'gy'}, dimensions={0}, use_global_device_ids=true | all-gather | bytes 884736 | tf_op jit(solution)/shard_map/all_gather | solution.py:588
  39.4 5.5 %shard_map.90 = (f32[144,256]{1,0:T(8,128)S(1)}, f32[96,256]{1,0:T(8,128)S(1)}, f32[96,256]{1,0:T(8,128)S(1)}, f32[3,4096]{1,0:T(4,128)S(1)}, f32[3,4096]{1,0:T(4,128)S(1)}, /*index=5*/bf16[384,256]{1,0:T(8,128)(2,1)S(1)}) custom-call(s32[1]{0:T(128)} %bitcast.place, f32[6,4096]{1,0:T(8,128)S(1)} %get-tuple-element.24.state, ...), custom_call_target="tpu_custom_call" | custom-call | tf_op jit(solution)/shard_map/pallas_call | solution.py:648
  45.0 1.9 %collective-permute-start.2 = (f32[96,256]{1,0:T(8,128)S(1)}, f32[96,256]{1,0:T(8,128)S(1)}, u32[]{:S(2)}, u32[]{:S(2)}) collective-permute-start(f32[96,256]{1,0:T(8,128)S(1)} %get-tuple-element.36), channel_id=1, source_target_pairs={{0,8},{8,16},{16,24},{24,32},{32,40},{40,48},{48,56},{56,64},{64,7... | collective-permute-start | bytes 294920 | tf_op jit(solution)/shard_map/ppermute | solution.py:584
  46.9 8.1 %collective-permute-start.3 = (f32[96,256]{1,0:T(8,128)S(1)}, f32[96,256]{1,0:T(8,128)S(1)}, u32[]{:S(2)}, u32[]{:S(2)}) collective-permute-start(f32[96,256]{1,0:T(8,128)S(1)} %get-tuple-element.37), channel_id=1, source_target_pairs={{8,0},{16,8},{24,16},{32,24},{40,32},{48,40},{56,48},{64,56},{72,6... | collective-permute-start | bytes 294920 | tf_op jit(solution)/shard_map/ppermute | solution.py:584
  55.0 0.2 shard_map.91.replies
  55.2 0.9 collective-permute-done.2.left
  56.2 0.9 collective-permute-done.3.right
  57.1 17.2 %all-gather.1 = f32[896,256]{1,0:T(8,128)S(1)} all-gather(f32[112,256]{1,0:T(8,128)S(1)} %shard_map.92), channel_id=3, replica_groups=mesh['gx'=64,'gy'=8] {'gy'}, dimensions={0}, use_global_device_ids=true | all-gather | bytes 1032192 | tf_op jit(solution)/shard_map/all_gather | solution.py:588
  74.3 0.8 shard_map.94
  75.1 1.9 %collective-permute-start.4 = (f32[80,256]{1,0:T(8,128)S(1)}, f32[80,256]{1,0:T(8,128)S(1)}, u32[]{:S(2)}, u32[]{:S(2)}) collective-permute-start(f32[80,256]{1,0:T(8,128)S(1)} %get-tuple-element.39), channel_id=1, source_target_pairs={{0,8},{8,16},{16,24},{24,32},{32,40},{40,48},{48,56},{56,64},{64,7... | collective-permute-start | bytes 245768 | tf_op jit(solution)/shard_map/ppermute | solution.py:584
  77.0 8.2 %collective-permute-start.5 = (f32[80,256]{1,0:T(8,128)S(1)}, f32[80,256]{1,0:T(8,128)S(1)}, u32[]{:S(2)}, u32[]{:S(2)}) collective-permute-start(f32[80,256]{1,0:T(8,128)S(1)} %get-tuple-element.40), channel_id=1, source_target_pairs={{8,0},{16,8},{24,16},{32,24},{40,32},{48,40},{56,48},{64,56},{72,6... | collective-permute-start | bytes 245768 | tf_op jit(solution)/shard_map/ppermute | solution.py:584
  85.3 1.8 %shard_map.93.pulls_pos = f32[3,4096]{1,0:T(4,128)S(1)} custom-call(s32[1]{0:T(128)} %bitcast.place, s32[5,4096]{1,0:T(8,128)S(1)} %get-tuple-element.25.labels, s32[1,4096]{1,0:T(1,128)S(1)} %get-tuple-element.33.ranks, f32[48,256]{1,0:T(8,128)S(1)} %get-tuple-element.34.lent.mine, f32[128,256]{1,0:T(8,128)S(1)} %collective-permute-done.left, ...), custom_call_target="tpu_custom_call" | custom-call | tf_op jit(solution)/shard_map/pallas_call | solution.py:674
  87.0 0.0 collective-permute-done.4.left
  87.1 0.0 collective-permute-done.5.right
  87.1 4.3 %shard_map.95 = (f32[48,256]{1,0:T(8,128)S(1)}, f32[32,256]{1,0:T(8,128)S(1)}, f32[32,256]{1,0:T(8,128)S(1)}, f32[6,4096]{1,0:T(8,128)S(1)}) custom-call(f32[6,4096]{1,0:T(8,128)S(1)} %get-tuple-element.24.state, s32[5,4096]{1,0:T(8,128)S(1)} %get-tuple-element.25.labels, bf16[256,4096]{1,0:T(8,128)(2,1)S(1)} %get-tuple-element.26.hot, ...), custom_call_target="tpu_custom_call" | custom-call | tf_op jit(solution)/shard_map/pallas_call | solution.py:680
  91.4 1.9 %collective-permute-start.6 = (f32[32,256]{1,0:T(8,128)S(1)}, f32[32,256]{1,0:T(8,128)S(1)}, u32[]{:S(2)}, u32[]{:S(2)}) collective-permute-start(f32[32,256]{1,0:T(8,128)S(1)} %get-tuple-element.44), channel_id=1, source_target_pairs={{0,8},{8,16},{16,24},{24,32},{32,40},{40,48},{48,56},{56,64},{64,7... | collective-permute-start | bytes 98312 | tf_op jit(solution)/shard_map/ppermute | solution.py:584
  93.3 8.0 %collective-permute-start.7 = (f32[32,256]{1,0:T(8,128)S(1)}, f32[32,256]{1,0:T(8,128)S(1)}, u32[]{:S(2)}, u32[]{:S(2)}) collective-permute-start(f32[32,256]{1,0:T(8,128)S(1)} %get-tuple-element.45), channel_id=1, source_target_pairs={{8,0},{16,8},{24,16},{32,24},{40,32},{48,40},{56,48},{64,56},{72,6... | collective-permute-start | bytes 98312 | tf_op jit(solution)/shard_map/ppermute | solution.py:584
  101.3 1.1 shard_map.96.partial
  102.4 0.0 collective-permute-done.6.left
  102.4 0.0 collective-permute-done.7.right
  102.5 17.1 %all-gather.2 = f32[384,256]{1,0:T(8,128)S(1)} all-gather(f32[48,256]{1,0:T(8,128)S(1)} %shard_map.97), channel_id=4, replica_groups=mesh['gx'=64,'gy'=8] {'gy'}, dimensions={0}, use_global_device_ids=true | all-gather | bytes 442368 | tf_op jit(solution)/shard_map/all_gather | solution.py:588
  119.6 1.9 %shard_map.98 = (f32[3,4096]{1,0:T(4,128)}, f32[3,4096]{1,0:T(4,128)}) custom-call(s32[1]{0:T(128)} %bitcast.place, f32[6,4096]{1,0:T(8,128)S(1)} %get-tuple-element.24.state, s32[5,4096]{1,0:T(8,128)S(1)} %get-tuple-element.25.labels, bf16[256,4096]{1,0:T(8,128)(2,1)S(1)} %get-tuple-element.26.hot, bf16[512,256]{1,0:T(8,128)(2,1)S(1)} %shard_map.87.depth, ...), custom_call_target="tpu_custom_call" | custom-call | tf_op jit(solution)/shard_map/pallas_call | solution.py:695
  (3 shorter events, 0.1 us)
Async XLA Ops:
  3.1 12.9 %collective-permute-start = (f32[128,256]{1,0:T(8,128)S(1)}, f32[128,256]{1,0:T(8,128)S(1)}, u32[]{:S(2)}, u32[]{:S(2)}) collective-permute-start(f32[128,256]{1,0:T(8,128)S(1)} %get-tuple-element.28.pulls.mine), channel_id=1, source_target_pairs={{0,8},{8,16},{16,24},{24,32},{32,40},{40,48},{48,56},{56,64},{64,7... | collective-permute-start | bytes 393224 | tf_op jit(solution)/shard_map/ppermute | solution.py:584
  7.1 9.8 %collective-permute-start.1 = (f32[128,256]{1,0:T(8,128)S(1)}, f32[128,256]{1,0:T(8,128)S(1)}, u32[]{:S(2)}, u32[]{:S(2)}) collective-permute-start(f32[128,256]{1,0:T(8,128)S(1)} %get-tuple-element.29), channel_id=1, source_target_pairs={{8,0},{16,8},{24,16},{32,24},{40,32},{48,40},{56,48},{64,56},{72,6... | collective-permute-start | bytes 393224 | tf_op jit(solution)/shard_map/ppermute | solution.py:584
  45.0 11.2 %collective-permute-start.2 = (f32[96,256]{1,0:T(8,128)S(1)}, f32[96,256]{1,0:T(8,128)S(1)}, u32[]{:S(2)}, u32[]{:S(2)}) collective-permute-start(f32[96,256]{1,0:T(8,128)S(1)} %get-tuple-element.36), channel_id=1, source_target_pairs={{0,8},{8,16},{16,24},{24,32},{32,40},{40,48},{48,56},{56,64},{64,7... | collective-permute-start | bytes 294920 | tf_op jit(solution)/shard_map/ppermute | solution.py:584
  46.9 10.1 %collective-permute-start.3 = (f32[96,256]{1,0:T(8,128)S(1)}, f32[96,256]{1,0:T(8,128)S(1)}, u32[]{:S(2)}, u32[]{:S(2)}) collective-permute-start(f32[96,256]{1,0:T(8,128)S(1)} %get-tuple-element.37), channel_id=1, source_target_pairs={{8,0},{16,8},{24,16},{32,24},{40,32},{48,40},{56,48},{64,56},{72,6... | collective-permute-start | bytes 294920 | tf_op jit(solution)/shard_map/ppermute | solution.py:584
  75.1 12.0 %collective-permute-start.4 = (f32[80,256]{1,0:T(8,128)S(1)}, f32[80,256]{1,0:T(8,128)S(1)}, u32[]{:S(2)}, u32[]{:S(2)}) collective-permute-start(f32[80,256]{1,0:T(8,128)S(1)} %get-tuple-element.39), channel_id=1, source_target_pairs={{0,8},{8,16},{16,24},{24,32},{32,40},{40,48},{48,56},{56,64},{64,7... | collective-permute-start | bytes 245768 | tf_op jit(solution)/shard_map/ppermute | solution.py:584
  77.0 10.1 %collective-permute-start.5 = (f32[80,256]{1,0:T(8,128)S(1)}, f32[80,256]{1,0:T(8,128)S(1)}, u32[]{:S(2)}, u32[]{:S(2)}) collective-permute-start(f32[80,256]{1,0:T(8,128)S(1)} %get-tuple-element.40), channel_id=1, source_target_pairs={{8,0},{16,8},{24,16},{32,24},{40,32},{48,40},{56,48},{64,56},{72,6... | collective-permute-start | bytes 245768 | tf_op jit(solution)/shard_map/ppermute | solution.py:584
  91.4 11.1 %collective-permute-start.6 = (f32[32,256]{1,0:T(8,128)S(1)}, f32[32,256]{1,0:T(8,128)S(1)}, u32[]{:S(2)}, u32[]{:S(2)}) collective-permute-start(f32[32,256]{1,0:T(8,128)S(1)} %get-tuple-element.44), channel_id=1, source_target_pairs={{0,8},{8,16},{16,24},{24,32},{32,40},{40,48},{48,56},{56,64},{64,7... | collective-permute-start | bytes 98312 | tf_op jit(solution)/shard_map/ppermute | solution.py:584
  93.3 9.1 %collective-permute-start.7 = (f32[32,256]{1,0:T(8,128)S(1)}, f32[32,256]{1,0:T(8,128)S(1)}, u32[]{:S(2)}, u32[]{:S(2)}) collective-permute-start(f32[32,256]{1,0:T(8,128)S(1)} %get-tuple-element.45), channel_id=1, source_target_pairs={{8,0},{16,8},{24,16},{32,24},{40,32},{48,40},{56,48},{64,56},{72,6... | collective-permute-start | bytes 98312 | tf_op jit(solution)/shard_map/ppermute | solution.py:584

commit v5 on v4

--- a/solution.py
+++ b/solution.py
@@ -577,11 +577,45 @@
         grad_mom[d : d + 1, :] = grads[d + 3 : d + 4, :] + STEP * total
 
 
-def swap(up, down, axis):
-    peers = lax.axis_size(axis)
-    forward = [(i, (i + 1) % peers) for i in range(peers)]
-    backward = [((i + 1) % peers, i) for i in range(peers)]
-    return lax.ppermute(up, axis, forward), lax.ppermute(down, axis, backward)
+def trade_x(first, second):
+    peers = lax.axis_size("gx")
+    inner = [(i, i ^ 1) for i in range(peers)]
+    outer = [(i, (i + 1 if i % 2 else i - 1) % peers) for i in range(peers)]
+    return lax.ppermute(first, "gx", inner), lax.ppermute(second, "gx", outer)
+
+
+def put_pair(odd, ones, others):
+    for flag in range(2):
+
+        @pl.when(odd == flag)
+        def _():
+            ones[0][...] = others[flag][...]
+            ones[1][...] = others[1 - flag][...]
+
+
+def sided(body, placed, arrived=None, sent=None):
+    def wrapped(place, *refs):
+        refs = list(refs)
+        odd = lax.shift_right_logical(place[0], 3) & 1
+        if sent is not None:
+            pair = refs[sent : sent + 2]
+            made = refs[-2:]
+            refs = refs[:-2]
+            refs[sent : sent + 2] = made
+        if arrived is not None:
+            came = refs[arrived : arrived + 2]
+            sides = refs[-2:]
+            refs = refs[:-2]
+            put_pair(odd, (sides[1], sides[0]), came)
+            refs[arrived : arrived + 2] = sides
+        if placed:
+            body(place, *refs)
+        else:
+            body(*refs)
+        if sent is not None:
+            put_pair(odd, pair, made)
+
+    return wrapped
 
 
 def gather_y(x):
@@ -589,7 +623,7 @@
 
 
 def local(pos, mom, cell, cell_second, dest, slot, pull_pos, pull_mom):
-    place = lax.axis_index("gy").astype(jnp.int32).reshape(1)
+    place = lax.axis_index(("gx", "gy")).astype(jnp.int32).reshape(1)
     dest = dest.reshape(1, NQ)
     slot = slot.reshape(1, NQ)
     scalar = pl.BlockSpec(memory_space=pltpu.SMEM)
@@ -615,7 +649,7 @@
         for x in (pos, mom, cell, dest, slot, pull_pos, pull_mom)
     ]
     own, up, down, lent, state, labels, hot = pl.pallas_call(
-        deposit_first_body,
+        sided(deposit_first_body, False, sent=8),
         out_shape=(
             shape(48, NZ),
             shape(128, NZ),
@@ -625,7 +659,7 @@
             shape(5, NQ, dtype=jnp.int32),
             shape(NZ, NQ, dtype=BF16),
         ),
-        in_specs=[pl.BlockSpec(memory_space=pltpu.HBM)] * 7,
+        in_specs=[scalar] + [pl.BlockSpec(memory_space=pltpu.HBM)] * 7,
         scratch_shapes=[
             pltpu.VMEM((4, 3, NQ), F32),
             pltpu.VMEM((3, NQ), jnp.int32),
@@ -633,20 +667,24 @@
             pltpu.SemaphoreType.DMA((7,)),
             pltpu.VMEM((128, BLK), BF16),
             pltpu.VMEM((64, NZ), F32),
+            pltpu.VMEM((128, NZ), F32),
+            pltpu.VMEM((128, NZ), F32),
         ],
         compiler_params=pltpu.CompilerParams(vmem_limit_bytes=VMEM_LIMIT),
-    )(*in_hbm)
-    mine, (left, right) = up, swap(up, down, "gx")
+    )(place, *in_hbm)
+    mine, (left, right) = up, trade_x(up, down)
     first_left, first_right = left, right
     wanted, ranks = call(
         requests_body,
         (shape(8, NZ), shape(1, NQ, dtype=jnp.int32)),
         [pltpu.VMEM((32, NZ), F32), pltpu.VMEM((16, NQ), F32)],
     )(labels)
-    gathered = gather_y(call(fold_first_body, shape(96, NZ))(own, left, right, up, wanted))
+    gathered = gather_y(call_at(
+            sided(fold_first_body, False, arrived=1), shape(96, NZ), [pltpu.VMEM((128, NZ), F32)] * 2, 5
+        )(place, own, left, right, up, wanted))
     replies = call_at(replies_body, shape(8, NZ), [pltpu.VMEM((96, NZ), BF16)], 2)(place, gathered, lent)
     own, up, down, drift, pulls, fields = call_at(
-        step_body,
+        sided(step_body, True, arrived=6, sent=9),
         (
             shape(144, NZ),
             shape(96, NZ),
@@ -662,23 +700,33 @@
             pltpu.VMEM((1024, BLK), BF16),
             pltpu.VMEM((512, NZ), F32),
             pltpu.VMEM((4, 5, ROWS, NZ), F32),
-        ],
+        ]
+        + [pltpu.VMEM((128, NZ), F32)] * 2
+        + [pltpu.VMEM((96, NZ), F32)] * 2,
         8,
     )(place, state, labels, hot, depth, gathered, mine, left, right)
-    left, right = swap(up, down, "gx")
-    gathered = gather_y(call(fold_second_body, shape(112, NZ))(own, left, right, replies))
-    own, up, down = call_at(lines_body, (shape(144, NZ), shape(80, NZ), shape(80, NZ)), [], 2)(
+    left, right = trade_x(up, down)
+    gathered = gather_y(call_at(
+            sided(fold_second_body, False, arrived=1), shape(112, NZ), [pltpu.VMEM((96, NZ), F32)] * 2, 4
+        )(place, own, left, right, replies))
+    own, up, down = call_at(
+        sided(lines_body, True, sent=3),
+        (shape(144, NZ), shape(80, NZ), shape(80, NZ)),
+        [pltpu.VMEM((80, NZ), F32)] * 2,
+        2,
+    )(
         place, depth, gathered
     )
-    left, right = swap(up, down, "gx")
+    left, right = trade_x(up, down)
     pulls_pos = call_at(
-        pulls_body,
+        sided(pulls_body, True, arrived=3),
         shape(3, NQ),
-        [pltpu.VMEM((288, NZ), BF16), pltpu.VMEM((16, NZ), F32), pltpu.VMEM((32, NZ), BF16)],
+        [pltpu.VMEM((288, NZ), BF16), pltpu.VMEM((16, NZ), F32), pltpu.VMEM((32, NZ), BF16)]
+        + [pltpu.VMEM((128, NZ), F32)] * 2,
         6,
     )(place, labels, ranks, lent, first_left, first_right, gathered)
-    own, up, down, grads = call(
-        back_body,
+    own, up, down, grads = call_at(
+        sided(back_body, False, arrived=7, sent=10),
         (shape(48, NZ), shape(32, NZ), shape(32, NZ), shape(6, NQ)),
         [
             pltpu.VMEM((3, 112, NZ), F32),
@@ -687,10 +735,15 @@
             pltpu.VMEM((384, BLK), BF16),
             pltpu.VMEM((192, NZ), F32),
             pltpu.VMEM((3, 7, ROWS, NZ), F32),
-        ],
-    )(state, labels, hot, drift, pulls, pulls_pos, own, left, right)
-    left, right = swap(up, down, "gx")
-    gathered = gather_y(call(fold_third_body, shape(48, NZ))(own, left, right))
+        ]
+        + [pltpu.VMEM((80, NZ), F32)] * 2
+        + [pltpu.VMEM((32, NZ), F32)] * 2,
+        9,
+    )(place, state, labels, hot, drift, pulls, pulls_pos, own, left, right)
+    left, right = trade_x(up, down)
+    gathered = gather_y(call_at(
+            sided(fold_third_body, False, arrived=1), shape(48, NZ), [pltpu.VMEM((32, NZ), F32)] * 2, 3
+        )(place, own, left, right))
     partial = call(push_body, shape(3, NQ))(state, labels, hot, grads, fields)
     return call_at(
         last_body,

time: 122 us -> 126 us (1.033)
  waiting for transfers between devices: 2.68 us -> 5.38 us
    ppermute x8, waiting for transfers between devices: 2.68 us -> 5.38 us  [trade_x(): return (lax.ppermute(first, 'gx', inner), lax.ppermute(second, 'gx', outer))]
  transfers between devices with their start and end apart: 8 -> 8, of which waited for: 3 -> 4; matrix products, arithmetic and copies ran while one was open for 0% -> 0% of each run, Pallas kernels for 3% -> 3%
where the time goes in v5:
time: 126 us; the launch traced here: 125 us
  blocking collectives  56.5 us (45%)
  starting transfers between devices  43.2 us (34%)
  Pallas kernels  19.5 us (15%)
  waiting for transfers between devices  5.38 us (4%)
    all_gather x3, blocking collectives, gather_y(): return lax.all_gather(x, 'gy', axis=0, tiled=False)  56.5 us
    ppermute x8, starting transfers between devices, trade_x(): return (lax.ppermute(first, 'gx', inner), lax.ppermute(second, 'gx', outer))  43.2 us
    pallas_call x1, Pallas kernels, local(): call_at(sided(step_body, True, arrived=6, sent=9), (shape(144, NZ), shape...  5.6 us
    ppermute x8, waiting for transfers between devices, trade_x(): return (lax.ppermute(first, 'gx', inner), lax.ppermute(second, 'gx', outer))  5.38 us
    pallas_call x1, Pallas kernels, local(): call_at(sided(back_body, False, arrived=7, sent=10), (shape(48, NZ), shap...  4.55 us
  transfers between devices with their start and end apart: 8, of which 4 were waited for; matrix products, arithmetic and copies ran while one was open for 0% of the time, Pallas kernels for 3%

profile of v5, /device:TPU:1, one launch (start us, length us, event | category | flops | bytes accessed | tf_op | source)
XLA Modules:
  0.0 125.3 jit_solution(1072919907897059270)
XLA Ops:
  0.6 2.5 %shard_map.86 = (f32[48,256]{1,0:T(8,128)S(1)}, f32[128,256]{1,0:T(8,128)S(1)}, f32[128,256]{1,0:T(8,128)S(1)}, f32[48,256]{1,0:T(8,128)S(1)}, f32[6,4096]{1,0:T...) custom-call(s32[1]{0:T(128)} %bitcast.place, f32[3,4096]{1,0:T(4,128)} %refs_0_.1, f32[3,4096]{1,0:T(4,128)} %refs_1_.1, ...), custom_call_target="tpu_custom_call" | custom-call | tf_op jit(solution)/shard_map/pallas_call | solution.py:651
  3.1 4.0 %collective-permute-start = (f32[128,256]{1,0:T(8,128)S(1)}, f32[128,256]{1,0:T(8,128)S(1)}, u32[]{:S(2)}, u32[]{:S(2)}) collective-permute-start(f32[128,256]{1,0:T(8,128)S(1)} %get-tuple-element.28.refs_3_.refs_5_), channel_id=1, source_target_pairs={{0,8},{8,0},{16,24},{24,16},{32,40},{40,32},{48,56},{56,48},{64,72... | collective-permute-start | bytes 393224 | tf_op jit(solution)/shard_map/ppermute | solution.py:584
  7.2 8.9 %collective-permute-start.1 = (f32[128,256]{1,0:T(8,128)S(1)}, f32[128,256]{1,0:T(8,128)S(1)}, u32[]{:S(2)}, u32[]{:S(2)}) collective-permute-start(f32[128,256]{1,0:T(8,128)S(1)} %get-tuple-element.29), channel_id=1, source_target_pairs={{0,504},{8,16},{16,8},{24,32},{32,24},{40,48},{48,40},{56,64},{64,... | collective-permute-start | bytes 393224 | tf_op jit(solution)/shard_map/ppermute | solution.py:584
  16.0 0.9 shard_map.88
  16.9 0.1 shard_map.87.refs_3_.refs_0_.depth
  17.1 0.0 collective-permute-done.refs_1_.refs_6_.refs_3_
  17.1 1.3 %collective-permute-done.1.refs_2_.refs_7_.refs_4_ = f32[128,256]{1,0:T(8,128)S(1)} collective-permute-done((f32[128,256]{1,0:T(8,128)S(1)}, f32[128,256]{1,0:T(8,128)S(1)}, u32[]{:S(2)}, u32[]{:S(2)}) %collective-permute-start.1) | collective-permute-done | bytes 131104 | tf_op jit(solution)/shard_map/ppermute | solution.py:584
  18.4 21.8 %all-gather = f32[768,256]{1,0:T(8,128)S(1)} all-gather(f32[96,256]{1,0:T(8,128)S(1)} %shard_map.89), channel_id=2, replica_groups=mesh['gx'=64,'gy'=8] {'gy'}, dimensions={0}, use_global_device_ids=true | all-gather | bytes 884736 | tf_op jit(solution)/shard_map/all_gather | solution.py:622
  40.2 5.6 %shard_map.90 = (f32[144,256]{1,0:T(8,128)S(1)}, f32[96,256]{1,0:T(8,128)S(1)}, f32[96,256]{1,0:T(8,128)S(1)}, f32[3,4096]{1,0:T(4,128)S(1)}, f32[3,4096]{1,0:T(4,128)S(1)}, /*index=5*/bf16[384,256]{1,0:T(8,128)(2,1)S(1)}) custom-call(s32[1]{0:T(128)} %bitcast.place, f32[6,4096]{1,0:T(8,128)S(1)} %get-tuple-element.24.refs_0_.state, ...), custom_call_target="tpu_custom_call" | custom-call | tf_op jit(solution)/shard_map/pallas_call | solution.py:686
  45.8 1.9 %collective-permute-start.2 = (f32[96,256]{1,0:T(8,128)S(1)}, f32[96,256]{1,0:T(8,128)S(1)}, u32[]{:S(2)}, u32[]{:S(2)}) collective-permute-start(f32[96,256]{1,0:T(8,128)S(1)} %get-tuple-element.36), channel_id=1, source_target_pairs={{0,8},{8,0},{16,24},{24,16},{32,40},{40,32},{48,56},{56,48},{64,72... | collective-permute-start | bytes 294920 | tf_op jit(solution)/shard_map/ppermute | solution.py:584
  47.8 9.3 %collective-permute-start.3 = (f32[96,256]{1,0:T(8,128)S(1)}, f32[96,256]{1,0:T(8,128)S(1)}, u32[]{:S(2)}, u32[]{:S(2)}) collective-permute-start(f32[96,256]{1,0:T(8,128)S(1)} %get-tuple-element.37), channel_id=1, source_target_pairs={{0,504},{8,16},{16,8},{24,32},{32,24},{40,48},{48,40},{56,64},{64,... | collective-permute-start | bytes 294920 | tf_op jit(solution)/shard_map/ppermute | solution.py:584
  57.0 0.2 shard_map.91.refs_3_
  57.3 0.0 collective-permute-done.2.refs_1_
  57.3 2.9 %collective-permute-done.3.refs_2_ = f32[96,256]{1,0:T(8,128)S(1)} collective-permute-done((f32[96,256]{1,0:T(8,128)S(1)}, f32[96,256]{1,0:T(8,128)S(1)}, u32[]{:S(2)}, u32[]{:S(2)}) %collective-permute-start.3) | collective-permute-done | bytes 98336 | tf_op jit(solution)/shard_map/ppermute | solution.py:584
  60.2 17.4 %all-gather.1 = f32[896,256]{1,0:T(8,128)S(1)} all-gather(f32[112,256]{1,0:T(8,128)S(1)} %shard_map.92), channel_id=3, replica_groups=mesh['gx'=64,'gy'=8] {'gy'}, dimensions={0}, use_global_device_ids=true | all-gather | bytes 1032192 | tf_op jit(solution)/shard_map/all_gather | solution.py:622
  77.6 0.8 shard_map.94
  78.4 1.9 %collective-permute-start.4 = (f32[80,256]{1,0:T(8,128)S(1)}, f32[80,256]{1,0:T(8,128)S(1)}, u32[]{:S(2)}, u32[]{:S(2)}) collective-permute-start(f32[80,256]{1,0:T(8,128)S(1)} %get-tuple-element.39), channel_id=1, source_target_pairs={{0,8},{8,0},{16,24},{24,16},{32,40},{40,32},{48,56},{56,48},{64,72... | collective-permute-start | bytes 245768 | tf_op jit(solution)/shard_map/ppermute | solution.py:584
  80.3 7.9 %collective-permute-start.5 = (f32[80,256]{1,0:T(8,128)S(1)}, f32[80,256]{1,0:T(8,128)S(1)}, u32[]{:S(2)}, u32[]{:S(2)}) collective-permute-start(f32[80,256]{1,0:T(8,128)S(1)} %get-tuple-element.40), channel_id=1, source_target_pairs={{0,504},{8,16},{16,8},{24,32},{32,24},{40,48},{48,40},{56,64},{64,... | collective-permute-start | bytes 245768 | tf_op jit(solution)/shard_map/ppermute | solution.py:584
  88.2 1.8 %shard_map.93.refs_5_ = f32[3,4096]{1,0:T(4,128)S(1)} custom-call(s32[1]{0:T(128)} %bitcast.place, s32[5,4096]{1,0:T(8,128)S(1)} %get-tuple-element.25.labels.refs_1_.refs_0_, s32[1,4096]{1,0:T(1,128)S(1)} %get-tuple-element.33.refs_1_, f32[48,256]{1,0:T(8,128)S(1)} %get-tuple-element.34.lent.refs_2_, ...), custom_call_target="tpu_custom_call" | custom-call | tf_op jit(solution)/shard_map/pallas_call | solution.py:721
  90.0 0.0 collective-permute-done.4.refs_7_
  90.0 0.8 collective-permute-done.5.refs_8_
  90.9 4.5 %shard_map.95 = (f32[48,256]{1,0:T(8,128)S(1)}, f32[32,256]{1,0:T(8,128)S(1)}, f32[32,256]{1,0:T(8,128)S(1)}, f32[6,4096]{1,0:T(8,128)S(1)}) custom-call(s32[1]{0:T(128)} %bitcast.place, f32[6,4096]{1,0:T(8,128)S(1)} %get-tuple-element.24.refs_0_.state, s32[5,4096]{1,0:T(8,128)S(1)} %get-tuple-element.25.labels.refs_1_.refs_0_, ...), custom_call_target="tpu_custom_call" | custom-call | tf_op jit(solution)/shard_map/pallas_call | solution.py:728
  95.4 1.9 %collective-permute-start.6 = (f32[32,256]{1,0:T(8,128)S(1)}, f32[32,256]{1,0:T(8,128)S(1)}, u32[]{:S(2)}, u32[]{:S(2)}) collective-permute-start(f32[32,256]{1,0:T(8,128)S(1)} %get-tuple-element.44), channel_id=1, source_target_pairs={{0,8},{8,0},{16,24},{24,16},{32,40},{40,32},{48,56},{56,48},{64,72... | collective-permute-start | bytes 98312 | tf_op jit(solution)/shard_map/ppermute | solution.py:584
  97.3 7.3 %collective-permute-start.7 = (f32[32,256]{1,0:T(8,128)S(1)}, f32[32,256]{1,0:T(8,128)S(1)}, u32[]{:S(2)}, u32[]{:S(2)}) collective-permute-start(f32[32,256]{1,0:T(8,128)S(1)} %get-tuple-element.45), channel_id=1, source_target_pairs={{0,504},{8,16},{16,8},{24,32},{32,24},{40,48},{48,40},{56,64},{64,... | collective-permute-start | bytes 98312 | tf_op jit(solution)/shard_map/ppermute | solution.py:584
  104.7 1.1 shard_map.96.partial
  105.8 0.0 collective-permute-done.6.refs_1_
  105.8 0.4 collective-permute-done.7.refs_2_
  106.2 17.2 %all-gather.2 = f32[384,256]{1,0:T(8,128)S(1)} all-gather(f32[48,256]{1,0:T(8,128)S(1)} %shard_map.97), channel_id=4, replica_groups=mesh['gx'=64,'gy'=8] {'gy'}, dimensions={0}, use_global_device_ids=true | all-gather | bytes 442368 | tf_op jit(solution)/shard_map/all_gather | solution.py:622
  123.4 1.9 %shard_map.98 = (f32[3,4096]{1,0:T(4,128)}, f32[3,4096]{1,0:T(4,128)}) custom-call(s32[1]{0:T(128)} %bitcast.place, f32[6,4096]{1,0:T(8,128)S(1)} %get-tuple-element.24.refs_0_.state, s32[5,4096]{1,0:T(8,128)S(1)} %get-tuple-element.25.labels.refs_1_.refs_0_, bf16[256,4096]{1,0:T(8,128)(2,1)S(1)} %get-tuple-element.26.refs_2_.hot, ...), custom_call_target="tpu_custom_call" | custom-call | tf_op jit(solution)/shard_map/pallas_call | solution.py:748
  (3 shorter events, 0.1 us)
Async XLA Ops:
  3.1 14.0 %collective-permute-start = (f32[128,256]{1,0:T(8,128)S(1)}, f32[128,256]{1,0:T(8,128)S(1)}, u32[]{:S(2)}, u32[]{:S(2)}) collective-permute-start(f32[128,256]{1,0:T(8,128)S(1)} %get-tuple-element.28.refs_3_.refs_5_), channel_id=1, source_target_pairs={{0,8},{8,0},{16,24},{24,16},{32,40},{40,32},{48,56},{56,48},{64,72... | collective-permute-start | bytes 393224 | tf_op jit(solution)/shard_map/ppermute | solution.py:584
  7.2 11.2 %collective-permute-start.1 = (f32[128,256]{1,0:T(8,128)S(1)}, f32[128,256]{1,0:T(8,128)S(1)}, u32[]{:S(2)}, u32[]{:S(2)}) collective-permute-start(f32[128,256]{1,0:T(8,128)S(1)} %get-tuple-element.29), channel_id=1, source_target_pairs={{0,504},{8,16},{16,8},{24,32},{32,24},{40,48},{48,40},{56,64},{64,... | collective-permute-start | bytes 393224 | tf_op jit(solution)/shard_map/ppermute | solution.py:584
  45.8 11.4 %collective-permute-start.2 = (f32[96,256]{1,0:T(8,128)S(1)}, f32[96,256]{1,0:T(8,128)S(1)}, u32[]{:S(2)}, u32[]{:S(2)}) collective-permute-start(f32[96,256]{1,0:T(8,128)S(1)} %get-tuple-element.36), channel_id=1, source_target_pairs={{0,8},{8,0},{16,24},{24,16},{32,40},{40,32},{48,56},{56,48},{64,72... | collective-permute-start | bytes 294920 | tf_op jit(solution)/shard_map/ppermute | solution.py:584
  47.8 12.4 %collective-permute-start.3 = (f32[96,256]{1,0:T(8,128)S(1)}, f32[96,256]{1,0:T(8,128)S(1)}, u32[]{:S(2)}, u32[]{:S(2)}) collective-permute-start(f32[96,256]{1,0:T(8,128)S(1)} %get-tuple-element.37), channel_id=1, source_target_pairs={{0,504},{8,16},{16,8},{24,32},{32,24},{40,48},{48,40},{56,64},{64,... | collective-permute-start | bytes 294920 | tf_op jit(solution)/shard_map/ppermute | solution.py:584
  78.4 11.6 %collective-permute-start.4 = (f32[80,256]{1,0:T(8,128)S(1)}, f32[80,256]{1,0:T(8,128)S(1)}, u32[]{:S(2)}, u32[]{:S(2)}) collective-permute-start(f32[80,256]{1,0:T(8,128)S(1)} %get-tuple-element.39), channel_id=1, source_target_pairs={{0,8},{8,0},{16,24},{24,16},{32,40},{40,32},{48,56},{56,48},{64,72... | collective-permute-start | bytes 245768 | tf_op jit(solution)/shard_map/ppermute | solution.py:584
  80.3 10.5 %collective-permute-start.5 = (f32[80,256]{1,0:T(8,128)S(1)}, f32[80,256]{1,0:T(8,128)S(1)}, u32[]{:S(2)}, u32[]{:S(2)}) collective-permute-start(f32[80,256]{1,0:T(8,128)S(1)} %get-tuple-element.40), channel_id=1, source_target_pairs={{0,504},{8,16},{16,8},{24,32},{32,24},{40,48},{48,40},{56,64},{64,... | collective-permute-start | bytes 245768 | tf_op jit(solution)/shard_map/ppermute | solution.py:584
  95.4 10.4 %collective-permute-start.6 = (f32[32,256]{1,0:T(8,128)S(1)}, f32[32,256]{1,0:T(8,128)S(1)}, u32[]{:S(2)}, u32[]{:S(2)}) collective-permute-start(f32[32,256]{1,0:T(8,128)S(1)} %get-tuple-element.44), channel_id=1, source_target_pairs={{0,8},{8,0},{16,24},{24,16},{32,40},{40,32},{48,56},{56,48},{64,72... | collective-permute-start | bytes 98312 | tf_op jit(solution)/shard_map/ppermute | solution.py:584
  97.3 8.9 %collective-permute-start.7 = (f32[32,256]{1,0:T(8,128)S(1)}, f32[32,256]{1,0:T(8,128)S(1)}, u32[]{:S(2)}, u32[]{:S(2)}) collective-permute-start(f32[32,256]{1,0:T(8,128)S(1)} %get-tuple-element.45), channel_id=1, source_target_pairs={{0,504},{8,16},{16,8},{24,32},{32,24},{40,48},{48,40},{56,64},{64,... | collective-permute-start | bytes 98312 | tf_op jit(solution)/shard_map/ppermute | solution.py:584

commit v6 on v4

--- a/solution.py
+++ b/solution.py
@@ -21,6 +21,12 @@
 highest = lax.Precision.HIGHEST
 SECOND_SPANS = [(11 * p, 11, -1) for p in range(6)] + [(66 + 13 * p, 13, -2) for p in range(3)]
 REPLIES = 105
+PHASES = [
+    ([(9 * p, 9, 0) for p in range(5)], 16, 96),
+    (SECOND_SPANS, 24, 112),
+    ([(16 * p, 16, -2) for p in range(3)], 16, 48),
+]
+LINES = 32 * sum(len(spans) for spans, _, _ in PHASES)
 VMEM_LIMIT = 24 * 1024 * 1024
 
 
@@ -133,28 +139,42 @@
     return jnp.where((source >= 0) & (source < rows), weight, 0.0)
 
 
-def depth_body(out):
+def depth_body(place, out, lines):
     target = lax.broadcasted_iota(jnp.int32, (NZ, NZ), 0)
     source = lax.broadcasted_iota(jnp.int32, (NZ, NZ), 1)
     away = jnp.abs(target - source)
     away = jnp.minimum(away, NZ - away)
     put_split(out, 0, jnp.exp(away.astype(F32) * (-1.0 / 16.0)))
-
-
-def product(a, b_high, b_low):
-    a_high, a_low = split(a)
+    at = 0
+    for spans, window, total in PHASES:
+        for start, rows, first_y in spans:
+            matrix = line_matrix(place[0], window, start - window_start(start, window, total), rows, first_y)
+            high, low = split(matrix)
+            lines[at : at + 16, 0 : 8 * window] = high
+            lines[at + 16 : at + 32, 0 : 8 * window] = low
+            at += 32
+
+
+def window_start(start, window, total):
+    return min(start // 8 * 8, total - window)
+
+
+def product(a_high, a_low, b_high, b_low):
     dot = functools.partial(jnp.dot, preferred_element_type=F32)
     return dot(a_high, b_high) + (dot(a_high, b_low) + dot(a_low, b_high))
 
 
-def smooth(me, depth, gathered, spans, window, kept):
-    for p, (start, rows, first_y) in enumerate(spans):
-        first = min(start // 8 * 8, gathered.shape[1] - window)
-        lines = line_matrix(me, window, start - first, rows, first_y)
+def smooth(depth, lines, gathered, phase, kept):
+    spans, window, total = PHASES[phase]
+    at = 32 * sum(len(PHASES[n][0]) for n in range(phase))
+    for p, (start, _, _) in enumerate(spans):
+        first = window_start(start, window, total)
         source = gathered[:, first : first + window, :].reshape(8 * window, NZ)
-        kept[p * ROWS : (p + 1) * ROWS, :] = product(lines, *split(source))
+        along = lines[at : at + 16, 0 : 8 * window], lines[at + 16 : at + 32, 0 : 8 * window]
+        kept[p * ROWS : (p + 1) * ROWS, :] = product(*along, *split(source))
+        at += 32
     kept[0 : len(spans) * ROWS, :] = product(
-        kept[0 : len(spans) * ROWS, :], depth[0:NZ, :], depth[NZ : 2 * NZ, :]
+        *split(kept[0 : len(spans) * ROWS, :]), depth[0:NZ, :], depth[NZ : 2 * NZ, :]
     )
 
 
@@ -234,13 +254,12 @@
         copy.start()
     own[...] = jnp.zeros_like(own)
     acc[...] = jnp.zeros_like(acc)
-    for copy in copies:
-        copy.wait()
+    copies[0].wait()
+    copies[1].wait()
     state[0:3, :] = held[0] + STEP * held[1]
     state[3:6, :] = held[1]
+    copies[2].wait()
     labels[0:3, :] = ints[...]
-    labels[3:4, :] = lone[0]
-    labels[4:5, :] = lone[1]
     hot[...] = one_hot(ints[2:3, :])
 
     def block(b, carry):
@@ -260,6 +279,10 @@
         own[x * ROWS + 2 : x * ROWS + 11, :] = density[x * 9 : x * 9 + 9, :]
     up[0:32, :] = own[16:48, :]
     down[0:32, :] = own[0:32, :]
+    for copy in copies[3:]:
+        copy.wait()
+    labels[3:4, :] = lone[0]
+    labels[4:5, :] = lone[1]
     for k in range(6):
         source = held.at[2 + k // 3]
         for c in range(16):
@@ -288,6 +311,7 @@
     labels,
     hot,
     depth,
+    lines,
     gathered,
     mine,
     left,
@@ -305,7 +329,7 @@
     acc,
     planes,
 ):
-    smooth(place[0], depth, gathered, [(9 * p, 9, 0) for p in range(5)], 16, kept)
+    smooth(depth, lines, gathered, 0, kept)
     pack[...] = jnp.zeros_like(pack)
     for x in range(3):
         mid = (x + 1) * ROWS
@@ -358,22 +382,22 @@
             drift[d : d + 1, at] = second[d]
             pulls[d : d + 1, at] = home[d]
         along_x, along_y = weights_of(
-            axis_hits(55, CY + 3, 64, cells[0] + to_x + 1, cells[1] + to_y + 1), second[0], second[1]
+            axis_hits(55, CY + 3, 56, cells[0] + to_x + 1, cells[1] + to_y + 1), second[0], second[1]
         )
         planar = along_x * along_y
         upper = planar * second[2]
         lower = planar - upper
         for c in range(4):
             scale = None if c == 0 else STEP * home[c - 1]
-            put_split(lhs, c * 128, lower if c == 0 else lower * scale)
-            put_split(lhs, c * 128 + 64, upper if c == 0 else upper * scale)
+            both = jnp.concatenate([lower, upper], 0)
+            put_split(lhs, c * 112, both if c == 0 else both * scale)
         acc[...] += spread_onto(lhs, hot[...])
         return carry
 
     lax.fori_loop(0, NQ // BLK, block, 0)
     planes[...] = jnp.zeros_like(planes)
     for c in range(4):
-        total = acc[c * 128 : c * 128 + 64, :] + prev_z(acc[c * 128 + 64 : c * 128 + 128, :])
+        total = acc[c * 112 : c * 112 + 56, :] + prev_z(acc[c * 112 + 56 : c * 112 + 112, :])
         for x in range(5):
             planes[c, x, 1:12, :] = total[x * 11 : x * 11 + 11, :]
     for x in range(5):
@@ -433,8 +457,8 @@
         out[n * 16 : n * 16 + 16, :] = values
 
 
-def lines_body(place, depth, gathered, own, up, down):
-    smooth(place[0], depth, gathered, SECOND_SPANS, 24, own)
+def lines_body(depth, lines, gathered, own, up, down):
+    smooth(depth, lines, gathered, 1, own)
     for c in range(2):
         up[c * 32 : c * 32 + 32, :] = own[c * 48 : c * 48 + 32, :]
         down[c * 32 : c * 32 + 32, :] = own[c * 48 + 16 : c * 48 + 48, :]
@@ -457,16 +481,16 @@
         mid = (x + 1) * 16
         first = x * 11
         pack[first : first + 11, :] = -0.5 * (wide[0, mid + 17 : mid + 28, :] - wide[0, mid - 15 : mid - 4, :])
-        pack[64 + first : 75 + first, :] = -0.5 * (
+        pack[56 + first : 67 + first, :] = -0.5 * (
             wide[0, mid + 2 : mid + 13, :] - wide[0, mid : mid + 11, :]
         )
-        pack[128 + first : 139 + first, :] = -diff_z(wide[0, mid : mid + 16, :])[1:12, :]
-        pack[192 + first : 203 + first, :] = (
+        pack[112 + first : 123 + first, :] = -diff_z(wide[0, mid : mid + 16, :])[1:12, :]
+        pack[168 + first : 179 + first, :] = (
             0.5 * (wide[1, mid + 17 : mid + 28, :] - wide[1, mid - 15 : mid - 4, :])
             + wide[2, mid + 1 : mid + 12, :]
         )
     put_split(fields, 0, pack[...])
-    put_split(fields, 256, next_z(pack[...]))
+    put_split(fields, 224, next_z(pack[...]))
     acc[...] = jnp.zeros_like(acc)
 
     def block(b, carry):
@@ -478,15 +502,15 @@
         pull_momentum = row3(pulls, at)
         to_x = jnp.where(moved == 1, 1, jnp.where(moved == 2, -1, 0))
         to_y = jnp.where(moved == 3, 1, jnp.where(moved == 4, -1, 0))
-        hits = axis_hits(55, CY + 3, 64, cells[0] + to_x + 1, cells[1] + to_y + 1)
+        hits = axis_hits(55, CY + 3, 56, cells[0] + to_x + 1, cells[1] + to_y + 1)
         along_x, along_y = weights_of(hits, second[0], second[1])
         slope_x, slope_y = slopes_of(hits)
         sampled = pick_from(fields, hot[...])
         sides = []
         for s in range(2):
-            mixed = sampled[s * 256 + 192 : s * 256 + 256, :]
+            mixed = sampled[s * 224 + 168 : s * 224 + 224, :]
             for d in range(3):
-                mixed = mixed + (STEP * pull_momentum[d]) * sampled[s * 256 + d * 64 : s * 256 + d * 64 + 64, :]
+                mixed = mixed + (STEP * pull_momentum[d]) * sampled[s * 224 + d * 56 : s * 224 + d * 56 + 56, :]
             sides.append(mixed)
         level = sides[0] + second[2] * (sides[1] - sides[0])
         rise = sides[1] - sides[0]
@@ -558,8 +582,8 @@
         out[d : d + 1, :] = grads[d : d + 1, :] + slopes[d]
 
 
-def last_body(place, state, labels, hot, depth, grads, partial, gathered, grad_pos, grad_mom, kept, pack, own_field):
-    smooth(place[0], depth, gathered, [(16 * p, 16, -2) for p in range(3)], 16, kept)
+def last_body(state, labels, hot, depth, lines, grads, partial, gathered, grad_pos, grad_mom, kept, pack, own_field):
+    smooth(depth, lines, gathered, 2, kept)
     pack[...] = jnp.zeros_like(pack)
     for x in range(3):
         pack[x * 9 : x * 9 + 9, :] = kept[x * 16 + 2 : x * 16 + 11, :]
@@ -604,12 +628,9 @@
             compiler_params=pltpu.CompilerParams(vmem_limit_bytes=VMEM_LIMIT),
         )
 
-    depth = pl.pallas_call(
-        depth_body,
-        out_shape=shape(2 * NZ, NZ, dtype=BF16),
-        compiler_params=pltpu.CompilerParams(vmem_limit_bytes=VMEM_LIMIT),
-        cost_estimate=pl.CostEstimate(flops=10**9, bytes_accessed=10**7, transcendentals=10**6),
-    )()
+    depth, lines = call_at(
+        depth_body, (shape(2 * NZ, NZ, dtype=BF16), shape(LINES, 192, dtype=BF16)), [], 0
+    )(place)
     in_hbm = [
         pltpu.with_memory_space_constraint(x, pltpu.HBM)
         for x in (pos, mom, cell, dest, slot, pull_pos, pull_mom)
@@ -659,17 +680,15 @@
             pltpu.VMEM((80, NZ), F32),
             pltpu.VMEM((96, NZ), F32),
             pltpu.VMEM((480, NZ), BF16),
-            pltpu.VMEM((1024, BLK), BF16),
-            pltpu.VMEM((512, NZ), F32),
+            pltpu.VMEM((896, BLK), BF16),
+            pltpu.VMEM((448, NZ), F32),
             pltpu.VMEM((4, 5, ROWS, NZ), F32),
         ],
-        8,
-    )(place, state, labels, hot, depth, gathered, mine, left, right)
+        9,
+    )(place, state, labels, hot, depth, lines, gathered, mine, left, right)
     left, right = swap(up, down, "gx")
     gathered = gather_y(call(fold_second_body, shape(112, NZ))(own, left, right, replies))
-    own, up, down = call_at(lines_body, (shape(144, NZ), shape(80, NZ), shape(80, NZ)), [], 2)(
-        place, depth, gathered
-    )
+    own, up, down = call(lines_body, (shape(144, NZ), shape(80, NZ), shape(80, NZ)))(depth, lines, gathered)
     left, right = swap(up, down, "gx")
     pulls_pos = call_at(
         pulls_body,
@@ -682,8 +701,8 @@
         (shape(48, NZ), shape(32, NZ), shape(32, NZ), shape(6, NQ)),
         [
             pltpu.VMEM((3, 112, NZ), F32),
-            pltpu.VMEM((256, NZ), F32),
-            pltpu.VMEM((1024, NZ), BF16),
+            pltpu.VMEM((224, NZ), F32),
+            pltpu.VMEM((896, NZ), BF16),
             pltpu.VMEM((384, BLK), BF16),
             pltpu.VMEM((192, NZ), F32),
             pltpu.VMEM((3, 7, ROWS, NZ), F32),
@@ -692,12 +711,11 @@
     left, right = swap(up, down, "gx")
     gathered = gather_y(call(fold_third_body, shape(48, NZ))(own, left, right))
     partial = call(push_body, shape(3, NQ))(state, labels, hot, grads, fields)
-    return call_at(
+    return call(
         last_body,
         (shape(3, NQ), shape(3, NQ)),
         [pltpu.VMEM((48, NZ), F32), pltpu.VMEM((32, NZ), F32), pltpu.VMEM((128, NZ), BF16)],
-        7,
-    )(place, state, labels, hot, depth, grads, partial, gathered)
+    )(state, labels, hot, depth, lines, grads, partial, gathered)
 
 
 def solution(mesh):

time: 122 us -> 121 us (level)
  no operation moved by 1% of the time
where the time goes in v6:
time: 121 us
  blocking collectives  56.3 us (47%)
  starting transfers between devices  42.7 us (35%)
  Pallas kernels  18.4 us (15%)
  waiting for transfers between devices  2.58 us (2%)
    all_gather x3, blocking collectives, gather_y(): return lax.all_gather(x, 'gy', axis=0, tiled=False)  56.3 us
    ppermute x8, starting transfers between devices, swap(): return (lax.ppermute(up, axis, forward), lax.ppermute(down, axis, backward))  42.7 us
    pallas_call x1, Pallas kernels, local(): call_at(step_body, (shape(144, NZ), shape(96, NZ), shape(96, NZ), shape(3...  5.28 us
    pallas_call x1, Pallas kernels, local(): call(back_body, (shape(48, NZ), shape(32, NZ), shape(32, NZ), shape(6, NQ...  3.97 us
    ppermute x8, waiting for transfers between devices, swap(): return (lax.ppermute(up, axis, forward), lax.ppermute(down, axis, backward))  2.58 us
  transfers between devices with their start and end apart: 8, of which 3 were waited for; matrix products, arithmetic and copies ran while one was open for 0% of the time, Pallas kernels for 3%

profile of v6, /device:TPU:1, one launch (start us, length us, event | category | flops | bytes accessed | tf_op | source)
XLA Modules:
  0.0 120.9 jit_solution(4935052997642923585)
XLA Ops:
  0.6 2.3 %shard_map.86 = (f32[48,256]{1,0:T(8,128)S(1)}, f32[128,256]{1,0:T(8,128)S(1)}, f32[128,256]{1,0:T(8,128)S(1)}, f32[48,256]{1,0:T(8,128)S(1)}, f32[6,4096]{1,0:T...) custom-call(f32[3,4096]{1,0:T(4,128)} %pos.1, f32[3,4096]{1,0:T(4,128)} %mom.1, s32[3,4096]{1,0:T(4,128)} %cell.1, ...), custom_call_target="tpu_custom_call" | custom-call | tf_op jit(solution)/shard_map/pallas_call | solution.py:638
  2.9 4.0 %collective-permute-start = (f32[128,256]{1,0:T(8,128)S(1)}, f32[128,256]{1,0:T(8,128)S(1)}, u32[]{:S(2)}, u32[]{:S(2)}) collective-permute-start(f32[128,256]{1,0:T(8,128)S(1)} %get-tuple-element.32.pulls.mine), channel_id=1, source_target_pairs={{0,8},{8,16},{16,24},{24,32},{32,40},{40,48},{48,56},{56,64},{64,7... | collective-permute-start | bytes 393224 | tf_op jit(solution)/shard_map/ppermute | solution.py:608
  7.0 7.8 %collective-permute-start.1 = (f32[128,256]{1,0:T(8,128)S(1)}, f32[128,256]{1,0:T(8,128)S(1)}, u32[]{:S(2)}, u32[]{:S(2)}) collective-permute-start(f32[128,256]{1,0:T(8,128)S(1)} %get-tuple-element.33), channel_id=1, source_target_pairs={{8,0},{16,8},{24,16},{32,24},{40,32},{48,40},{56,48},{64,56},{72,6... | collective-permute-start | bytes 393224 | tf_op jit(solution)/shard_map/ppermute | solution.py:608
  14.8 0.2 shard_map.87
  15.1 0.9 shard_map.88
  16.0 0.0 collective-permute-done.left
  16.0 0.8 collective-permute-done.1.right
  16.8 22.3 %all-gather = f32[768,256]{1,0:T(8,128)S(1)} all-gather(f32[96,256]{1,0:T(8,128)S(1)} %shard_map.89), channel_id=2, replica_groups=mesh['gx'=64,'gy'=8] {'gy'}, dimensions={0}, use_global_device_ids=true | all-gather | bytes 884736 | tf_op jit(solution)/shard_map/all_gather | solution.py:612
  39.0 5.3 %shard_map.90 = (f32[144,256]{1,0:T(8,128)S(1)}, f32[96,256]{1,0:T(8,128)S(1)}, f32[96,256]{1,0:T(8,128)S(1)}, f32[3,4096]{1,0:T(4,128)S(1)}, f32[3,4096]{1,0:T(4,128)S(1)}, /*index=5*/bf16[384,256]{1,0:T(8,128)(2,1)S(1)}) custom-call(s32[1]{0:T(128)} %bitcast.2.place, f32[6,4096]{1,0:T(8,128)S(1)} %get-tuple-element.26.state, ...), custom_call_target="tpu_custom_call" | custom-call | tf_op jit(solution)/shard_map/pallas_call | solution.py:669
  44.3 1.9 %collective-permute-start.2 = (f32[96,256]{1,0:T(8,128)S(1)}, f32[96,256]{1,0:T(8,128)S(1)}, u32[]{:S(2)}, u32[]{:S(2)}) collective-permute-start(f32[96,256]{1,0:T(8,128)S(1)} %get-tuple-element.40), channel_id=1, source_target_pairs={{0,8},{8,16},{16,24},{24,32},{32,40},{40,48},{48,56},{56,64},{64,7... | collective-permute-start | bytes 294920 | tf_op jit(solution)/shard_map/ppermute | solution.py:608
  46.3 8.4 %collective-permute-start.3 = (f32[96,256]{1,0:T(8,128)S(1)}, f32[96,256]{1,0:T(8,128)S(1)}, u32[]{:S(2)}, u32[]{:S(2)}) collective-permute-start(f32[96,256]{1,0:T(8,128)S(1)} %get-tuple-element.41), channel_id=1, source_target_pairs={{8,0},{16,8},{24,16},{32,24},{40,32},{48,40},{56,48},{64,56},{72,6... | collective-permute-start | bytes 294920 | tf_op jit(solution)/shard_map/ppermute | solution.py:608
  54.6 0.2 shard_map.91.replies
  54.8 0.9 collective-permute-done.2.left
  55.8 0.9 collective-permute-done.3.right
  56.7 16.7 %all-gather.1 = f32[896,256]{1,0:T(8,128)S(1)} all-gather(f32[112,256]{1,0:T(8,128)S(1)} %shard_map.92), channel_id=3, replica_groups=mesh['gx'=64,'gy'=8] {'gy'}, dimensions={0}, use_global_device_ids=true | all-gather | bytes 1032192 | tf_op jit(solution)/shard_map/all_gather | solution.py:612
  73.4 0.7 shard_map.94
  74.2 1.9 %collective-permute-start.4 = (f32[80,256]{1,0:T(8,128)S(1)}, f32[80,256]{1,0:T(8,128)S(1)}, u32[]{:S(2)}, u32[]{:S(2)}) collective-permute-start(f32[80,256]{1,0:T(8,128)S(1)} %get-tuple-element.43), channel_id=1, source_target_pairs={{0,8},{8,16},{16,24},{24,32},{32,40},{40,48},{48,56},{56,64},{64,7... | collective-permute-start | bytes 245768 | tf_op jit(solution)/shard_map/ppermute | solution.py:608
  76.1 8.7 %collective-permute-start.5 = (f32[80,256]{1,0:T(8,128)S(1)}, f32[80,256]{1,0:T(8,128)S(1)}, u32[]{:S(2)}, u32[]{:S(2)}) collective-permute-start(f32[80,256]{1,0:T(8,128)S(1)} %get-tuple-element.44), channel_id=1, source_target_pairs={{8,0},{16,8},{24,16},{32,24},{40,32},{48,40},{56,48},{64,56},{72,6... | collective-permute-start | bytes 245768 | tf_op jit(solution)/shard_map/ppermute | solution.py:608
  84.8 1.8 %shard_map.93.pulls_pos = f32[3,4096]{1,0:T(4,128)S(1)} custom-call(s32[1]{0:T(128)} %bitcast.2.place, s32[5,4096]{1,0:T(8,128)S(1)} %get-tuple-element.27.labels, s32[1,4096]{1,0:T(1,128)S(1)} %get-tuple-element.37.ranks, f32[48,256]{1,0:T(8,128)S(1)} %get-tuple-element.38.lent.mine, f32[128,256]{1,0:T(8,128)S(1)} %collective-permute-done.left, ...), custom_call_target="tpu_custom_call" | custom-call | tf_op jit(solution)/shard_map/pallas_call | solution.py:693
  86.6 0.0 collective-permute-done.4.left
  86.6 0.0 collective-permute-done.5.right
  86.6 4.0 %shard_map.95 = (f32[48,256]{1,0:T(8,128)S(1)}, f32[32,256]{1,0:T(8,128)S(1)}, f32[32,256]{1,0:T(8,128)S(1)}, f32[6,4096]{1,0:T(8,128)S(1)}) custom-call(f32[6,4096]{1,0:T(8,128)S(1)} %get-tuple-element.26.state, s32[5,4096]{1,0:T(8,128)S(1)} %get-tuple-element.27.labels, bf16[256,4096]{1,0:T(8,128)(2,1)S(1)} %get-tuple-element.28.hot, ...), custom_call_target="tpu_custom_call" | custom-call | tf_op jit(solution)/shard_map/pallas_call | solution.py:699
  90.6 1.9 %collective-permute-start.6 = (f32[32,256]{1,0:T(8,128)S(1)}, f32[32,256]{1,0:T(8,128)S(1)}, u32[]{:S(2)}, u32[]{:S(2)}) collective-permute-start(f32[32,256]{1,0:T(8,128)S(1)} %get-tuple-element.48), channel_id=1, source_target_pairs={{0,8},{8,16},{16,24},{24,32},{32,40},{40,48},{48,56},{56,64},{64,7... | collective-permute-start | bytes 98312 | tf_op jit(solution)/shard_map/ppermute | solution.py:608
  92.5 8.0 %collective-permute-start.7 = (f32[32,256]{1,0:T(8,128)S(1)}, f32[32,256]{1,0:T(8,128)S(1)}, u32[]{:S(2)}, u32[]{:S(2)}) collective-permute-start(f32[32,256]{1,0:T(8,128)S(1)} %get-tuple-element.49), channel_id=1, source_target_pairs={{8,0},{16,8},{24,16},{32,24},{40,32},{48,40},{56,48},{64,56},{72,6... | collective-permute-start | bytes 98312 | tf_op jit(solution)/shard_map/ppermute | solution.py:608
  100.5 1.1 shard_map.96.partial
  101.6 0.0 collective-permute-done.6.left
  101.6 0.0 collective-permute-done.7.right
  101.7 17.3 %all-gather.2 = f32[384,256]{1,0:T(8,128)S(1)} all-gather(f32[48,256]{1,0:T(8,128)S(1)} %shard_map.97), channel_id=4, replica_groups=mesh['gx'=64,'gy'=8] {'gy'}, dimensions={0}, use_global_device_ids=true | all-gather | bytes 442368 | tf_op jit(solution)/shard_map/all_gather | solution.py:612
  119.0 1.9 %shard_map.98 = (f32[3,4096]{1,0:T(4,128)}, f32[3,4096]{1,0:T(4,128)}) custom-call(f32[6,4096]{1,0:T(8,128)S(1)} %get-tuple-element.26.state, s32[5,4096]{1,0:T(8,128)S(1)} %get-tuple-element.27.labels, bf16[256,4096]{1,0:T(8,128)(2,1)S(1)} %get-tuple-element.28.hot, bf16[512,256]{1,0:T(8,128)(2,1)S(1)} %get-tuple-element.29.depth, ...), custom_call_target="tpu_custom_call" | custom-call | tf_op jit(solution)/shard_map/pallas_call | solution.py:714
  (3 shorter events, 0.1 us)
Async XLA Ops:
  2.9 13.0 %collective-permute-start = (f32[128,256]{1,0:T(8,128)S(1)}, f32[128,256]{1,0:T(8,128)S(1)}, u32[]{:S(2)}, u32[]{:S(2)}) collective-permute-start(f32[128,256]{1,0:T(8,128)S(1)} %get-tuple-element.32.pulls.mine), channel_id=1, source_target_pairs={{0,8},{8,16},{16,24},{24,32},{32,40},{40,48},{48,56},{56,64},{64,7... | collective-permute-start | bytes 393224 | tf_op jit(solution)/shard_map/ppermute | solution.py:608
  7.0 9.8 %collective-permute-start.1 = (f32[128,256]{1,0:T(8,128)S(1)}, f32[128,256]{1,0:T(8,128)S(1)}, u32[]{:S(2)}, u32[]{:S(2)}) collective-permute-start(f32[128,256]{1,0:T(8,128)S(1)} %get-tuple-element.33), channel_id=1, source_target_pairs={{8,0},{16,8},{24,16},{32,24},{40,32},{48,40},{56,48},{64,56},{72,6... | collective-permute-start | bytes 393224 | tf_op jit(solution)/shard_map/ppermute | solution.py:608
  44.3 11.5 %collective-permute-start.2 = (f32[96,256]{1,0:T(8,128)S(1)}, f32[96,256]{1,0:T(8,128)S(1)}, u32[]{:S(2)}, u32[]{:S(2)}) collective-permute-start(f32[96,256]{1,0:T(8,128)S(1)} %get-tuple-element.40), channel_id=1, source_target_pairs={{0,8},{8,16},{16,24},{24,32},{32,40},{40,48},{48,56},{56,64},{64,7... | collective-permute-start | bytes 294920 | tf_op jit(solution)/shard_map/ppermute | solution.py:608
  46.3 10.4 %collective-permute-start.3 = (f32[96,256]{1,0:T(8,128)S(1)}, f32[96,256]{1,0:T(8,128)S(1)}, u32[]{:S(2)}, u32[]{:S(2)}) collective-permute-start(f32[96,256]{1,0:T(8,128)S(1)} %get-tuple-element.41), channel_id=1, source_target_pairs={{8,0},{16,8},{24,16},{32,24},{40,32},{48,40},{56,48},{64,56},{72,6... | collective-permute-start | bytes 294920 | tf_op jit(solution)/shard_map/ppermute | solution.py:608
  74.2 12.4 %collective-permute-start.4 = (f32[80,256]{1,0:T(8,128)S(1)}, f32[80,256]{1,0:T(8,128)S(1)}, u32[]{:S(2)}, u32[]{:S(2)}) collective-permute-start(f32[80,256]{1,0:T(8,128)S(1)} %get-tuple-element.43), channel_id=1, source_target_pairs={{0,8},{8,16},{16,24},{24,32},{32,40},{40,48},{48,56},{56,64},{64,7... | collective-permute-start | bytes 245768 | tf_op jit(solution)/shard_map/ppermute | solution.py:608
  76.1 10.5 %collective-permute-start.5 = (f32[80,256]{1,0:T(8,128)S(1)}, f32[80,256]{1,0:T(8,128)S(1)}, u32[]{:S(2)}, u32[]{:S(2)}) collective-permute-start(f32[80,256]{1,0:T(8,128)S(1)} %get-tuple-element.44), channel_id=1, source_target_pairs={{8,0},{16,8},{24,16},{32,24},{40,32},{48,40},{56,48},{64,56},{72,6... | collective-permute-start | bytes 245768 | tf_op jit(solution)/shard_map/ppermute | solution.py:608
  90.6 11.1 %collective-permute-start.6 = (f32[32,256]{1,0:T(8,128)S(1)}, f32[32,256]{1,0:T(8,128)S(1)}, u32[]{:S(2)}, u32[]{:S(2)}) collective-permute-start(f32[32,256]{1,0:T(8,128)S(1)} %get-tuple-element.48), channel_id=1, source_target_pairs={{0,8},{8,16},{16,24},{24,32},{32,40},{40,48},{48,56},{56,64},{64,7... | collective-permute-start | bytes 98312 | tf_op jit(solution)/shard_map/ppermute | solution.py:608
  92.5 9.2 %collective-permute-start.7 = (f32[32,256]{1,0:T(8,128)S(1)}, f32[32,256]{1,0:T(8,128)S(1)}, u32[]{:S(2)}, u32[]{:S(2)}) collective-permute-start(f32[32,256]{1,0:T(8,128)S(1)} %get-tuple-element.49), channel_id=1, source_target_pairs={{8,0},{16,8},{24,16},{32,24},{40,32},{48,40},{56,48},{64,56},{72,6... | collective-permute-start | bytes 98312 | tf_op jit(solution)/shard_map/ppermute | solution.py:608

commit v7 on v6

--- a/solution.py
+++ b/solution.py
@@ -464,6 +464,12 @@
         down[c * 32 : c * 32 + 32, :] = own[c * 48 + 16 : c * 48 + 48, :]
     up[64:80, :] = own[112:128, :]
     down[64:80, :] = own[112:128, :]
+
+
+def slope_weights(hits, frac_x, frac_y):
+    along_x, along_y = weights_of(hits, frac_x, frac_y)
+    slope_x, slope_y = slopes_of(hits)
+    return slope_x * along_y, slope_y * along_x, along_x * along_y
 
 
 def back_body(
@@ -554,19 +560,15 @@
             down[x * 16 : (x + 1) * 16, :] = spread
 
 
-def mix_slopes(hits, frac, sides):
-    along_x, along_y = weights_of(hits, frac[0], frac[1])
-    slope_x, slope_y = slopes_of(hits)
+def mix_slopes(weights, frac_z, sides):
     rise = sides[1] - sides[0]
-    level = sides[0] + frac[2] * rise
+    level = sides[0] + frac_z * rise
     return [
-        jnp.sum(slope_x * (along_y * level), axis=0, keepdims=True),
-        jnp.sum(slope_y * (along_x * level), axis=0, keepdims=True),
-        jnp.sum(along_x * (along_y * rise), axis=0, keepdims=True),
+        jnp.sum(weights[d] * (level if d < 2 else rise), axis=0, keepdims=True) for d in range(3)
     ]
 
 
-def push_body(state, labels, hot, grads, fields, out):
+def push_body(state, labels, hot, grads, fields, out, weights):
     frac = row3(state, slice(None))
     cells = row3(labels, slice(None))
     grad_kick = row3(grads, slice(None), 3)
@@ -577,24 +579,23 @@
         for d in range(1, 3):
             mixed = mixed + (STEP * grad_kick[d]) * sampled[s * 96 + d * 32 : s * 96 + d * 32 + 32, :]
         sides.append(mixed)
-    slopes = mix_slopes(axis_hits(27, CY + 1, 32, cells[0], cells[1]), frac, sides)
+    hits = axis_hits(27, CY + 1, 32, cells[0], cells[1])
+    for n, values in enumerate(slope_weights(hits, frac[0], frac[1])):
+        weights[n] = values
+    slopes = mix_slopes(weights, frac[2], sides)
     for d in range(3):
         out[d : d + 1, :] = grads[d : d + 1, :] + slopes[d]
 
 
-def last_body(state, labels, hot, depth, lines, grads, partial, gathered, grad_pos, grad_mom, kept, pack, own_field):
+def last_body(state, weights, hot, depth, lines, grads, partial, gathered, grad_pos, grad_mom, kept, pack, own_field):
     smooth(depth, lines, gathered, 2, kept)
     pack[...] = jnp.zeros_like(pack)
     for x in range(3):
         pack[x * 9 : x * 9 + 9, :] = kept[x * 16 + 2 : x * 16 + 11, :]
     put_split(own_field, 0, pack[...])
     put_split(own_field, 32, next_z(pack[...]))
-    frac = row3(state, slice(None))
-    cells = row3(labels, slice(None))
     sampled = pick_from(own_field, hot[...])
-    slopes = mix_slopes(
-        axis_hits(27, CY + 1, 32, cells[0], cells[1]), frac, [sampled[0:32, :], sampled[32:64, :]]
-    )
+    slopes = mix_slopes(weights, state[2:3, :], [sampled[0:32, :], sampled[32:64, :]])
     for d in range(3):
         total = partial[d : d + 1, :] + slopes[d]
         grad_pos[d : d + 1, :] = total
@@ -710,12 +711,12 @@
     )(state, labels, hot, drift, pulls, pulls_pos, own, left, right)
     left, right = swap(up, down, "gx")
     gathered = gather_y(call(fold_third_body, shape(48, NZ))(own, left, right))
-    partial = call(push_body, shape(3, NQ))(state, labels, hot, grads, fields)
+    partial, near_weights = call(push_body, (shape(3, NQ), shape(3, 32, NQ)))(state, labels, hot, grads, fields)
     return call(
         last_body,
         (shape(3, NQ), shape(3, NQ)),
         [pltpu.VMEM((48, NZ), F32), pltpu.VMEM((32, NZ), F32), pltpu.VMEM((128, NZ), BF16)],
-    )(state, labels, hot, depth, lines, grads, partial, gathered)
+    )(state, near_weights, hot, depth, lines, grads, partial, gathered)
 
 
 def solution(mesh):

time: 121 us -> 121 us (level)
  no operation moved by 1% of the time
where the time goes in v7:
time: 121 us
  blocking collectives  56.3 us (47%)
  starting transfers between devices  42.7 us (35%)
  Pallas kernels  18.2 us (15%)
  waiting for transfers between devices  2.58 us (2%)
    all_gather x3, blocking collectives, gather_y(): return lax.all_gather(x, 'gy', axis=0, tiled=False)  56.3 us
    ppermute x8, starting transfers between devices, swap(): return (lax.ppermute(up, axis, forward), lax.ppermute(down, axis, backward))  42.7 us
    pallas_call x1, Pallas kernels, local(): call_at(step_body, (shape(144, NZ), shape(96, NZ), shape(96, NZ), shape(3...  5.28 us
    pallas_call x1, Pallas kernels, local(): call(back_body, (shape(48, NZ), shape(32, NZ), shape(32, NZ), shape(6, NQ...  3.97 us
    ppermute x8, waiting for transfers between devices, swap(): return (lax.ppermute(up, axis, forward), lax.ppermute(down, axis, backward))  2.58 us
  transfers between devices with their start and end apart: 8, of which 3 were waited for; matrix products, arithmetic and copies ran while one was open for 0% of the time, Pallas kernels for 3%

profile of v7, /device:TPU:1, one launch (start us, length us, event | category | flops | bytes accessed | tf_op | source)
XLA Modules:
  0.0 120.6 jit_solution(7924661454874613854)
XLA Ops:
  0.6 2.3 %shard_map.86 = (f32[48,256]{1,0:T(8,128)S(1)}, f32[128,256]{1,0:T(8,128)S(1)}, f32[128,256]{1,0:T(8,128)S(1)}, f32[48,256]{1,0:T(8,128)S(1)}, f32[6,4096]{1,0:T...) custom-call(f32[3,4096]{1,0:T(4,128)} %pos.1, f32[3,4096]{1,0:T(4,128)} %mom.1, s32[3,4096]{1,0:T(4,128)} %cell.1, ...), custom_call_target="tpu_custom_call" | custom-call | tf_op jit(solution)/shard_map/pallas_call | solution.py:639
  2.9 4.0 %collective-permute-start = (f32[128,256]{1,0:T(8,128)S(1)}, f32[128,256]{1,0:T(8,128)S(1)}, u32[]{:S(2)}, u32[]{:S(2)}) collective-permute-start(f32[128,256]{1,0:T(8,128)S(1)} %get-tuple-element.34.pulls.mine), channel_id=1, source_target_pairs={{0,8},{8,16},{16,24},{24,32},{32,40},{40,48},{48,56},{56,64},{64,7... | collective-permute-start | bytes 393224 | tf_op jit(solution)/shard_map/ppermute | solution.py:609
  7.0 7.8 %collective-permute-start.1 = (f32[128,256]{1,0:T(8,128)S(1)}, f32[128,256]{1,0:T(8,128)S(1)}, u32[]{:S(2)}, u32[]{:S(2)}) collective-permute-start(f32[128,256]{1,0:T(8,128)S(1)} %get-tuple-element.35), channel_id=1, source_target_pairs={{8,0},{16,8},{24,16},{32,24},{40,32},{48,40},{56,48},{64,56},{72,6... | collective-permute-start | bytes 393224 | tf_op jit(solution)/shard_map/ppermute | solution.py:609
  14.8 0.2 shard_map.87
  15.1 0.9 shard_map.88
  16.0 0.0 collective-permute-done.left
  16.0 0.8 collective-permute-done.1.right
  16.8 22.3 %all-gather = f32[768,256]{1,0:T(8,128)S(1)} all-gather(f32[96,256]{1,0:T(8,128)S(1)} %shard_map.89), channel_id=2, replica_groups=mesh['gx'=64,'gy'=8] {'gy'}, dimensions={0}, use_global_device_ids=true | all-gather | bytes 884736 | tf_op jit(solution)/shard_map/all_gather | solution.py:613
  39.0 5.3 %shard_map.90 = (f32[144,256]{1,0:T(8,128)S(1)}, f32[96,256]{1,0:T(8,128)S(1)}, f32[96,256]{1,0:T(8,128)S(1)}, f32[3,4096]{1,0:T(4,128)S(1)}, f32[3,4096]{1,0:T(4,128)S(1)}, /*index=5*/bf16[384,256]{1,0:T(8,128)(2,1)S(1)}) custom-call(s32[1]{0:T(128)} %bitcast.2.place, f32[6,4096]{1,0:T(8,128)S(1)} %get-tuple-element.28.state, ...), custom_call_target="tpu_custom_call" | custom-call | tf_op jit(solution)/shard_map/pallas_call | solution.py:670
  44.3 1.9 %collective-permute-start.2 = (f32[96,256]{1,0:T(8,128)S(1)}, f32[96,256]{1,0:T(8,128)S(1)}, u32[]{:S(2)}, u32[]{:S(2)}) collective-permute-start(f32[96,256]{1,0:T(8,128)S(1)} %get-tuple-element.42), channel_id=1, source_target_pairs={{0,8},{8,16},{16,24},{24,32},{32,40},{40,48},{48,56},{56,64},{64,7... | collective-permute-start | bytes 294920 | tf_op jit(solution)/shard_map/ppermute | solution.py:609
  46.3 8.4 %collective-permute-start.3 = (f32[96,256]{1,0:T(8,128)S(1)}, f32[96,256]{1,0:T(8,128)S(1)}, u32[]{:S(2)}, u32[]{:S(2)}) collective-permute-start(f32[96,256]{1,0:T(8,128)S(1)} %get-tuple-element.43), channel_id=1, source_target_pairs={{8,0},{16,8},{24,16},{32,24},{40,32},{48,40},{56,48},{64,56},{72,6... | collective-permute-start | bytes 294920 | tf_op jit(solution)/shard_map/ppermute | solution.py:609
  54.6 0.2 shard_map.91.replies
  54.8 0.9 collective-permute-done.2.left
  55.8 0.9 collective-permute-done.3.right
  56.7 16.7 %all-gather.1 = f32[896,256]{1,0:T(8,128)S(1)} all-gather(f32[112,256]{1,0:T(8,128)S(1)} %shard_map.92), channel_id=3, replica_groups=mesh['gx'=64,'gy'=8] {'gy'}, dimensions={0}, use_global_device_ids=true | all-gather | bytes 1032192 | tf_op jit(solution)/shard_map/all_gather | solution.py:613
  73.4 0.7 shard_map.94
  74.2 1.9 %collective-permute-start.4 = (f32[80,256]{1,0:T(8,128)S(1)}, f32[80,256]{1,0:T(8,128)S(1)}, u32[]{:S(2)}, u32[]{:S(2)}) collective-permute-start(f32[80,256]{1,0:T(8,128)S(1)} %get-tuple-element.45), channel_id=1, source_target_pairs={{0,8},{8,16},{16,24},{24,32},{32,40},{40,48},{48,56},{56,64},{64,7... | collective-permute-start | bytes 245768 | tf_op jit(solution)/shard_map/ppermute | solution.py:609
  76.1 8.7 %collective-permute-start.5 = (f32[80,256]{1,0:T(8,128)S(1)}, f32[80,256]{1,0:T(8,128)S(1)}, u32[]{:S(2)}, u32[]{:S(2)}) collective-permute-start(f32[80,256]{1,0:T(8,128)S(1)} %get-tuple-element.46), channel_id=1, source_target_pairs={{8,0},{16,8},{24,16},{32,24},{40,32},{48,40},{56,48},{64,56},{72,6... | collective-permute-start | bytes 245768 | tf_op jit(solution)/shard_map/ppermute | solution.py:609
  84.8 1.8 %shard_map.93.pulls_pos = f32[3,4096]{1,0:T(4,128)S(1)} custom-call(s32[1]{0:T(128)} %bitcast.2.place, s32[5,4096]{1,0:T(8,128)S(1)} %get-tuple-element.29.labels, s32[1,4096]{1,0:T(1,128)S(1)} %get-tuple-element.39.ranks, f32[48,256]{1,0:T(8,128)S(1)} %get-tuple-element.40.lent.mine, f32[128,256]{1,0:T(8,128)S(1)} %collective-permute-done.left, ...), custom_call_target="tpu_custom_call" | custom-call | tf_op jit(solution)/shard_map/pallas_call | solution.py:694
  86.6 0.0 collective-permute-done.4.left
  86.6 0.0 collective-permute-done.5.right
  86.6 4.0 %shard_map.95 = (f32[48,256]{1,0:T(8,128)S(1)}, f32[32,256]{1,0:T(8,128)S(1)}, f32[32,256]{1,0:T(8,128)S(1)}, f32[6,4096]{1,0:T(8,128)S(1)}) custom-call(f32[6,4096]{1,0:T(8,128)S(1)} %get-tuple-element.28.state, s32[5,4096]{1,0:T(8,128)S(1)} %get-tuple-element.29.labels, bf16[256,4096]{1,0:T(8,128)(2,1)S(1)} %get-tuple-element.30.hot, ...), custom_call_target="tpu_custom_call" | custom-call | tf_op jit(solution)/shard_map/pallas_call | solution.py:700
  90.6 1.9 %collective-permute-start.6 = (f32[32,256]{1,0:T(8,128)S(1)}, f32[32,256]{1,0:T(8,128)S(1)}, u32[]{:S(2)}, u32[]{:S(2)}) collective-permute-start(f32[32,256]{1,0:T(8,128)S(1)} %get-tuple-element.52), channel_id=1, source_target_pairs={{0,8},{8,16},{16,24},{24,32},{32,40},{40,48},{48,56},{56,64},{64,7... | collective-permute-start | bytes 98312 | tf_op jit(solution)/shard_map/ppermute | solution.py:609
  92.5 8.0 %collective-permute-start.7 = (f32[32,256]{1,0:T(8,128)S(1)}, f32[32,256]{1,0:T(8,128)S(1)}, u32[]{:S(2)}, u32[]{:S(2)}) collective-permute-start(f32[32,256]{1,0:T(8,128)S(1)} %get-tuple-element.53), channel_id=1, source_target_pairs={{8,0},{16,8},{24,16},{32,24},{40,32},{48,40},{56,48},{64,56},{72,6... | collective-permute-start | bytes 98312 | tf_op jit(solution)/shard_map/ppermute | solution.py:609
  100.5 1.1 shard_map.96
  101.6 0.0 collective-permute-done.6.left
  101.6 0.0 collective-permute-done.7.right
  101.7 17.3 %all-gather.2 = f32[384,256]{1,0:T(8,128)S(1)} all-gather(f32[48,256]{1,0:T(8,128)S(1)} %shard_map.97), channel_id=4, replica_groups=mesh['gx'=64,'gy'=8] {'gy'}, dimensions={0}, use_global_device_ids=true | all-gather | bytes 442368 | tf_op jit(solution)/shard_map/all_gather | solution.py:613
  119.0 1.6 %shard_map.98 = (f32[3,4096]{1,0:T(4,128)}, f32[3,4096]{1,0:T(4,128)}) custom-call(f32[6,4096]{1,0:T(8,128)S(1)} %get-tuple-element.28.state, f32[3,32,4096]{2,1,0:T(8,128)S(1)} %get-tuple-element.49.weights, bf16[256,4096]{1,0:T(8,128)(2,1)S(1)} %get-tuple-element.30.hot, bf16[512,256]{1,0:T(8,128)(2,1)S(1)} %get-tuple-element.31.depth, ...), custom_call_target="tpu_custom_call" | custom-call | tf_op jit(solution)/shard_map/pallas_call | solution.py:715
  (3 shorter events, 0.1 us)
Async XLA Ops:
  2.9 13.0 %collective-permute-start = (f32[128,256]{1,0:T(8,128)S(1)}, f32[128,256]{1,0:T(8,128)S(1)}, u32[]{:S(2)}, u32[]{:S(2)}) collective-permute-start(f32[128,256]{1,0:T(8,128)S(1)} %get-tuple-element.34.pulls.mine), channel_id=1, source_target_pairs={{0,8},{8,16},{16,24},{24,32},{32,40},{40,48},{48,56},{56,64},{64,7... | collective-permute-start | bytes 393224 | tf_op jit(solution)/shard_map/ppermute | solution.py:609
  7.0 9.8 %collective-permute-start.1 = (f32[128,256]{1,0:T(8,128)S(1)}, f32[128,256]{1,0:T(8,128)S(1)}, u32[]{:S(2)}, u32[]{:S(2)}) collective-permute-start(f32[128,256]{1,0:T(8,128)S(1)} %get-tuple-element.35), channel_id=1, source_target_pairs={{8,0},{16,8},{24,16},{32,24},{40,32},{48,40},{56,48},{64,56},{72,6... | collective-permute-start | bytes 393224 | tf_op jit(solution)/shard_map/ppermute | solution.py:609
  44.3 11.5 %collective-permute-start.2 = (f32[96,256]{1,0:T(8,128)S(1)}, f32[96,256]{1,0:T(8,128)S(1)}, u32[]{:S(2)}, u32[]{:S(2)}) collective-permute-start(f32[96,256]{1,0:T(8,128)S(1)} %get-tuple-element.42), channel_id=1, source_target_pairs={{0,8},{8,16},{16,24},{24,32},{32,40},{40,48},{48,56},{56,64},{64,7... | collective-permute-start | bytes 294920 | tf_op jit(solution)/shard_map/ppermute | solution.py:609
  46.3 10.4 %collective-permute-start.3 = (f32[96,256]{1,0:T(8,128)S(1)}, f32[96,256]{1,0:T(8,128)S(1)}, u32[]{:S(2)}, u32[]{:S(2)}) collective-permute-start(f32[96,256]{1,0:T(8,128)S(1)} %get-tuple-element.43), channel_id=1, source_target_pairs={{8,0},{16,8},{24,16},{32,24},{40,32},{48,40},{56,48},{64,56},{72,6... | collective-permute-start | bytes 294920 | tf_op jit(solution)/shard_map/ppermute | solution.py:609
  74.2 12.4 %collective-permute-start.4 = (f32[80,256]{1,0:T(8,128)S(1)}, f32[80,256]{1,0:T(8,128)S(1)}, u32[]{:S(2)}, u32[]{:S(2)}) collective-permute-start(f32[80,256]{1,0:T(8,128)S(1)} %get-tuple-element.45), channel_id=1, source_target_pairs={{0,8},{8,16},{16,24},{24,32},{32,40},{40,48},{48,56},{56,64},{64,7... | collective-permute-start | bytes 245768 | tf_op jit(solution)/shard_map/ppermute | solution.py:609
  76.1 10.5 %collective-permute-start.5 = (f32[80,256]{1,0:T(8,128)S(1)}, f32[80,256]{1,0:T(8,128)S(1)}, u32[]{:S(2)}, u32[]{:S(2)}) collective-permute-start(f32[80,256]{1,0:T(8,128)S(1)} %get-tuple-element.46), channel_id=1, source_target_pairs={{8,0},{16,8},{24,16},{32,24},{40,32},{48,40},{56,48},{64,56},{72,6... | collective-permute-start | bytes 245768 | tf_op jit(solution)/shard_map/ppermute | solution.py:609
  90.6 11.1 %collective-permute-start.6 = (f32[32,256]{1,0:T(8,128)S(1)}, f32[32,256]{1,0:T(8,128)S(1)}, u32[]{:S(2)}, u32[]{:S(2)}) collective-permute-start(f32[32,256]{1,0:T(8,128)S(1)} %get-tuple-element.52), channel_id=1, source_target_pairs={{0,8},{8,16},{16,24},{24,32},{32,40},{40,48},{48,56},{56,64},{64,7... | collective-permute-start | bytes 98312 | tf_op jit(solution)/shard_map/ppermute | solution.py:609
  92.5 9.2 %collective-permute-start.7 = (f32[32,256]{1,0:T(8,128)S(1)}, f32[32,256]{1,0:T(8,128)S(1)}, u32[]{:S(2)}, u32[]{:S(2)}) collective-permute-start(f32[32,256]{1,0:T(8,128)S(1)} %get-tuple-element.53), channel_id=1, source_target_pairs={{8,0},{16,8},{24,16},{32,24},{40,32},{48,40},{56,48},{64,56},{72,6... | collective-permute-start | bytes 98312 | tf_op jit(solution)/shard_map/ppermute | solution.py:609
